TPU v7x, 512 devices: a whole 4x4x16 slice. The times are simulated.
512 devices in a mesh: dp: 8 (over z_lo), slab: 64 (over y, x, z_hi, core).
Axes of the slice: x: 4, y: 4, z: 16 (z_hi: 2, z_lo: 8; z = z_hi * 8 + z_lo), core: 2. Of those that a mesh axis runs over, the one named last changes fastest.
Arguments:
- features: bfloat16 [65536, 128], P(('dp', 'slab')), may hold values from -6 to 6
- counts: int32 [512], P(('dp', 'slab')), may hold values from 16 to 128, as said below
- neighbours: int32 [65536, 27], P(('dp', 'slab')), may hold values from 0 to 192, as said below
- low_faces: int32 [16384], P(('dp', 'slab')), may hold values from 0 to 127, as said below
- high_faces: int32 [16384], P(('dp', 'slab')), may hold values from 0 to 127, as said below
- weight_one: bfloat16 [27, 128, 128], replicated, may hold values from -0.109375 to 0.109375
- weight_two: bfloat16 [27, 128, 128], replicated, may hold values from -0.109375 to 0.109375
- cotangent: bfloat16 [65536, 128], P(('dp', 'slab')), may hold values from -12 to 12
Outputs:
- response: bfloat16 [65536, 128], P(('dp', 'slab'))
- input_grad: bfloat16 [65536, 128], P(('dp', 'slab'))
- first_grad: bfloat16 [27, 128, 128], replicated
- second_grad: bfloat16 [27, 128, 128], replicated
Inputs may be any that keep to these rules, and one draw needn't show every extreme that they name: `counts`: at least one slab holds 128 live sites and one holds 16. `neighbours`: entry [i, 13] is i mod 128. Values below 128 name sites of the same slab, 128 to 159 the rows from the lower slab, the next 32 those from the upper slab, and 192 an empty neighbour. `low_faces`: each slab's 32 entries name its own sites, repeats allowed. `high_faces`: each slab's 32 entries name its own sites, repeats allowed.
All inputs are finite; a program needn't handle non-finite values.
Results may differ from a plain program's by a relative error of at most 0.0052.
Values may be sent and summed in bfloat16 or wider, within the bound.
No kernel may reach another device: no remote copies, remote signals or barrier semaphores. Data moves between devices by JAX's collectives and lax.ppermute only.
A program may use at most 128 MiB of HBM per device.

v0:
```python
import math

import jax
import jax.numpy as jnp
from jax import lax
from jax.sharding import PartitionSpec as P


def from_behind(block, axis, distance):
    devices = range(lax.axis_size(axis))
    route = [(i - distance, i) for i in devices if i - distance in devices]
    return lax.ppermute(block, axis, route)


def extend_rows(values, low_faces, high_faces):
    send_up = jnp.take(values, high_faces, axis=0)
    send_down = jnp.take(values, low_faces, axis=0)
    from_below = from_behind(send_up, "slab", 1)
    from_above = from_behind(send_down, "slab", -1)
    zero_row = jnp.zeros((1, values.shape[1]), values.dtype)
    return jnp.concatenate([values, from_below, from_above, zero_row], 0)


def retract_rows(ext_grad, site_count, rim_rows, low_faces, high_faces):
    own_rows = ext_grad[:site_count]
    to_below = ext_grad[site_count : site_count + rim_rows]
    to_above = ext_grad[site_count + rim_rows : site_count + 2 * rim_rows]
    got_above = from_behind(to_below, "slab", -1)
    got_below = from_behind(to_above, "slab", 1)
    own_rows = own_rows.at[high_faces].add(got_above)
    return own_rows.at[low_faces].add(got_below)


def convolve(extended, neighbours, weight, block_total, row_block):
    site_count = neighbours.shape[0]
    channels = weight.shape[2]

    def convolve_one_block(block_id, result):
        summed = jnp.zeros((row_block, channels), jnp.float32)
        for offset in range(weight.shape[0]):
            picked = jnp.take(extended, neighbours[:, offset], axis=0)
            summed = summed + jnp.dot(picked, weight[offset], preferred_element_type=jnp.float32)
        return summed

    return lax.fori_loop(
        0, block_total, convolve_one_block, jnp.zeros((site_count, channels), jnp.float32)
    )


def backprop(extended, neighbours, weight, grad_out, block_total):
    channels = weight.shape[2]

    def backprop_one_block(block_id, carry):
        kernel_acc, ext_grad = carry
        for offset in range(weight.shape[0]):
            picked = jnp.take(extended, neighbours[:, offset], axis=0)
            term = lax.dot_general(
                picked, grad_out, (((0,), (0,)), ((), ())), preferred_element_type=jnp.float32
            )
            kernel_acc = kernel_acc.at[offset].add(term)
            back = lax.dot_general(
                grad_out,
                weight[offset],
                (((1,), (1,)), ((), ())),
                preferred_element_type=jnp.float32,
            )
            ext_grad = ext_grad.at[neighbours[:, offset]].add(back)
        return (kernel_acc, ext_grad)

    start_acc = jnp.zeros((weight.shape[0], weight.shape[1], channels), jnp.float32)
    start_ext = jnp.zeros((extended.shape[0], weight.shape[1]), jnp.float32)
    return lax.fori_loop(0, block_total, backprop_one_block, (start_acc, start_ext))


def reduce_kernel(kernel_acc, scaling):
    total = lax.psum(kernel_acc, ("dp", "slab"))
    return (total * scaling).astype(jnp.bfloat16)


def on_device(
    features, counts, neighbours, low_faces, high_faces, weight_one, weight_two, cotangent
):
    site_count = features.shape[0]
    rim_rows = low_faces.shape[0]
    row_block = min(512, site_count)
    scaling = 1.0 / math.sqrt(lax.axis_size("dp") * lax.axis_size("slab") * site_count)
    live_mask = (lax.broadcasted_iota(jnp.int32, (site_count, 1), 0) < counts[0]).astype(
        jnp.float32
    )
    block_total = site_count // row_block
    masked = (features * live_mask).astype(jnp.bfloat16)
    ext_one = extend_rows(masked, low_faces, high_faces)
    first_pre = convolve(ext_one, neighbours, weight_one, block_total, row_block)
    hidden = (jax.nn.gelu(first_pre) * live_mask).astype(jnp.bfloat16)
    ext_two = extend_rows(hidden, low_faces, high_faces)
    second_pre = convolve(ext_two, neighbours, weight_two, block_total, row_block)
    response = (second_pre * live_mask).astype(jnp.bfloat16)
    out_grad = (cotangent * live_mask).astype(jnp.bfloat16)
    second_acc, hidden_ext_grad = backprop(ext_two, neighbours, weight_two, out_grad, block_total)
    second_grad = reduce_kernel(second_acc, scaling)
    hidden_grad = retract_rows(hidden_ext_grad, site_count, rim_rows, low_faces, high_faces)
    pullback = jax.vjp(jax.nn.gelu, first_pre)[1]
    pre_grad = pullback(hidden_grad * live_mask)[0].astype(jnp.bfloat16)
    first_acc, input_ext_grad = backprop(ext_one, neighbours, weight_one, pre_grad, block_total)
    first_grad = reduce_kernel(first_acc, scaling)
    input_grad = (
        retract_rows(input_ext_grad, site_count, rim_rows, low_faces, high_faces) * live_mask
    ).astype(jnp.bfloat16)
    return (response, input_grad, first_grad, second_grad)


def solution(mesh):
    placed = (
        P(("dp", "slab"), None),
        P(("dp", "slab")),
        P(("dp", "slab"), None),
        P(("dp", "slab")),
        P(("dp", "slab")),
        P(),
        P(),
        P(("dp", "slab"), None),
    )
    return jax.shard_map(
        on_device,
        mesh=mesh,
        in_specs=placed,
        out_specs=(P(("dp", "slab"), None), P(("dp", "slab"), None), P(), P()),
        check_vma=False,
    )
```

profile of v0, /device:TPU:1, one launch (start us, length us, event | category | flops | bytes accessed | tf_op | source)
XLA Modules:
  0.0 770.1 jit_solution(8284207323050910321)
XLA Ops:
  12.1 16.8 %collective-permute-start = (bf16[32,128]{1,0:T(8,128)(2,1)S(1)}, bf16[32,128]{1,0:T(8,128)(2,1)S(1)}, u32[]{:S(2)}, u32[]{:S(2)}) collective-permute-start(bf16[32,128]{1,0:T(8,128)(2,1)S(1)} %broadcast_select_fusion.165), channel_id=1, source_target_pairs={{0,1},{1,2},{2,3},{3,4},{4,5},{5,6},{6,7},{7,8},{8,9},{9,10},{10,1... | collective-permute-start | bytes 24584 | tf_op jit(solution)/shard_map/ppermute | solution.py:12
  31.3 1.9 collective-permute-start.1
  50.5 1.2 scatter_fusion
  51.8 1.2 scatter_fusion.1
  53.0 1.2 scatter_fusion.2
  54.3 1.2 scatter_fusion.3
  55.6 1.2 scatter_fusion.4
  56.8 1.2 scatter_fusion.5
  58.1 1.2 scatter_fusion.6
  59.4 1.2 scatter_fusion.7
  60.6 1.2 scatter_fusion.8
  61.9 1.2 scatter_fusion.9
  63.2 1.3 scatter_fusion.10
  64.4 1.2 scatter_fusion.11
  65.7 1.2 scatter_fusion.12
  67.0 1.2 scatter_fusion.13
  68.2 1.5 scatter_fusion.14
  69.7 1.2 scatter_fusion.15
  71.0 1.2 scatter_fusion.16
  72.2 1.2 scatter_fusion.17
  73.5 1.2 scatter_fusion.18
  74.8 1.2 scatter_fusion.19
  76.0 1.2 scatter_fusion.20
  77.3 1.2 scatter_fusion.21
  78.6 1.2 scatter_fusion.22
  79.8 1.2 scatter_fusion.23
  81.1 1.2 scatter_fusion.24
  82.4 1.2 scatter_fusion.25
  83.6 12.4 %collective-permute-start.5 = (f32[32,128]{1,0:T(8,128)S(1)}, f32[32,128]{1,0:T(8,128)S(1)}, u32[]{:S(2)}, u32[]{:S(2)}) collective-permute-start(f32[32,128]{1,0:T(8,128)S(1)} %get-tuple-element.1052), channel_id=1, source_target_pairs={{0,1},{1,2},{2,3},{3,4},{4,5},{5,6},{6,7},{7,8},{8,9},{9,10},{10,1... | collective-permute-start | bytes 49160 | tf_op jit(solution)/shard_map/ppermute | solution.py:12
  96.0 2.3 collective-permute-start.4
  149.7 12.3 %collective-permute-start.2 = (bf16[32,128]{1,0:T(8,128)(2,1)S(1)}, bf16[32,128]{1,0:T(8,128)(2,1)S(1)}, u32[]{:S(2)}, u32[]{:S(2)}) collective-permute-start(bf16[32,128]{1,0:T(8,128)(2,1)S(1)} %broadcast_select_fusion.164), channel_id=1, source_target_pairs={{0,1},{1,2},{2,3},{3,4},{4,5},{5,6},{6,7},{7,8},{8,9},{9,10},{10,1... | collective-permute-start | bytes 24584 | tf_op jit(solution)/shard_map/ppermute | solution.py:12
  162.0 1.9 collective-permute-start.3
  163.9 1.3 scatter_custom_fusion.29
  165.3 1.4 scatter_fusion.28
  166.7 1.4 scatter_fusion.29
  168.1 1.4 scatter_fusion.30
  169.5 1.2 scatter_fusion.31
  170.8 1.2 scatter_fusion.32
  172.1 1.4 scatter_fusion.33
  173.5 1.2 scatter_fusion.34
  174.8 1.2 scatter_fusion.35
  176.1 1.2 scatter_fusion.36
  177.4 1.2 scatter_fusion.37
  178.7 1.3 scatter_fusion.38
  180.0 1.2 scatter_fusion.39
  181.3 1.2 scatter_fusion.40
  182.6 1.2 scatter_fusion.41
  183.9 1.2 scatter_fusion.42
  185.2 1.2 scatter_fusion.43
  186.5 1.2 scatter_fusion.44
  187.7 1.2 scatter_fusion.45
  189.0 1.2 scatter_fusion.46
  190.3 1.2 scatter_fusion.47
  191.6 1.2 scatter_fusion.48
  192.8 1.2 scatter_fusion.49
  194.1 1.2 scatter_fusion.50
  195.4 1.5 scatter_fusion.51
  196.8 1.2 scatter_fusion.52
  200.1 12.3 %collective-permute-start.7 = (f32[32,128]{1,0:T(8,128)}, f32[32,128]{1,0:T(8,128)}, u32[]{:S(2)}, u32[]{:S(2)}) collective-permute-start(f32[32,128]{1,0:T(8,128)} %get-tuple-element.1050), channel_id=1, source_target_pairs={{0,1},{1,2},{2,3},{3,4},{4,5},{5,6},{6,7},{7,8},{8,9},{9,10},{10,1... | collective-permute-start | bytes 49160 | tf_op jit(solution)/shard_map/ppermute | solution.py:12
  212.5 1.9 collective-permute-start.6
  242.1 1.4 gather_fusion.35
  245.2 1.4 gather_fusion.32
  269.2 489.8 %all-reduce.5.cloned.1.call-done = (f32[27,128,128]{2,1,0:T(8,128)}, f32[27,128,128]{2,1,0:T(8,128)}) async-done(((f32[27,128,128]{2,1,0:T(8,128)}, f32[27,128,128]{2,1,0:T(8,128)}), (f32[27,128,128]{2,1,0:T(8,128)}, f32[27,128,128]{2,1,0:T(8,128)})) %all-reduce.5.cloned.1.call-update) | async-done | bytes 3538960 | tf_op jit(solution)/shard_map/psum | solution.py:76
  759.0 2.7 multiply_convert_fusion.1
  (605 shorter events, 127.9 us)
Async XLA Ops:
  7.2 39.1 %copy-start = (bf16[128,128]{1,0:T(8,128)(2,1)S(1)}, bf16[128,128]{1,0:T(8,128)(2,1)}, u32[]{:S(2)}) copy-start(bf16[128,128]{1,0:T(8,128)(2,1)} %param.127) | copy-start | bytes 98308
  7.2 39.1 %copy-start.3 = (bf16[27,128,128]{2,1,0:T(8,128)(2,1)S(1)}, bf16[27,128,128]{2,1,0:T(8,128)(2,1)}, u32[]{:S(2)}) copy-start(bf16[27,128,128]{2,1,0:T(8,128)(2,1)} %param.126) | copy-start | bytes 2654212
  7.2 751.8 %all-reduce.5.cloned.1.call-start = ((), (), s32[]{:S(2)}) async-start(), calls=%async_computation | async-start | bytes 7077888 | tf_op jit(solution)/shard_map/psum | solution.py:76
  12.1 92.2 %collective-permute-start = (bf16[32,128]{1,0:T(8,128)(2,1)S(1)}, bf16[32,128]{1,0:T(8,128)(2,1)S(1)}, u32[]{:S(2)}, u32[]{:S(2)}) collective-permute-start(bf16[32,128]{1,0:T(8,128)(2,1)S(1)} %broadcast_select_fusion.165), channel_id=1, source_target_pairs={{0,1},{1,2},{2,3},{3,4},{4,5},{5,6},{6,7},{7,8},{8,9},{9,10},{10,1... | collective-permute-start | bytes 24584 | tf_op jit(solution)/shard_map/ppermute | solution.py:12
  31.3 73.0 %collective-permute-start.1 = (bf16[32,128]{1,0:T(8,128)(2,1)S(1)}, bf16[32,128]{1,0:T(8,128)(2,1)S(1)}, u32[]{:S(2)}, u32[]{:S(2)}) collective-permute-start(bf16[32,128]{1,0:T(8,128)(2,1)S(1)} %broadcast_select_fusion.163), channel_id=1, source_target_pairs={{1,0},{2,1},{3,2},{4,3},{5,4},{6,5},{7,6},{8,7},{9,8},{10,9},{11,1... | collective-permute-start | bytes 24584 | tf_op jit(solution)/shard_map/ppermute | solution.py:12
  34.2 36.7 %copy-start.129 = (s32[128]{0:T(128)}, s32[128]{0:T(128)S(1)}, u32[]{:S(2)}) copy-start(s32[128]{0:T(128)S(1)} %get-tuple-element.1075) | copy-start | bytes 1540
  34.2 38.0 %copy-start.127 = (s32[128]{0:T(128)}, s32[128]{0:T(128)S(1)}, u32[]{:S(2)}) copy-start(s32[128]{0:T(128)S(1)} %get-tuple-element.1076) | copy-start | bytes 1540
  34.2 39.2 %copy-start.125 = (s32[128]{0:T(128)}, s32[128]{0:T(128)S(1)}, u32[]{:S(2)}) copy-start(s32[128]{0:T(128)S(1)} %get-tuple-element.1077) | copy-start | bytes 1540
  34.2 40.5 %copy-start.121 = (s32[128]{0:T(128)}, s32[128]{0:T(128)S(1)}, u32[]{:S(2)}) copy-start(s32[128]{0:T(128)S(1)} %get-tuple-element.1078) | copy-start | bytes 1540
  34.3 41.8 %copy-start.119 = (s32[128]{0:T(128)}, s32[128]{0:T(128)S(1)}, u32[]{:S(2)}) copy-start(s32[128]{0:T(128)S(1)} %get-tuple-element.1079) | copy-start | bytes 1540
  34.3 43.0 %copy-start.117 = (s32[128]{0:T(128)}, s32[128]{0:T(128)S(1)}, u32[]{:S(2)}) copy-start(s32[128]{0:T(128)S(1)} %get-tuple-element.1080) | copy-start | bytes 1540
  34.3 44.3 %copy-start.115 = (s32[128]{0:T(128)}, s32[128]{0:T(128)S(1)}, u32[]{:S(2)}) copy-start(s32[128]{0:T(128)S(1)} %get-tuple-element.1081) | copy-start | bytes 1540
  34.3 45.5 %copy-start.113 = (s32[128]{0:T(128)}, s32[128]{0:T(128)S(1)}, u32[]{:S(2)}) copy-start(s32[128]{0:T(128)S(1)} %get-tuple-element.1082) | copy-start | bytes 1540
  34.3 46.8 %copy-start.111 = (s32[128]{0:T(128)}, s32[128]{0:T(128)S(1)}, u32[]{:S(2)}) copy-start(s32[128]{0:T(128)S(1)} %get-tuple-element.1074) | copy-start | bytes 1540
  35.4 22.7 %copy-start.149 = (s32[128]{0:T(128)}, s32[128]{0:T(128)S(1)}, u32[]{:S(2)}) copy-start(s32[128]{0:T(128)S(1)} %get-tuple-element.1064) | copy-start | bytes 1540
  35.4 23.9 %copy-start.147 = (s32[128]{0:T(128)}, s32[128]{0:T(128)S(1)}, u32[]{:S(2)}) copy-start(s32[128]{0:T(128)S(1)} %get-tuple-element.1065) | copy-start | bytes 1540
  35.4 25.2 %copy-start.145 = (s32[128]{0:T(128)}, s32[128]{0:T(128)S(1)}, u32[]{:S(2)}) copy-start(s32[128]{0:T(128)S(1)} %get-tuple-element.1066) | copy-start | bytes 1540
  35.4 26.5 %copy-start.143 = (s32[128]{0:T(128)}, s32[128]{0:T(128)S(1)}, u32[]{:S(2)}) copy-start(s32[128]{0:T(128)S(1)} %get-tuple-element.1067) | copy-start | bytes 1540
  35.4 27.7 %copy-start.141 = (s32[128]{0:T(128)}, s32[128]{0:T(128)S(1)}, u32[]{:S(2)}) copy-start(s32[128]{0:T(128)S(1)} %get-tuple-element.1068) | copy-start | bytes 1540
  35.4 29.0 %copy-start.139 = (s32[128]{0:T(128)}, s32[128]{0:T(128)S(1)}, u32[]{:S(2)}) copy-start(s32[128]{0:T(128)S(1)} %get-tuple-element.1069) | copy-start | bytes 1540
  35.5 30.2 %copy-start.137 = (s32[128]{0:T(128)}, s32[128]{0:T(128)S(1)}, u32[]{:S(2)}) copy-start(s32[128]{0:T(128)S(1)} %get-tuple-element.1070) | copy-start | bytes 1540
  35.5 31.5 %copy-start.135 = (s32[128]{0:T(128)}, s32[128]{0:T(128)S(1)}, u32[]{:S(2)}) copy-start(s32[128]{0:T(128)S(1)} %get-tuple-element.1071) | copy-start | bytes 1540
  35.5 32.7 %copy-start.133 = (s32[128]{0:T(128)}, s32[128]{0:T(128)S(1)}, u32[]{:S(2)}) copy-start(s32[128]{0:T(128)S(1)} %get-tuple-element.1072) | copy-start | bytes 1540
  35.5 34.2 %copy-start.131 = (s32[128]{0:T(128)}, s32[128]{0:T(128)S(1)}, u32[]{:S(2)}) copy-start(s32[128]{0:T(128)S(1)} %get-tuple-element.1073) | copy-start | bytes 1540
  35.5 46.9 %copy-start.123 = (s32[128]{0:T(128)}, s32[128]{0:T(128)S(1)}, u32[]{:S(2)}) copy-start(s32[128]{0:T(128)S(1)} %get-tuple-element.1056) | copy-start | bytes 1540
  83.6 49.1 %collective-permute-start.5 = (f32[32,128]{1,0:T(8,128)S(1)}, f32[32,128]{1,0:T(8,128)S(1)}, u32[]{:S(2)}, u32[]{:S(2)}) collective-permute-start(f32[32,128]{1,0:T(8,128)S(1)} %get-tuple-element.1052), channel_id=1, source_target_pairs={{0,1},{1,2},{2,3},{3,4},{4,5},{5,6},{6,7},{7,8},{8,9},{9,10},{10,1... | collective-permute-start | bytes 49160 | tf_op jit(solution)/shard_map/ppermute | solution.py:12
  96.0 35.8 %collective-permute-start.4 = (f32[32,128]{1,0:T(8,128)S(1)}, f32[32,128]{1,0:T(8,128)S(1)}, u32[]{:S(2)}, u32[]{:S(2)}) collective-permute-start(f32[32,128]{1,0:T(8,128)S(1)} %get-tuple-element.1053), channel_id=1, source_target_pairs={{1,0},{2,1},{3,2},{4,3},{5,4},{6,5},{7,6},{8,7},{9,8},{10,9},{11,1... | collective-permute-start | bytes 49160 | tf_op jit(solution)/shard_map/ppermute | solution.py:12
  98.4 27.3 %copy-start.91 = (pred[128]{0:T(512)(128)(4,1)}, pred[128]{0:T(512)(128)(4,1)S(1)}, u32[]{:S(2)}) copy-start(pred[128]{0:T(512)(128)(4,1)S(1)} %get-tuple-element.1129) | copy-start | bytes 388
  98.4 27.5 %copy-start.89 = (pred[128]{0:T(512)(128)(4,1)}, pred[128]{0:T(512)(128)(4,1)S(1)}, u32[]{:S(2)}) copy-start(pred[128]{0:T(512)(128)(4,1)S(1)} %get-tuple-element.1127) | copy-start | bytes 388
  98.4 27.9 %copy-start.84 = (pred[128]{0:T(512)(128)(4,1)}, pred[128]{0:T(512)(128)(4,1)S(1)}, u32[]{:S(2)}) copy-start(pred[128]{0:T(512)(128)(4,1)S(1)} %get-tuple-element.1123) | copy-start | bytes 388
  98.4 28.1 %copy-start.81 = (pred[128]{0:T(512)(128)(4,1)}, pred[128]{0:T(512)(128)(4,1)S(1)}, u32[]{:S(2)}) copy-start(pred[128]{0:T(512)(128)(4,1)S(1)} %get-tuple-element.1121) | copy-start | bytes 388
  98.4 28.3 %copy-start.78 = (pred[128]{0:T(512)(128)(4,1)}, pred[128]{0:T(512)(128)(4,1)S(1)}, u32[]{:S(2)}) copy-start(pred[128]{0:T(512)(128)(4,1)S(1)} %get-tuple-element.1119) | copy-start | bytes 388
  98.4 28.5 %copy-start.75 = (pred[128]{0:T(512)(128)(4,1)}, pred[128]{0:T(512)(128)(4,1)S(1)}, u32[]{:S(2)}) copy-start(pred[128]{0:T(512)(128)(4,1)S(1)} %get-tuple-element.1117) | copy-start | bytes 388
  98.4 29.8 %copy-start.87 = (pred[128]{0:T(512)(128)(4,1)}, pred[128]{0:T(512)(128)(4,1)S(1)}, u32[]{:S(2)}) copy-start(pred[128]{0:T(512)(128)(4,1)S(1)} %get-tuple-element.1125) | copy-start | bytes 388
  98.4 32.4 %copy-start.72 = (pred[128]{0:T(512)(128)(4,1)}, pred[128]{0:T(512)(128)(4,1)S(1)}, u32[]{:S(2)}) copy-start(pred[128]{0:T(512)(128)(4,1)S(1)} %get-tuple-element.998) | copy-start | bytes 388
  98.4 37.3 %copy-start.93 = (pred[128]{0:T(512)(128)(4,1)}, pred[128]{0:T(512)(128)(4,1)S(1)}, u32[]{:S(2)}) copy-start(pred[128]{0:T(512)(128)(4,1)S(1)} %get-tuple-element.1131) | copy-start | bytes 388
  98.5 28.6 %copy-start.69 = (pred[128]{0:T(512)(128)(4,1)}, pred[128]{0:T(512)(128)(4,1)S(1)}, u32[]{:S(2)}) copy-start(pred[128]{0:T(512)(128)(4,1)S(1)} %get-tuple-element.1115) | copy-start | bytes 388
  98.5 28.8 %copy-start.66 = (pred[128]{0:T(512)(128)(4,1)}, pred[128]{0:T(512)(128)(4,1)S(1)}, u32[]{:S(2)}) copy-start(pred[128]{0:T(512)(128)(4,1)S(1)} %get-tuple-element.1113) | copy-start | bytes 388
  98.5 29.1 %copy-start.63 = (pred[128]{0:T(512)(128)(4,1)}, pred[128]{0:T(512)(128)(4,1)S(1)}, u32[]{:S(2)}) copy-start(pred[128]{0:T(512)(128)(4,1)S(1)} %get-tuple-element.1111) | copy-start | bytes 388
  98.5 29.3 %copy-start.60 = (pred[128]{0:T(512)(128)(4,1)}, pred[128]{0:T(512)(128)(4,1)S(1)}, u32[]{:S(2)}) copy-start(pred[128]{0:T(512)(128)(4,1)S(1)} %get-tuple-element.1109) | copy-start | bytes 388
  98.6 29.5 %copy-start.57 = (pred[128]{0:T(512)(128)(4,1)}, pred[128]{0:T(512)(128)(4,1)S(1)}, u32[]{:S(2)}) copy-start(pred[128]{0:T(512)(128)(4,1)S(1)} %get-tuple-element.1107) | copy-start | bytes 388
  98.6 29.7 %copy-start.54 = (pred[128]{0:T(512)(128)(4,1)}, pred[128]{0:T(512)(128)(4,1)S(1)}, u32[]{:S(2)}) copy-start(pred[128]{0:T(512)(128)(4,1)S(1)} %get-tuple-element.1105) | copy-start | bytes 388
  98.6 29.9 %copy-start.51 = (pred[128]{0:T(512)(128)(4,1)}, pred[128]{0:T(512)(128)(4,1)S(1)}, u32[]{:S(2)}) copy-start(pred[128]{0:T(512)(128)(4,1)S(1)} %get-tuple-element.1103) | copy-start | bytes 388
  98.6 30.1 %copy-start.48 = (pred[128]{0:T(512)(128)(4,1)}, pred[128]{0:T(512)(128)(4,1)S(1)}, u32[]{:S(2)}) copy-start(pred[128]{0:T(512)(128)(4,1)S(1)} %get-tuple-element.1101) | copy-start | bytes 388
  98.6 30.3 %copy-start.45 = (pred[128]{0:T(512)(128)(4,1)}, pred[128]{0:T(512)(128)(4,1)S(1)}, u32[]{:S(2)}) copy-start(pred[128]{0:T(512)(128)(4,1)S(1)} %get-tuple-element.1099) | copy-start | bytes 388
  98.6 30.5 %copy-start.42 = (pred[128]{0:T(512)(128)(4,1)}, pred[128]{0:T(512)(128)(4,1)S(1)}, u32[]{:S(2)}) copy-start(pred[128]{0:T(512)(128)(4,1)S(1)} %get-tuple-element.1097) | copy-start | bytes 388
  98.6 30.7 %copy-start.39 = (pred[128]{0:T(512)(128)(4,1)}, pred[128]{0:T(512)(128)(4,1)S(1)}, u32[]{:S(2)}) copy-start(pred[128]{0:T(512)(128)(4,1)S(1)} %get-tuple-element.1095) | copy-start | bytes 388
  98.6 30.9 %copy-start.36 = (pred[128]{0:T(512)(128)(4,1)}, pred[128]{0:T(512)(128)(4,1)S(1)}, u32[]{:S(2)}) copy-start(pred[128]{0:T(512)(128)(4,1)S(1)} %get-tuple-element.1093) | copy-start | bytes 388
  98.6 31.1 %copy-start.33 = (pred[128]{0:T(512)(128)(4,1)}, pred[128]{0:T(512)(128)(4,1)S(1)}, u32[]{:S(2)}) copy-start(pred[128]{0:T(512)(128)(4,1)S(1)} %get-tuple-element.1091) | copy-start | bytes 388
  98.6 31.3 %copy-start.30 = (pred[128]{0:T(512)(128)(4,1)}, pred[128]{0:T(512)(128)(4,1)S(1)}, u32[]{:S(2)}) copy-start(pred[128]{0:T(512)(128)(4,1)S(1)} %get-tuple-element.1089) | copy-start | bytes 388
  98.7 31.6 %copy-start.28 = (pred[128]{0:T(512)(128)(4,1)}, pred[128]{0:T(512)(128)(4,1)S(1)}, u32[]{:S(2)}) copy-start(pred[128]{0:T(512)(128)(4,1)S(1)} %get-tuple-element.1087) | copy-start | bytes 388
  98.7 31.8 %copy-start.26 = (pred[128]{0:T(512)(128)(4,1)}, pred[128]{0:T(512)(128)(4,1)S(1)}, u32[]{:S(2)}) copy-start(pred[128]{0:T(512)(128)(4,1)S(1)} %get-tuple-element.1085) | copy-start | bytes 388
  98.7 35.0 %copy-start.95 = (pred[128]{0:T(512)(128)(4,1)}, pred[128]{0:T(512)(128)(4,1)S(1)}, u32[]{:S(2)}) copy-start(pred[128]{0:T(512)(128)(4,1)S(1)} %get-tuple-element.996) | copy-start | bytes 388
  98.7 26.0 %copy-start.98 = (s32[1024]{0:T(1024)}, s32[1024]{0:T(1024)S(1)}, u32[]{:S(2)}) copy-start(s32[1024]{0:T(1024)S(1)} %pad_clamp_fusion.26) | copy-start | bytes 12292
  98.7 32.3 %copy-start.106 = (s32[1024]{0:T(1024)}, s32[1024]{0:T(1024)S(1)}, u32[]{:S(2)}) copy-start(s32[1024]{0:T(1024)S(1)} %pad_clamp_fusion) | copy-start | bytes 12292
  98.8 22.4 %copy-start.100 = (s32[1024]{0:T(1024)}, s32[1024]{0:T(1024)S(1)}, u32[]{:S(2)}) copy-start(s32[1024]{0:T(1024)S(1)} %get-tuple-element.1138) | copy-start | bytes 12292
  98.8 23.0 %copy-start.103 = (s32[1024]{0:T(1024)}, s32[1024]{0:T(1024)S(1)}, u32[]{:S(2)}) copy-start(s32[1024]{0:T(1024)S(1)} %get-tuple-element.1139) | copy-start | bytes 12292
  98.8 23.7 %copy-start.102 = (s32[1024]{0:T(1024)}, s32[1024]{0:T(1024)S(1)}, u32[]{:S(2)}) copy-start(s32[1024]{0:T(1024)S(1)} %get-tuple-element.1140) | copy-start | bytes 12292
  98.8 24.4 %copy-start.105 = (s32[1024]{0:T(1024)}, s32[1024]{0:T(1024)S(1)}, u32[]{:S(2)}) copy-start(s32[1024]{0:T(1024)S(1)} %get-tuple-element.1141) | copy-start | bytes 12292
  98.9 25.1 %copy-start.104 = (s32[1024]{0:T(1024)}, s32[1024]{0:T(1024)S(1)}, u32[]{:S(2)}) copy-start(s32[1024]{0:T(1024)S(1)} %get-tuple-element.1142) | copy-start | bytes 12292
  149.7 72.2 %collective-permute-start.2 = (bf16[32,128]{1,0:T(8,128)(2,1)S(1)}, bf16[32,128]{1,0:T(8,128)(2,1)S(1)}, u32[]{:S(2)}, u32[]{:S(2)}) collective-permute-start(bf16[32,128]{1,0:T(8,128)(2,1)S(1)} %broadcast_select_fusion.164), channel_id=1, source_target_pairs={{0,1},{1,2},{2,3},{3,4},{4,5},{5,6},{6,7},{7,8},{8,9},{9,10},{10,1... | collective-permute-start | bytes 24584 | tf_op jit(solution)/shard_map/ppermute | solution.py:12
  162.0 61.1 %collective-permute-start.3 = (bf16[32,128]{1,0:T(8,128)(2,1)S(1)}, bf16[32,128]{1,0:T(8,128)(2,1)S(1)}, u32[]{:S(2)}, u32[]{:S(2)}) collective-permute-start(bf16[32,128]{1,0:T(8,128)(2,1)S(1)} %broadcast_select_fusion.162), channel_id=1, source_target_pairs={{1,0},{2,1},{3,2},{4,3},{5,4},{6,5},{7,6},{8,7},{9,8},{10,9},{11,1... | collective-permute-start | bytes 24584 | tf_op jit(solution)/shard_map/ppermute | solution.py:12
  200.1 67.4 %collective-permute-start.7 = (f32[32,128]{1,0:T(8,128)}, f32[32,128]{1,0:T(8,128)}, u32[]{:S(2)}, u32[]{:S(2)}) collective-permute-start(f32[32,128]{1,0:T(8,128)} %get-tuple-element.1050), channel_id=1, source_target_pairs={{0,1},{1,2},{2,3},{3,4},{4,5},{5,6},{6,7},{7,8},{8,9},{9,10},{10,1... | collective-permute-start | bytes 49160 | tf_op jit(solution)/shard_map/ppermute | solution.py:12
  212.5 54.0 %collective-permute-start.6 = (f32[32,128]{1,0:T(8,128)}, f32[32,128]{1,0:T(8,128)}, u32[]{:S(2)}, u32[]{:S(2)}) collective-permute-start(f32[32,128]{1,0:T(8,128)} %get-tuple-element.1051), channel_id=1, source_target_pairs={{1,0},{2,1},{3,2},{4,3},{5,4},{6,5},{7,6},{8,7},{9,8},{10,9},{11,1... | collective-permute-start | bytes 49160 | tf_op jit(solution)/shard_map/ppermute | solution.py:12
  (110 other events, 903.2 us)
Sparse Core Ops, SparseCore 0:
  264.6 494.3 all-reduce.4
where the time goes:
time: 781 us; the launch traced here: 770 us
  waiting for transfers between devices  490 us (63%)
  other arithmetic  90.3 us (12%)
  starting transfers between devices  62 us (8%)
  matrix products  56.6 us (7%)
  local copies, waits for them, and re-layouts  52.5 us (7%)
  between operations  18.9 us (2%)
    psum x1, waiting for transfers between devices, reduce_kernel(): total = lax.psum(kernel_acc, ('dp', 'slab'))  490 us
    scatter-add x54, other arithmetic, backprop_one_block(): ext_grad = ext_grad.at[neighbours[:, offset]].add(back)  68.2 us
    ppermute x8, starting transfers between devices, from_behind(): return lax.ppermute(block, axis, route)  61.9 us
    gather x54, local copies, waits for them, and re-layouts, convolve_one_block(): picked = jnp.take(extended, neighbours[:, offset], axis=0)  44.7 us
    dot_general x54, matrix products, backprop_one_block(): lax.dot_general(grad_out, weight[offset], (((1,), (1,)), ((), ())), prefe...  27.3 us
    dot_general x54, matrix products, backprop_one_block(): lax.dot_general(picked, grad_out, (((0,), (0,)), ((), ())), preferred_ele...  15.8 us
  transfers between devices with their start and end apart: 9, of which 1 were waited for; matrix products, arithmetic and copies ran while one was open for 22% of the time, Pallas kernels for 0%

commit v1 on v0

v1 whole, which is shorter than its diff:
```python
import math

import jax
import jax.numpy as jnp
from jax import lax
from jax.experimental import pallas as pl
from jax.experimental.pallas import tpu as pltpu
from jax.sharding import Mesh, PartitionSpec as P

AXES = ("dp", "y", "x", "zh", "core")
SLAB = ("y", "x", "zh", "core")
PLANE = ("y", "x")
DEPTH = ("dp", "zh")
BF = jnp.bfloat16
F32 = jnp.float32
WIDE = 256
TILE = 16


def dot(a, b, contract=(1, 0), exact=False):
    return lax.dot_general(
        a,
        b,
        (((contract[0],), (contract[1],)), ((), ())),
        preferred_element_type=F32,
        precision=lax.Precision.HIGHEST if exact else None,
    )


def live_rows(counts_ref, sites):
    return lax.broadcasted_iota(jnp.int32, (sites, 1), 0) < counts_ref[0]


def face_sites(faces_ref, sites):
    row = faces_ref[...]
    return (lax.broadcasted_iota(jnp.int32, (sites, row.shape[1]), 0) == row).astype(F32)


def pick_matrix(nb_ref, offset):
    sites = nb_ref.shape[0]
    column = nb_ref[:, offset : offset + 1]
    lanes = lax.broadcasted_iota(jnp.int32, (sites, WIDE), 1)
    return jnp.where(lanes == column, 1.0, 0.0).astype(BF)


def spread(grad, picks, w_ref, kept):
    turned = grad.T.astype(BF)
    offsets = w_ref.shape[0]
    total = jnp.zeros((w_ref.shape[1], WIDE), F32)
    for k in range(offsets):
        kept[k] = dot(turned, picks(k)).astype(BF)
        total = total + dot(w_ref[k], kept[k])
    return total.T


def gather_conv(extended, picks, w_ref):
    total = jnp.zeros((w_ref.shape[1], w_ref.shape[2]), F32)
    for k in range(w_ref.shape[0]):
        total = total + dot(dot(picks(k), extended).astype(BF), w_ref[k])
    return total


def kernel_grad(extended, kept, out_ref):
    turned = extended.astype(F32).T.astype(BF)
    offsets = kept.shape[0]
    for k in range(offsets):
        out_ref[k] = dot(turned, kept[k], (1, 1)).astype(BF)
    out_ref[offsets] = jnp.zeros(out_ref.shape[1:], BF)


def extend(values, below, above):
    rim = below.shape[0]
    pad = jnp.zeros((WIDE - values.shape[0] - 2 * rim, values.shape[1]), F32)
    return jnp.concatenate([values, below, above, pad], 0).astype(BF)


def send_rows(values, ext_grad, low, high, up_ref, down_ref, sites):
    rim = low.shape[1]
    up_ref[:rim] = dot(high.T.astype(BF), values)
    up_ref[rim:] = ext_grad[sites + rim : sites + 2 * rim]
    down_ref[:rim] = dot(low.T.astype(BF), values)
    down_ref[rim:] = ext_grad[sites : sites + rim]


def retract(own, below_ref, above_ref, low, high):
    rim = low.shape[1]
    own = own + dot(high, above_ref[rim:], exact=True)
    return own + dot(low, below_ref[rim:], exact=True)


def first_kernel(
    counts, feat, nb, low_ref, high_ref, cot, w_two, up, down, own, kept
):
    sites = feat.shape[0]
    live = live_rows(counts, sites)
    low, high = face_sites(low_ref, sites), face_sites(high_ref, sites)
    masked = jnp.where(live, feat[...].astype(F32), 0.0).astype(BF)
    out_grad = jnp.where(live, cot[...].astype(F32), 0.0)
    ext_grad = spread(out_grad, lambda k: pick_matrix(nb, k), w_two, kept)
    own[...] = ext_grad[:sites]
    send_rows(masked, ext_grad, low, high, up, down, sites)


def second_kernel(
    counts, feat, nb, low_ref, high_ref, below, above, hidden_own, w_one,
    up, down, own, hidden_ref, sums, picks, kept,
):
    sites = feat.shape[0]
    rim = low_ref.shape[1]
    live = live_rows(counts, sites)
    low, high = face_sites(low_ref, sites), face_sites(high_ref, sites)
    for k in range(w_one.shape[0]):
        picks[k] = pick_matrix(nb, k)
    masked = jnp.where(live, feat[...].astype(F32), 0.0)
    extended = extend(masked, below[:rim], above[:rim])
    x = gather_conv(extended, lambda k: picks[k], w_one)
    slope = math.sqrt(2.0 / math.pi)
    t = jnp.tanh(slope * (x + 0.044715 * (x * x * x)))
    cdf = 0.5 * (1.0 + t)
    hidden = jnp.where(live, x * cdf, 0.0).astype(BF)
    hidden_ref[...] = hidden
    bend = cdf + 0.5 * x * (1.0 - t * t) * (slope * (1.0 + 3 * 0.044715 * (x * x)))
    hidden_grad = retract(hidden_own[...], below, above, low, high)
    pre_grad = jnp.where(live, bend * hidden_grad, 0.0)
    ext_grad = spread(pre_grad, lambda k: picks[k], w_one, kept)
    own[...] = ext_grad[:sites]
    send_rows(hidden, ext_grad, low, high, up, down, sites)
    kernel_grad(extended, kept, sums)


def third_kernel(
    counts, hidden, nb, low_ref, high_ref, below, above, input_own, w_two, kept,
    response, input_grad, sums,
):
    sites = hidden.shape[0]
    rim = low_ref.shape[1]
    live = live_rows(counts, sites)
    low, high = face_sites(low_ref, sites), face_sites(high_ref, sites)
    extended = extend(hidden[...].astype(F32), below[:rim], above[:rim])
    kernel_grad(extended, kept, sums)
    second_pre = gather_conv(extended, lambda k: pick_matrix(nb, k), w_two)
    response[...] = jnp.where(live, second_pre, 0.0).astype(BF)
    grad = retract(input_own[...], below, above, low, high)
    input_grad[...] = jnp.where(live, grad, 0.0).astype(BF)


def call(kernel, outs, scratch=(), **cost):
    def run(*args):
        specs = [pl.BlockSpec(memory_space=pltpu.SMEM)]
        specs += [pl.BlockSpec(memory_space=pltpu.VMEM)] * (len(args) - 1)
        return pl.pallas_call(
            kernel,
            out_shape=[jax.ShapeDtypeStruct(s, d) for s, d in outs],
            in_specs=specs,
            out_specs=[pl.BlockSpec(memory_space=pltpu.VMEM)] * len(outs),
            scratch_shapes=[pltpu.VMEM(s, d) for s, d in scratch],
            compiler_params=pltpu.CompilerParams(vmem_limit_bytes=40 * 2**20),
        )(*args)

    return run


def neighbours_of(up, down):
    last = lax.axis_size(SLAB) - 1
    below = lax.ppermute(up, SLAB, [(i, i + 1) for i in range(last)])
    above = lax.ppermute(down, SLAB, [(i + 1, i) for i in range(last)])
    return below, above


def swap(block, axis):
    return lax.all_to_all(block, axis, 0, 0, tiled=True)


def total_of(parts):
    return jnp.sum(parts.astype(F32), 0)


def scatter_plane(sums):
    rows, channels = sums.shape[0] * sums.shape[1], sums.shape[2]
    cores, plane = lax.axis_size("core"), lax.axis_size(PLANE)
    halves = swap(sums.reshape(cores, rows // cores, channels), "core")
    share = total_of(halves).astype(BF).reshape(plane, -1, channels)
    return total_of(swap(share, PLANE))


def finish(shares, scaling, offsets, channels):
    grads, rows = len(shares), shares[0].shape[0]
    depth, plane, cores = lax.axis_size(DEPTH), lax.axis_size(PLANE), lax.axis_size("core")
    parts = jnp.stack(shares).reshape(grads, depth, rows // depth, channels)
    parts = parts.transpose(1, 0, 2, 3)
    mine = (total_of(swap(parts, DEPTH)) * scaling).astype(BF)
    column = swap(jnp.broadcast_to(mine, (depth, *mine.shape)), DEPTH)
    column = column.transpose(1, 0, 2, 3).reshape(grads, rows, channels)
    whole = swap(jnp.broadcast_to(column, (plane, *column.shape)), PLANE)
    whole = swap(jnp.broadcast_to(whole, (cores, *whole.shape)), "core")
    whole = whole.transpose(2, 0, 1, 3, 4).reshape(grads, -1, channels, channels)
    return [whole[g, :offsets] for g in range(grads)]


def on_device(feat, counts, nb, low, high, w_one, w_two, cot):
    sites, channels = feat.shape
    offsets, rim = nb.shape[1], low.shape[0]
    scaling = 1.0 / math.sqrt(lax.axis_size(AXES) * sites)
    low, high = low.reshape(1, rim), high.reshape(1, rim)
    rims = ((2 * rim, channels), F32)
    field = ((sites, channels), F32)
    kept = ((offsets, channels, WIDE), BF)
    picks = ((offsets, sites, WIDE), BF)
    sums = ((offsets + 1, channels, channels), BF)
    flat = ((sites, channels), BF)
    up, down, hidden_own, kept_two = call(first_kernel, (rims, rims, field, kept))(
        counts, feat, nb, low, high, cot, w_two
    )
    below, above = neighbours_of(up, down)
    up, down, input_own, hidden, sums_one = call(
        second_kernel, (rims, rims, field, flat, sums), (picks, kept)
    )(counts, feat, nb, low, high, below, above, hidden_own, w_one)
    below, above = neighbours_of(up, down)
    share_one = scatter_plane(sums_one)
    response, input_grad, sums_two = call(third_kernel, (flat, flat, sums))(
        counts, hidden, nb, low, high, below, above, input_own, w_two, kept_two
    )
    share_two = scatter_plane(sums_two)
    first, second = finish((share_one, share_two), scaling, offsets, channels)
    return response, input_grad, first, second


def solution(mesh):
    groups, slabs = mesh.devices.shape
    side = {64: 4, 16: 2, 4: 1}[slabs]
    fine = Mesh(mesh.devices.reshape(groups, side, side, 2, 2), AXES)
    rows, row = P(AXES, None), P(AXES)
    return jax.shard_map(
        on_device,
        mesh=fine,
        in_specs=(rows, row, rows, row, row, P(), P(), rows),
        out_specs=(rows, rows, P(), P()),
        check_vma=False,
    )
```

time: 781 us -> 160 us (0.20); the launches traced: 770 us -> 159 us
  waiting for transfers between devices: 490 us -> 34.1 us
  other arithmetic: 90.3 us -> 3.49 us
  blocking collectives: 0 us -> 69.4 us
  matrix products: 56.6 us -> 0 us
  local copies, waits for them, and re-layouts: 52.5 us -> 8.01 us
  starting transfers between devices: 62 us -> 34.6 us
  between operations: 18.9 us -> 1.46 us
  Pallas kernels: 0 us -> 7.83 us
    psum x1 -> x0, waiting for transfers between devices: 490 us -> none  [reduce_kernel(): total = lax.psum(kernel_acc, ('dp', 'slab'))]
    scatter-add x58 -> x0, other arithmetic: 71.9 us -> none  [the longest x54 68.2 us: backprop_one_block(): ext_grad = ext_grad.at[neighbours[:, offset]].add(back)]
    all_to_all x0 -> x6, blocking collectives: none -> 69.4 us  [swap(): return lax.all_to_all(block, axis, 0, 0, tiled=True)]
    dot_general x162 -> x0, matrix products: 56.6 us -> none  [the longest x54 27.3 us: backprop_one_block(): lax.dot_general(grad_out, weight[offset], (((1,), (1,)), ((), ())), prefe...]
    gather x58 -> x0, local copies, waits for them, and re-layouts: 47.7 us -> none  [the longest x54 44.7 us: convolve_one_block(): picked = jnp.take(extended, neighbours[:, offset], axis=0)]
    ppermute x8 -> x4, starting transfers between devices: 61.9 us -> 23.2 us  [the longest x2 18.9 us: neighbours_of(): below = lax.ppermute(up, SLAB, [(i, i + 1) for i in range(last)])]
    all_to_all x0 -> x2, waiting for transfers between devices: none -> 17.7 us  [swap(): return lax.all_to_all(block, axis, 0, 0, tiled=True)]
    ppermute x8 -> x4, waiting for transfers between devices: 0.02 us -> 16.4 us  [the longest x2 16.4 us: neighbours_of(): above = lax.ppermute(down, SLAB, [(i + 1, i) for i in range(last)])]
  transfers between devices with their start and end apart: 9 -> 6, of which waited for: 1 -> 4; matrix products, arithmetic and copies ran while one was open for 22% -> 2% of each run, Pallas kernels for 0% -> 0%
where the time goes in v1:
time: 160 us; the launch traced here: 159 us
  blocking collectives  69.4 us (43%)
  starting transfers between devices  34.6 us (22%)
  waiting for transfers between devices  34.1 us (21%)
  local copies, waits for them, and re-layouts  8.01 us (5%)
  Pallas kernels  7.83 us (5%)
  other arithmetic  3.49 us (2%)
    all_to_all x6, blocking collectives, swap(): return lax.all_to_all(block, axis, 0, 0, tiled=True)  69.4 us
    ppermute x2, starting transfers between devices, neighbours_of(): below = lax.ppermute(up, SLAB, [(i, i + 1) for i in range(last)])  18.9 us
    all_to_all x2, waiting for transfers between devices, swap(): return lax.all_to_all(block, axis, 0, 0, tiled=True)  17.7 us
    ppermute x2, waiting for transfers between devices, neighbours_of(): above = lax.ppermute(down, SLAB, [(i + 1, i) for i in range(last)])  16.4 us
    all_to_all x2, starting transfers between devices, swap(): return lax.all_to_all(block, axis, 0, 0, tiled=True)  11.4 us
    pallas_call x3, Pallas kernels, run(): pl.pallas_call(kernel, out_shape=[jax.ShapeDtypeStruct(s, d) for s, d in...  7.83 us
    unnamed x19, local copies, waits for them, and re-layouts  5.99 us
    ppermute x2, starting transfers between devices, neighbours_of(): above = lax.ppermute(down, SLAB, [(i + 1, i) for i in range(last)])  4.32 us
  transfers between devices with their start and end apart: 6, of which 4 were waited for; matrix products, arithmetic and copies ran while one was open for 2% of the time, Pallas kernels for 0%

profile of v1, /device:TPU:1, one launch (start us, length us, event | category | flops | bytes accessed | tf_op | source)
XLA Modules:
  0.0 158.9 jit_solution(10595424790699139135)
XLA Ops:
  1.3 0.8 copy.37.nb
  2.1 0.0 copy-start
  2.1 1.2 copy-done
  3.3 0.0 copy-start.3
  3.3 0.8 copy-done.3
  4.0 0.0 copy-start.4
  4.0 0.8 copy-done.4
  4.8 0.0 copy-start.5
  4.8 0.7 copy-done.5
  5.4 0.0 copy-start.7
  5.4 0.7 copy-done.7
  6.1 1.4 shard_map.111
  7.5 16.8 %collective-permute-start = (f32[64,128]{1,0:T(8,128)S(1)}, f32[64,128]{1,0:T(8,128)S(1)}, u32[]{:S(2)}, u32[]{:S(2)}) collective-permute-start(f32[64,128]{1,0:T(8,128)S(1)} %get-tuple-element.16), channel_id=1, source_target_pairs={{0,1},{1,2},{2,3},{3,4},{4,5},{5,6},{6,7},{7,8},{8,9},{9,10},{10,1... | collective-permute-start | bytes 98312 | tf_op jit(solution)/shard_map/ppermute | solution.py:165
  24.3 1.9 %collective-permute-start.1 = (f32[64,128]{1,0:T(8,128)S(1)}, f32[64,128]{1,0:T(8,128)S(1)}, u32[]{:S(2)}, u32[]{:S(2)}) collective-permute-start(f32[64,128]{1,0:T(8,128)S(1)} %get-tuple-element.17), channel_id=1, source_target_pairs={{1,0},{2,1},{3,2},{4,3},{5,4},{6,5},{7,6},{8,7},{9,8},{10,9},{11,1... | collective-permute-start | bytes 98312 | tf_op jit(solution)/shard_map/ppermute | solution.py:166
  26.2 0.0 collective-permute-done.below
  26.2 12.0 %collective-permute-done.1.above = f32[64,128]{1,0:T(8,128)S(1)} collective-permute-done((f32[64,128]{1,0:T(8,128)S(1)}, f32[64,128]{1,0:T(8,128)S(1)}, u32[]{:S(2)}, u32[]{:S(2)}) %collective-permute-start.1) | collective-permute-done | bytes 32800 | tf_op jit(solution)/shard_map/ppermute | solution.py:166
  38.2 0.0 copy-start.2
  38.2 1.2 copy-done.2
  39.4 3.7 %shard_map.112 = (f32[64,128]{1,0:T(8,128)S(1)}, f32[64,128]{1,0:T(8,128)S(1)}, f32[128,128]{1,0:T(8,128)S(1)}, bf16[128,128]{1,0:T(8,128)(2,1)S(1)}, bf16[28,128,128]{2,1,0:T(8,128)(2,1)S(1)}) custom-call(s32[1]{0:T(128)S(6)} %copy.49.counts, bf16[128,128]{1,0:T(8,128)(2,1)S(1)} %copy-done.3, s32[128,27]{1,0:T(8,128)S(1)} %copy.37.nb, ...), custom_call_target="tpu_custom_call" | custom-call | tf_op jit(solution)/shard_map/pallas_call | solution.py:151
  43.1 0.0 copy-start.1
  43.1 0.0 copy-start.6
  43.1 0.0 copy-start.8
  43.1 2.1 %collective-permute-start.2 = (f32[64,128]{1,0:T(8,128)S(1)}, f32[64,128]{1,0:T(8,128)S(1)}, u32[]{:S(2)}, u32[]{:S(2)}) collective-permute-start(f32[64,128]{1,0:T(8,128)S(1)} %get-tuple-element.20), channel_id=1, source_target_pairs={{0,1},{1,2},{2,3},{3,4},{4,5},{5,6},{6,7},{7,8},{8,9},{9,10},{10,1... | collective-permute-start | bytes 98312 | tf_op jit(solution)/shard_map/ppermute | solution.py:165
  45.2 2.4 %collective-permute-start.3 = (f32[64,128]{1,0:T(8,128)S(1)}, f32[64,128]{1,0:T(8,128)S(1)}, u32[]{:S(2)}, u32[]{:S(2)}) collective-permute-start(f32[64,128]{1,0:T(8,128)S(1)} %get-tuple-element.21), channel_id=1, source_target_pairs={{1,0},{2,1},{3,2},{4,3},{5,4},{6,5},{7,6},{8,7},{9,8},{10,9},{11,1... | collective-permute-start | bytes 98312 | tf_op jit(solution)/shard_map/ppermute | solution.py:166
  47.6 4.9 %all_to_all.40 = bf16[2,1792,128]{2,1,0:T(8,128)(2,1)} all-to-all(bf16[2,1792,128]{2,1,0:T(8,128)(2,1)S(1)} %bitcast.18), channel_id=1, replica_groups=mesh['dp'=8,'y'=4,'x'=4,'zh'=2,'core'=2] {'core'}, dimensions={0} | all-to-all | bytes 1835008 | tf_op jit(solution)/shard_map/all_to_all | solution.py:171
  52.5 2.2 %reduce_sum.51 = bf16[1792,128]{1,0:T(8,128)(2,1)} reduce(bf16[2,1792,128]{2,1,0:T(8,128)(2,1)} %all_to_all.40, bf16[]{:T(256)} %constant.4.clone.1), dimensions={0}, to_apply=%region_0.0 | reduce | flops 229376 | bytes 1376258 | tf_op jit(solution)/shard_map/reduce_sum | solution.py:175
  54.7 0.0 collective-permute-done.2.below
  54.7 4.4 %collective-permute-done.3.above = f32[64,128]{1,0:T(8,128)S(1)} collective-permute-done((f32[64,128]{1,0:T(8,128)S(1)}, f32[64,128]{1,0:T(8,128)S(1)}, u32[]{:S(2)}, u32[]{:S(2)}) %collective-permute-start.3) | collective-permute-done | bytes 32800 | tf_op jit(solution)/shard_map/ppermute | solution.py:166
  59.1 0.0 copy-done.1
  59.1 0.0 copy-done.6
  59.1 0.0 copy-done.8
  59.1 2.8 %shard_map.113 = (bf16[128,128]{1,0:T(8,128)(2,1)}, bf16[128,128]{1,0:T(8,128)(2,1)}, bf16[28,128,128]{2,1,0:T(8,128)(2,1)S(1)}) custom-call(s32[1]{0:T(128)S(6)} %copy.49.counts, bf16[128,128]{1,0:T(8,128)(2,1)S(1)} %get-tuple-element.19.hidden, s32[128,27]{1,0:T(8,128)S(1)} %copy.37.nb, s32[1,32]{1,0:T(1,128)S(1)} %bitcast.22, s32[1,32]{1,0:T(1,128)S(1)} %bitcast.25, ...), custom_call_target="tpu_custom_call" | custom-call | tf_op jit(solution)/shard_map/pallas_call | solution.py:151
  61.9 4.1 %all_to_all.41 = bf16[2,1792,128]{2,1,0:T(8,128)(2,1)S(1)} all-to-all(bf16[2,1792,128]{2,1,0:T(8,128)(2,1)S(1)} %bitcast.19), channel_id=1, replica_groups=mesh['dp'=8,'y'=4,'x'=4,'zh'=2,'core'=2] {'core'}, dimensions={0} | all-to-all | bytes 1835008 | tf_op jit(solution)/shard_map/all_to_all | solution.py:171
  66.0 7.8 %all-to-all-start.1 = ((bf16[16,112,128]{2,1,0:T(8,128)(2,1)}), bf16[16,112,128]{2,1,0:T(8,128)(2,1)S(1)}, u32[]{:S(2)}, u32[]{:S(2)}) async-start(bf16[16,112,128]{2,1,0:T(8,128)(2,1)} %bitcast.3), calls=%async_computation.1 | async-start | bytes 917504 | tf_op jit(solution)/shard_map/all_to_all | solution.py:171
  73.8 1.0 reduce_sum.53
  74.9 8.9 %all-to-all-done.1 = bf16[16,112,128]{2,1,0:T(8,128)(2,1)S(1)} async-done(((bf16[16,112,128]{2,1,0:T(8,128)(2,1)}), bf16[16,112,128]{2,1,0:T(8,128)(2,1)S(1)}, u32[]{:S(2)}, u32[]{:S(2)}) %all-to-all-start.1) | async-done | bytes 458784 | tf_op jit(solution)/shard_map/all_to_all | solution.py:171
  83.8 3.6 %all-to-all-start.3 = ((bf16[16,112,128]{2,1,0:T(8,128)(2,1)}), bf16[16,112,128]{2,1,0:T(8,128)(2,1)S(1)}, u32[]{:S(2)}, u32[]{:S(2)}) async-start(bf16[16,112,128]{2,1,0:T(8,128)(2,1)} %bitcast.5), calls=%async_computation.3 | async-start | bytes 917504 | tf_op jit(solution)/shard_map/all_to_all | solution.py:171
  87.3 0.1 convert_reduce_fusion.1
  87.4 8.8 %all-to-all-done.3 = bf16[16,112,128]{2,1,0:T(8,128)(2,1)S(1)} async-done(((bf16[16,112,128]{2,1,0:T(8,128)(2,1)}), bf16[16,112,128]{2,1,0:T(8,128)(2,1)S(1)}, u32[]{:S(2)}, u32[]{:S(2)}) %all-to-all-start.3) | async-done | bytes 458784 | tf_op jit(solution)/shard_map/all_to_all | solution.py:171
  96.2 0.1 convert_reduce_fusion
  96.3 0.1 copy.39
  96.4 20.2 %all_to_all.42 = f32[16,2,7,128]{3,1,2,0:T(2,128)S(1)} all-to-all(f32[16,2,7,128]{3,1,2,0:T(2,128)S(1)} %copy.39), channel_id=1, replica_groups=mesh['dp'=8,'y'=4,'x'=4,'zh'=2,'core'=2] {'dp','zh'}, dimensions={0} | all-to-all | bytes 229376 | tf_op jit(solution)/shard_map/all_to_all | solution.py:171
  116.7 0.1 reduce_sum.55
  116.8 14.7 %all_to_all.43 = bf16[16,2,7,128]{3,1,2,0:T(2,128)(2,1)S(1)} all-to-all(bf16[16,2,7,128]{3,1,2,0:T(2,128)(2,1)S(1)} %broadcast_in_dim.9), channel_id=1, replica_groups=mesh['dp'=8,'y'=4,'x'=4,'zh'=2,'core'=2] {'dp','zh'}, dimensions={0} | all-to-all | bytes 114688 | tf_op jit(solution)/shard_map/all_to_all | solution.py:171
  131.5 0.1 broadcast_in_dim.10
  131.6 13.9 %all_to_all.44 = bf16[16,2,112,128]{3,2,1,0:T(8,128)(2,1)S(1)} all-to-all(bf16[16,2,112,128]{3,2,1,0:T(8,128)(2,1)S(1)} %broadcast_in_dim.10), channel_id=1, replica_groups=mesh['dp'=8,'y'=4,'x'=4,'zh'=2,'core'=2] {'y','x'}, dimensions={0} | all-to-all | bytes 1835008 | tf_op jit(solution)/shard_map/all_to_all | solution.py:171
  145.5 0.1 copy.43
  145.5 0.2 broadcast_in_dim.11
  145.8 11.6 %all_to_all.45 = bf16[2,16,2,112,128]{4,3,1,2,0:T(8,128)(2,1)S(1)} all-to-all(bf16[2,16,2,112,128]{4,3,1,2,0:T(8,128)(2,1)S(1)} %broadcast_in_dim.11), channel_id=1, replica_groups=mesh['dp'=8,'y'=4,'x'=4,'zh'=2,'core'=2] {'core'}, dimensions={0} | all-to-all | bytes 3670016 | tf_op jit(solution)/shard_map/all_to_all | solution.py:171
  157.4 0.1 copy.44
  157.5 1.3 slice_bitcast_fusion
  (7 shorter events, 0.1 us)
Async XLA Ops:
  2.1 1.2 copy-start
  3.3 0.8 copy-start.3
  4.0 0.8 copy-start.4
  4.8 0.7 copy-start.5
  5.4 0.7 copy-start.7
  7.5 18.8 %collective-permute-start = (f32[64,128]{1,0:T(8,128)S(1)}, f32[64,128]{1,0:T(8,128)S(1)}, u32[]{:S(2)}, u32[]{:S(2)}) collective-permute-start(f32[64,128]{1,0:T(8,128)S(1)} %get-tuple-element.16), channel_id=1, source_target_pairs={{0,1},{1,2},{2,3},{3,4},{4,5},{5,6},{6,7},{7,8},{8,9},{9,10},{10,1... | collective-permute-start | bytes 98312 | tf_op jit(solution)/shard_map/ppermute | solution.py:165
  24.3 13.9 %collective-permute-start.1 = (f32[64,128]{1,0:T(8,128)S(1)}, f32[64,128]{1,0:T(8,128)S(1)}, u32[]{:S(2)}, u32[]{:S(2)}) collective-permute-start(f32[64,128]{1,0:T(8,128)S(1)} %get-tuple-element.17), channel_id=1, source_target_pairs={{1,0},{2,1},{3,2},{4,3},{5,4},{6,5},{7,6},{8,7},{9,8},{10,9},{11,1... | collective-permute-start | bytes 98312 | tf_op jit(solution)/shard_map/ppermute | solution.py:166
  38.2 1.2 copy-start.2
  43.1 16.0 %copy-start.1 = (bf16[27,128,128]{2,1,0:T(8,128)(2,1)S(1)}, bf16[27,128,128]{2,1,0:T(8,128)(2,1)}, u32[]{:S(2)}) copy-start(bf16[27,128,128]{2,1,0:T(8,128)(2,1)} %w_two.3) | copy-start | bytes 2654212
  43.1 16.0 %copy-start.6 = (s32[32]{0:T(128)S(1)}, s32[32]{0:T(128)}, u32[]{:S(2)}) copy-start(s32[32]{0:T(128)} %param.11) | copy-start | bytes 388
  43.1 16.0 %copy-start.8 = (s32[32]{0:T(128)S(1)}, s32[32]{0:T(128)}, u32[]{:S(2)}) copy-start(s32[32]{0:T(128)} %param.12) | copy-start | bytes 388
  43.1 11.6 %collective-permute-start.2 = (f32[64,128]{1,0:T(8,128)S(1)}, f32[64,128]{1,0:T(8,128)S(1)}, u32[]{:S(2)}, u32[]{:S(2)}) collective-permute-start(f32[64,128]{1,0:T(8,128)S(1)} %get-tuple-element.20), channel_id=1, source_target_pairs={{0,1},{1,2},{2,3},{3,4},{4,5},{5,6},{6,7},{7,8},{8,9},{9,10},{10,1... | collective-permute-start | bytes 98312 | tf_op jit(solution)/shard_map/ppermute | solution.py:165
  45.2 13.9 %collective-permute-start.3 = (f32[64,128]{1,0:T(8,128)S(1)}, f32[64,128]{1,0:T(8,128)S(1)}, u32[]{:S(2)}, u32[]{:S(2)}) collective-permute-start(f32[64,128]{1,0:T(8,128)S(1)} %get-tuple-element.21), channel_id=1, source_target_pairs={{1,0},{2,1},{3,2},{4,3},{5,4},{6,5},{7,6},{8,7},{9,8},{10,9},{11,1... | collective-permute-start | bytes 98312 | tf_op jit(solution)/shard_map/ppermute | solution.py:166
  66.0 17.7 %all-to-all-start.1 = ((bf16[16,112,128]{2,1,0:T(8,128)(2,1)}), bf16[16,112,128]{2,1,0:T(8,128)(2,1)S(1)}, u32[]{:S(2)}, u32[]{:S(2)}) async-start(bf16[16,112,128]{2,1,0:T(8,128)(2,1)} %bitcast.3), calls=%async_computation.1 | async-start | bytes 917504 | tf_op jit(solution)/shard_map/all_to_all | solution.py:171
  83.8 12.5 %all-to-all-start.3 = ((bf16[16,112,128]{2,1,0:T(8,128)(2,1)}), bf16[16,112,128]{2,1,0:T(8,128)(2,1)S(1)}, u32[]{:S(2)}, u32[]{:S(2)}) async-start(bf16[16,112,128]{2,1,0:T(8,128)(2,1)} %bitcast.5), calls=%async_computation.3 | async-start | bytes 917504 | tf_op jit(solution)/shard_map/all_to_all | solution.py:171

commit v2 on v1

v2 whole, which is shorter than its diff:
```python
import math

import jax
import jax.numpy as jnp
from jax import lax
from jax.experimental import pallas as pl
from jax.experimental.pallas import tpu as pltpu
from jax.sharding import Mesh, PartitionSpec as P

AXES = ("dp", "y", "x", "zh", "core")
SLAB = ("y", "x", "zh", "core")
PLANE = ("y", "x")
DEPTH = ("dp", "zh")
BF = jnp.bfloat16
F32 = jnp.float32
WIDE = 256
NOWHERE = 255.0


def dot(a, b, contract=(1, 0), exact=False):
    return lax.dot_general(
        a,
        b,
        (((contract[0],), (contract[1],)), ((), ())),
        preferred_element_type=F32,
        precision=lax.Precision.HIGHEST if exact else None,
    )


def iota(shape, dim):
    return lax.broadcasted_iota(jnp.int32, shape, dim).astype(F32)


def live_rows(counts_ref, sites):
    return lax.broadcasted_iota(jnp.int32, (sites, 1), 0) < counts_ref[0]


def face_sites(row, sites):
    return (iota((sites, row.shape[1]), 0) == row).astype(F32)


def pick_matrix(columns, k):
    sites = columns.shape[0]
    return jnp.where(iota((sites, WIDE), 1) == columns[:, k : k + 1], 1.0, 0.0).astype(BF)


def gather_conv(extended, picks, w_ref):
    total = jnp.zeros((w_ref.shape[1], w_ref.shape[2]), F32)
    for k in range(w_ref.shape[0]):
        total = total + dot(dot(picks(k), extended).astype(BF), w_ref[k])
    return total


def extend(values, below, above):
    rim = below.shape[0]
    pad = jnp.zeros((WIDE - values.shape[0] - 2 * rim, values.shape[1]), F32)
    return jnp.concatenate([values, below, above, pad], 0).astype(BF)


def fetch(sources, targets, sems):
    copies = [
        pltpu.make_async_copy(s, t, sems.at[i])
        for i, (s, t) in enumerate(zip(sources, targets))
    ]
    for copy in copies:
        copy.start()
    return copies


def pack_kernel(
    counts, feat_h, cot_h, map_h, low_h, high_h, up, down, masked_ref, faces,
    feat, cot, table, low_s, high_s, sems,
):
    for copy in fetch(
        (feat_h, cot_h, map_h, low_h, high_h), (feat, cot, table, low_s, high_s), sems
    ):
        copy.wait()
    sites, rim = feat.shape[0], low_s.shape[1]
    live = live_rows(counts, sites)
    masked = jnp.where(live, feat[...].astype(F32), 0.0).astype(BF)
    masked_ref[...] = masked
    grad = jnp.where(live, cot[...].astype(F32), 0.0).astype(BF)
    offsets = table.shape[0]
    names = jnp.concatenate(
        [table[...].astype(F32), jnp.full((rim - offsets, sites), NOWHERE, F32)], 0
    ).astype(BF)
    faces[0:1] = low_s[...].astype(F32)
    faces[1:2] = high_s[...].astype(F32)
    for out, row in ((up, faces[1:2]), (down, faces[0:1])):
        out[:sites] = grad
        picks = face_sites(row, sites).T.astype(BF)
        out[sites : sites + rim] = dot(picks, masked).astype(BF)
        out[sites + rim :] = names


def sites_of(names, first, row):
    found = jnp.full(names.shape, NOWHERE, F32)
    for j in range(row.shape[1]):
        found = jnp.where(names == first + j, row[:, j : j + 1], found)
    return found


def main_kernel(
    counts, masked, own, faces, below, above, w_one_h, w_two_h,
    up, down, own_grad, hidden_ref, mine, theirs,
    w_one, w_two, picks, held, kept, sems,
):
    copies = fetch((w_one_h, w_two_h), (w_one, w_two), sems)
    offsets, channels = w_one.shape[0], w_one.shape[1]
    sites, rim = masked.shape[0], faces.shape[1]
    live = live_rows(counts, sites)
    low_row, high_row = faces[0:1], faces[1:2]
    names = own[sites + rim :].astype(F32)
    columns = names.T
    for k in range(offsets):
        picks[k] = pick_matrix(columns, k)
    rims = slice(sites, sites + rim)
    extended = extend(
        masked[...].astype(F32), below[rims].astype(F32), above[rims].astype(F32)
    )

    above_names = sites_of(above[sites + rim :].astype(F32), sites, high_row)
    below_names = sites_of(below[sites + rim :].astype(F32), sites + rim, low_row)
    names = jnp.concatenate([names, above_names, below_names], 1)
    grads = jnp.concatenate([own[:sites], above[:sites], below[:sites]], 0)
    rows = iota((sites, 3 * sites), 0)
    for k in range(offsets):
        hits = jnp.where(rows == names[k : k + 1], 1.0, 0.0).astype(BF)
        held[k] = dot(hits, grads).astype(BF)
    copies[0].wait()
    x = gather_conv(extended, lambda k: picks[k], w_one)
    copies[1].wait()
    hidden_grad = jnp.zeros((sites, channels), F32)
    for k in range(offsets):
        hidden_grad = hidden_grad + dot(held[k], w_two[k], (1, 1))

    slope = math.sqrt(2.0 / math.pi)
    t = jnp.tanh(slope * (x + 0.044715 * (x * x * x)))
    cdf = 0.5 * (1.0 + t)
    hidden = jnp.where(live, x * cdf, 0.0)
    hidden_ref[...] = hidden.astype(BF)
    bend = cdf + 0.5 * x * (1.0 - t * t) * (slope * (1.0 + 3 * 0.044715 * (x * x)))
    pre_grad = jnp.where(live, bend * hidden_grad, 0.0)

    turned = pre_grad.T.astype(BF)
    extended_t = extended.astype(F32).T.astype(BF)
    hidden_t = hidden.T.astype(BF)
    total = jnp.zeros((channels, WIDE), F32)
    first_is_mine = lax.axis_index("core") == 0
    for k in range(offsets):
        kept[k] = dot(turned, picks[k]).astype(BF)
        total = total + dot(w_one[k], kept[k])
        first = dot(extended_t, kept[k], (1, 1))
        second = dot(hidden_t, held[k])
        mine[k] = jnp.where(first_is_mine, first, second).astype(BF)
        theirs[k] = jnp.where(first_is_mine, second, first).astype(BF)
    mine[offsets] = jnp.zeros((channels, channels), BF)
    theirs[offsets] = jnp.zeros((channels, channels), BF)
    ext_grad = total.T
    own_grad[...] = ext_grad[:sites]
    low, high = face_sites(low_row, sites), face_sites(high_row, sites)
    up[:rim] = dot(high.T.astype(BF), hidden.astype(BF))
    up[rim:] = ext_grad[sites + rim : sites + 2 * rim]
    down[:rim] = dot(low.T.astype(BF), hidden.astype(BF))
    down[rim:] = ext_grad[sites : sites + rim]


def last_kernel(
    counts, hidden, own, faces, below, above, own_grad, w_two_h,
    response, input_grad, w_two, sems,
):
    copies = fetch((w_two_h,), (w_two,), sems)
    sites, rim = hidden.shape[0], faces.shape[1]
    live = live_rows(counts, sites)
    low, high = face_sites(faces[0:1], sites), face_sites(faces[1:2], sites)
    grad = own_grad[...] + dot(high, above[rim:], exact=True)
    grad = grad + dot(low, below[rim:], exact=True)
    input_grad[...] = jnp.where(live, grad, 0.0).astype(BF)
    columns = own[sites + rim :].astype(F32).T
    extended = extend(hidden[...].astype(F32), below[:rim], above[:rim])
    copies[0].wait()
    second_pre = gather_conv(extended, lambda k: pick_matrix(columns, k), w_two)
    response[...] = jnp.where(live, second_pre, 0.0).astype(BF)


def call(kernel, places, outs, scratch, copies, us):
    memory = {"s": pltpu.SMEM, "v": pltpu.VMEM, "h": pltpu.HBM}
    return pl.pallas_call(
        kernel,
        out_shape=[jax.ShapeDtypeStruct(s, d) for s, d in outs],
        in_specs=[pl.BlockSpec(memory_space=memory[p]) for p in places],
        out_specs=[pl.BlockSpec(memory_space=pltpu.VMEM)] * len(outs),
        scratch_shapes=[pltpu.VMEM(s, d) for s, d in scratch]
        + [pltpu.SemaphoreType.DMA((copies,))],
        compiler_params=pltpu.CompilerParams(vmem_limit_bytes=40 * 2**20),
        cost_estimate=pl.CostEstimate(
            flops=0, bytes_accessed=int(us * 3e6), transcendentals=0
        ),
    )


def exchange(up, down):
    last = lax.axis_size(SLAB) - 1
    below = lax.ppermute(up, SLAB, [(i, i + 1) for i in range(last)])
    above = lax.ppermute(down, SLAB, [(i + 1, i) for i in range(last)])
    return below, above


def swap(block, axis):
    return lax.all_to_all(block, axis, 0, 0, tiled=True)


def other_core(block):
    return lax.ppermute(block, "core", [(0, 1), (1, 0)])


def on_device(feat, counts, nb, low, high, w_one, w_two, cot):
    sites, channels = feat.shape
    offsets, rim = nb.shape[1], low.shape[0]
    scaling = 1.0 / math.sqrt(lax.axis_size(AXES) * sites)
    flat = ((sites, channels), BF)
    field = ((sites, channels), F32)
    letter = ((sites + 2 * rim, channels), BF)
    ends = ((2 * rim, channels), F32)
    weight = ((offsets, channels, channels), BF)
    sums = ((offsets + 1, channels, channels), BF)
    row = ((1, rim), jnp.int32)
    up, down, masked, faces = call(
        pack_kernel, "shhhhh", (letter, letter, flat, ((2, rim), F32)),
        (flat, flat, ((offsets, sites), jnp.int32), row, row), 5, 1,
    )(counts, feat, cot, nb.T, low.reshape(1, rim), high.reshape(1, rim))
    below, above = exchange(up, down)
    picks = ((offsets, sites, WIDE), BF)
    kept = ((offsets, channels, WIDE), BF)
    up_two, down_two, own_grad, hidden, mine, theirs = call(
        main_kernel, "svvvvvhh", (ends, ends, field, flat, sums, sums),
        (weight, weight, picks, weight, kept), 2, 5,
    )(counts, masked, up, faces, below, above, w_one, w_two)

    depth, plane = lax.axis_size(DEPTH), lax.axis_size(PLANE)
    share = (mine.astype(F32) + other_core(theirs).astype(F32)).astype(BF)
    share, up_two, down_two = lax.optimization_barrier((share, up_two, down_two))
    parts = swap(share.reshape(plane, -1, channels), PLANE)
    below, above = exchange(up_two, down_two)
    parts = jnp.sum(parts.astype(F32), 0).reshape(depth, -1, channels)
    total = jnp.sum(swap(parts, DEPTH), 0) * scaling
    response, input_grad = call(
        last_kernel, "svvvvvvh", (flat, flat), (weight,), 1, 3
    )(counts, hidden, up, faces, below, above, own_grad, w_two)

    total = total.astype(BF)
    column = swap(jnp.broadcast_to(total, (depth, *total.shape)), DEPTH)
    column = column.reshape(-1, channels)
    whole = swap(jnp.broadcast_to(column, (plane, *column.shape)), PLANE)
    whole = whole.reshape(offsets + 1, channels, channels)
    other = other_core(whole)
    first_is_mine = lax.axis_index("core") == 0
    first = jnp.where(first_is_mine, whole, other)[:offsets]
    second = jnp.where(first_is_mine, other, whole)[:offsets]
    return response, input_grad, first, second


def solution(mesh):
    groups, slabs = mesh.devices.shape
    side = {64: 4, 16: 2, 4: 1}[slabs]
    fine = Mesh(mesh.devices.reshape(groups, side, side, 2, 2), AXES)
    rows, row = P(AXES, None), P(AXES)
    return jax.shard_map(
        on_device,
        mesh=fine,
        in_specs=(rows, row, rows, row, row, P(), P(), rows),
        out_specs=(rows, rows, P(), P()),
        check_vma=False,
    )
```

time: 160 us -> 156 us (0.975)
  waiting for transfers between devices: 34.1 us -> 15.6 us
  blocking collectives: 69.4 us -> 85.7 us
  Pallas kernels: 7.83 us -> 13.6 us
  starting transfers between devices: 34.6 us -> 30.8 us
  local copies, waits for them, and re-layouts: 8.01 us -> 6.05 us
  other arithmetic: 3.49 us -> 1.86 us
    all_to_all x2 -> x0, waiting for transfers between devices: 17.7 us -> none  [swap(): return lax.all_to_all(block, axis, 0, 0, tiled=True)]
    all_to_all x6 -> x4, blocking collectives: 69.4 us -> 85.7 us  [swap(): return lax.all_to_all(block, axis, 0, 0, tiled=True)]
    all_to_all x2 -> x0, starting transfers between devices: 11.4 us -> none  [swap(): return lax.all_to_all(block, axis, 0, 0, tiled=True)]
    ppermute x4 -> x6, starting transfers between devices: 23.2 us -> 30.8 us  [the longest x2 12.4 us: exchange(): below = lax.ppermute(up, SLAB, [(i, i + 1) for i in range(last)])]
    pallas_call x3, Pallas kernels: 7.83 us -> 13.6 us  [the longest x1 10.3 us: on_device(): call(main_kernel, 'svvvvvhh', (ends, ends, field, flat, sums, sums), (wei...]
    reduce_sum x5 -> x2, other arithmetic: 3.46 us -> 0.15 us  [the longest x1 0.12 us: on_device(): parts = jnp.sum(parts.astype(F32), 0).reshape(depth, -1, channels)]
    ppermute x4 -> x6, waiting for transfers between devices: 16.4 us -> 15.6 us  [the longest x2 12.1 us: exchange(): above = lax.ppermute(down, SLAB, [(i + 1, i) for i in range(last)])]
    unnamed x19 -> x16, local copies, waits for them, and re-layouts: 5.99 us -> 5.87 us
  transfers between devices with their start and end apart: 6 -> 6, of which waited for: 4 -> 3; matrix products, arithmetic and copies ran while one was open for 2% -> 0% of each run, Pallas kernels for 0% -> 2%
where the time goes in v2:
time: 156 us; the launch traced here: 155 us
  blocking collectives  85.7 us (55%)
  starting transfers between devices  30.8 us (20%)
  waiting for transfers between devices  15.6 us (10%)
  Pallas kernels  13.6 us (9%)
  local copies, waits for them, and re-layouts  6.05 us (4%)
  other arithmetic  1.86 us (1%)
    all_to_all x4, blocking collectives, swap(): return lax.all_to_all(block, axis, 0, 0, tiled=True)  85.7 us
    ppermute x2, starting transfers between devices, exchange(): below = lax.ppermute(up, SLAB, [(i, i + 1) for i in range(last)])  12.4 us
    ppermute x2, waiting for transfers between devices, exchange(): above = lax.ppermute(down, SLAB, [(i + 1, i) for i in range(last)])  12.1 us
    ppermute x2, starting transfers between devices, exchange(): above = lax.ppermute(down, SLAB, [(i + 1, i) for i in range(last)])  10.7 us
    pallas_call x1, Pallas kernels, on_device(): call(main_kernel, 'svvvvvhh', (ends, ends, field, flat, sums, sums), (wei...  10.3 us
    ppermute x2, starting transfers between devices, other_core(): return lax.ppermute(block, 'core', [(0, 1), (1, 0)])  7.67 us
    unnamed x16, local copies, waits for them, and re-layouts  5.87 us
  transfers between devices with their start and end apart: 6, of which 3 were waited for; matrix products, arithmetic and copies ran while one was open for 0% of the time, Pallas kernels for 2%

profile of v2, /device:TPU:1, one launch (start us, length us, event | category | flops | bytes accessed | tf_op | source)
XLA Modules:
  0.0 155.0 jit_solution(18400567406143057519)
XLA Ops:
  1.3 0.0 copy-start.3
  1.3 0.7 copy-done.3
  2.0 0.0 copy-start.4
  2.0 0.8 copy-done.4
  2.8 0.0 copy-start.5
  2.8 0.7 copy-done.5
  3.5 0.0 copy-start.6
  3.5 0.7 copy-done.6
  4.2 0.0 copy-start.7
  4.2 0.7 copy-done.7
  4.8 0.3 shard_map.111
  5.2 8.8 %collective-permute-start.1 = (bf16[192,128]{1,0:T(8,128)(2,1)S(1)}, bf16[192,128]{1,0:T(8,128)(2,1)S(1)}, u32[]{:S(2)}, u32[]{:S(2)}) collective-permute-start(bf16[192,128]{1,0:T(8,128)(2,1)S(1)} %get-tuple-element.22), channel_id=1, source_target_pairs={{1,0},{2,1},{3,2},{4,3},{5,4},{6,5},{7,6},{8,7},{9,8},{10,9},{11,1... | collective-permute-start | bytes 147464 | tf_op jit(solution)/shard_map/ppermute | solution.py:205
  13.9 10.0 %collective-permute-start = (bf16[192,128]{1,0:T(8,128)(2,1)S(1)}, bf16[192,128]{1,0:T(8,128)(2,1)S(1)}, u32[]{:S(2)}, u32[]{:S(2)}) collective-permute-start(bf16[192,128]{1,0:T(8,128)(2,1)S(1)} %get-tuple-element.20.own), channel_id=1, source_target_pairs={{0,1},{1,2},{2,3},{3,4},{4,5},{5,6},{6,7},{7,8},{8,9},{9,10},{10,1... | collective-permute-start | bytes 147464 | tf_op jit(solution)/shard_map/ppermute | solution.py:204
  23.9 0.0 collective-permute-done.1.above
  23.9 1.1 collective-permute-done.below
  25.1 0.0 copy-start
  25.1 1.2 copy-done
  26.2 0.0 copy-start.2
  26.2 1.2 copy-done.2
  27.4 10.3 %shard_map.112 = (f32[64,128]{1,0:T(8,128)S(1)}, f32[64,128]{1,0:T(8,128)S(1)}, f32[128,128]{1,0:T(8,128)S(1)}, bf16[128,128]{1,0:T(8,128)(2,1)S(1)}, bf16[28,12...) custom-call(s32[1]{0:T(128)S(6)} %copy.12.counts, bf16[128,128]{1,0:T(8,128)(2,1)S(1)} %get-tuple-element.19.masked, ...), custom_call_target="tpu_custom_call" | custom-call | bytes 15000000 | tf_op jit(solution)/shard_map/pallas_call | solution.py:235
  37.7 1.9 %collective-permute-start.2 = (bf16[28,128,128]{2,1,0:T(8,128)(2,1)S(1)}, bf16[28,128,128]{2,1,0:T(8,128)(2,1)S(1)}, u32[]{:S(2)}, u32[]{:S(2)}) collective-permute-start(bf16[28,128,128]{2,1,0:T(8,128)(2,1)S(1)} %get-tuple-element.25), channel_id=1, source_target_pairs={{0,1},{1,0},{2,3},{3,2},{4,5},{5,4},{6,7},{7,6},{8,9},{9,8},{10,11... | collective-permute-start | bytes 2752520 | tf_op jit(solution)/shard_map/ppermute | solution.py:214
  39.6 2.4 %collective-permute-done.2 = bf16[28,128,128]{2,1,0:T(8,128)(2,1)S(1)} collective-permute-done((bf16[28,128,128]{2,1,0:T(8,128)(2,1)S(1)}, bf16[28,128,128]{2,1,0:T(8,128)(2,1)S(1)}, u32[]{:S(2)}, u32[]{:S(2)}) %collective-permute-start.2) | collective-permute-done | bytes 917536 | tf_op jit(solution)/shard_map/ppermute | solution.py:214
  42.1 0.4 add_convert_fusion
  42.5 35.0 %all_to_all.20 = bf16[16,224,128]{2,1,0:T(8,128)(2,1)S(1)} all-to-all(bf16[16,224,128]{2,1,0:T(8,128)(2,1)S(1)} %bitcast.8), channel_id=1, replica_groups=mesh['dp'=8,'y'=4,'x'=4,'zh'=2,'core'=2] {'y','x'}, dimensions={0} | all-to-all | bytes 1835008 | tf_op jit(solution)/shard_map/all_to_all | solution.py:210
  77.4 0.1 convert_reduce_fusion
  77.6 17.6 %all_to_all.21 = f32[16,14,128]{2,1,0:T(8,128)S(1)} all-to-all(f32[16,14,128]{2,1,0:T(8,128)S(1)} %reshape.29), channel_id=1, replica_groups=mesh['dp'=8,'y'=4,'x'=4,'zh'=2,'core'=2] {'dp','zh'}, dimensions={0} | all-to-all | bytes 229376 | tf_op jit(solution)/shard_map/all_to_all | solution.py:210
  95.3 16.6 %all_to_all.22 = bf16[16,14,128]{2,1,0:T(8,128)(2,1)S(1)} all-to-all(bf16[16,14,128]{2,1,0:T(8,128)(2,1)S(1)} %broadcast_in_dim.6), channel_id=1, replica_groups=mesh['dp'=8,'y'=4,'x'=4,'zh'=2,'core'=2] {'dp','zh'}, dimensions={0} | all-to-all | bytes 114688 | tf_op jit(solution)/shard_map/all_to_all | solution.py:210
  111.9 0.1 broadcast_in_dim.7
  112.1 0.0 copy-start.1
  112.1 16.4 %all_to_all.23 = bf16[16,224,128]{2,1,0:T(8,128)(2,1)S(1)} all-to-all(bf16[16,224,128]{2,1,0:T(8,128)(2,1)S(1)} %broadcast_in_dim.7), channel_id=1, replica_groups=mesh['dp'=8,'y'=4,'x'=4,'zh'=2,'core'=2] {'y','x'}, dimensions={0} | all-to-all | bytes 1835008 | tf_op jit(solution)/shard_map/all_to_all | solution.py:210
  128.5 5.7 %collective-permute-start.5 = (bf16[28,128,128]{2,1,0:T(8,128)(2,1)S(1)}, bf16[28,128,128]{2,1,0:T(8,128)(2,1)S(1)}, u32[]{:S(2)}, u32[]{:S(2)}) collective-permute-start(bf16[28,128,128]{2,1,0:T(8,128)(2,1)S(1)} %bitcast.9), channel_id=1, source_target_pairs={{0,1},{1,0},{2,3},{3,2},{4,5},{5,4},{6,7},{7,6},{8,9},{9,8},{10,11... | collective-permute-start | bytes 2752520 | tf_op jit(solution)/shard_map/ppermute | solution.py:214
  134.3 2.4 %collective-permute-start.3 = (f32[64,128]{1,0:T(8,128)S(1)}, f32[64,128]{1,0:T(8,128)S(1)}, u32[]{:S(2)}, u32[]{:S(2)}) collective-permute-start(f32[64,128]{1,0:T(8,128)S(1)} %get-tuple-element.28), channel_id=1, source_target_pairs={{0,1},{1,2},{2,3},{3,4},{4,5},{5,6},{6,7},{7,8},{8,9},{9,10},{10,1... | collective-permute-start | bytes 98312 | tf_op jit(solution)/shard_map/ppermute | solution.py:204
  136.7 1.9 %collective-permute-start.4 = (f32[64,128]{1,0:T(8,128)S(1)}, f32[64,128]{1,0:T(8,128)S(1)}, u32[]{:S(2)}, u32[]{:S(2)}) collective-permute-start(f32[64,128]{1,0:T(8,128)S(1)} %get-tuple-element.29), channel_id=1, source_target_pairs={{1,0},{2,1},{3,2},{4,3},{5,4},{6,5},{7,6},{8,7},{9,8},{10,9},{11,1... | collective-permute-start | bytes 98312 | tf_op jit(solution)/shard_map/ppermute | solution.py:205
  138.6 0.0 collective-permute-done.3.below
  138.6 12.1 %collective-permute-done.4.above = f32[64,128]{1,0:T(8,128)S(1)} collective-permute-done((f32[64,128]{1,0:T(8,128)S(1)}, f32[64,128]{1,0:T(8,128)S(1)}, u32[]{:S(2)}, u32[]{:S(2)}) %collective-permute-start.4) | collective-permute-done | bytes 32800 | tf_op jit(solution)/shard_map/ppermute | solution.py:205
  150.7 0.0 copy-done.1
  150.7 2.9 %shard_map.113 = (bf16[128,128]{1,0:T(8,128)(2,1)}, bf16[128,128]{1,0:T(8,128)(2,1)}) custom-call(s32[1]{0:T(128)S(6)} %copy.12.counts, bf16[128,128]{1,0:T(8,128)(2,1)S(1)} %get-tuple-element.23.hidden, bf16[192,128]{1,0:T(8,128)(2,1)S(1)} %get-tuple-element.20.own, f32[2,32]{1,0:T(2,128)S(1)} %get-tuple-element.21.faces, ...), custom_call_target="tpu_custom_call" | custom-call | bytes 9000000 | tf_op jit(solution)/shard_map/pallas_call | solution.py:247
  153.6 0.0 collective-permute-done.5
  153.7 1.3 broadcast_select_fusion
  (5 shorter events, 0.1 us)
Async XLA Ops:
  1.3 0.8 copy-start.3
  2.0 0.8 copy-start.4
  2.8 0.7 copy-start.5
  3.5 0.7 copy-start.6
  4.2 0.7 copy-start.7
  5.2 18.8 %collective-permute-start.1 = (bf16[192,128]{1,0:T(8,128)(2,1)S(1)}, bf16[192,128]{1,0:T(8,128)(2,1)S(1)}, u32[]{:S(2)}, u32[]{:S(2)}) collective-permute-start(bf16[192,128]{1,0:T(8,128)(2,1)S(1)} %get-tuple-element.22), channel_id=1, source_target_pairs={{1,0},{2,1},{3,2},{4,3},{5,4},{6,5},{7,6},{8,7},{9,8},{10,9},{11,1... | collective-permute-start | bytes 147464 | tf_op jit(solution)/shard_map/ppermute | solution.py:205
  13.9 11.1 %collective-permute-start = (bf16[192,128]{1,0:T(8,128)(2,1)S(1)}, bf16[192,128]{1,0:T(8,128)(2,1)S(1)}, u32[]{:S(2)}, u32[]{:S(2)}) collective-permute-start(bf16[192,128]{1,0:T(8,128)(2,1)S(1)} %get-tuple-element.20.own), channel_id=1, source_target_pairs={{0,1},{1,2},{2,3},{3,4},{4,5},{5,6},{6,7},{7,8},{8,9},{9,10},{10,1... | collective-permute-start | bytes 147464 | tf_op jit(solution)/shard_map/ppermute | solution.py:204
  25.1 1.2 copy-start
  26.2 1.2 copy-start.2
  37.7 4.4 %collective-permute-start.2 = (bf16[28,128,128]{2,1,0:T(8,128)(2,1)S(1)}, bf16[28,128,128]{2,1,0:T(8,128)(2,1)S(1)}, u32[]{:S(2)}, u32[]{:S(2)}) collective-permute-start(bf16[28,128,128]{2,1,0:T(8,128)(2,1)S(1)} %get-tuple-element.25), channel_id=1, source_target_pairs={{0,1},{1,0},{2,3},{3,2},{4,5},{5,4},{6,7},{7,6},{8,9},{9,8},{10,11... | collective-permute-start | bytes 2752520 | tf_op jit(solution)/shard_map/ppermute | solution.py:214
  112.1 38.6 %copy-start.1 = (bf16[27,128,128]{2,1,0:T(8,128)(2,1)S(1)}, bf16[27,128,128]{2,1,0:T(8,128)(2,1)}, u32[]{:S(2)}) copy-start(bf16[27,128,128]{2,1,0:T(8,128)(2,1)} %w_two_h.3) | copy-start | bytes 2654212
  128.5 25.1 %collective-permute-start.5 = (bf16[28,128,128]{2,1,0:T(8,128)(2,1)S(1)}, bf16[28,128,128]{2,1,0:T(8,128)(2,1)S(1)}, u32[]{:S(2)}, u32[]{:S(2)}) collective-permute-start(bf16[28,128,128]{2,1,0:T(8,128)(2,1)S(1)} %bitcast.9), channel_id=1, source_target_pairs={{0,1},{1,0},{2,3},{3,2},{4,5},{5,4},{6,7},{7,6},{8,9},{9,8},{10,11... | collective-permute-start | bytes 2752520 | tf_op jit(solution)/shard_map/ppermute | solution.py:214
  134.3 4.4 %collective-permute-start.3 = (f32[64,128]{1,0:T(8,128)S(1)}, f32[64,128]{1,0:T(8,128)S(1)}, u32[]{:S(2)}, u32[]{:S(2)}) collective-permute-start(f32[64,128]{1,0:T(8,128)S(1)} %get-tuple-element.28), channel_id=1, source_target_pairs={{0,1},{1,2},{2,3},{3,4},{4,5},{5,6},{6,7},{7,8},{8,9},{9,10},{10,1... | collective-permute-start | bytes 98312 | tf_op jit(solution)/shard_map/ppermute | solution.py:204
  136.7 14.0 %collective-permute-start.4 = (f32[64,128]{1,0:T(8,128)S(1)}, f32[64,128]{1,0:T(8,128)S(1)}, u32[]{:S(2)}, u32[]{:S(2)}) collective-permute-start(f32[64,128]{1,0:T(8,128)S(1)} %get-tuple-element.29), channel_id=1, source_target_pairs={{1,0},{2,1},{3,2},{4,3},{5,4},{6,5},{7,6},{8,7},{9,8},{10,9},{11,1... | collective-permute-start | bytes 98312 | tf_op jit(solution)/shard_map/ppermute | solution.py:205

commit v3 on v2

v3 whole, which is shorter than its diff:
```python
import math

import jax
import jax.numpy as jnp
from jax import lax
from jax.experimental import pallas as pl
from jax.experimental.pallas import tpu as pltpu
from jax.sharding import Mesh, PartitionSpec as P

AXES = ("dp", "y", "x", "zh", "core")
SLAB = ("y", "x", "zh", "core")
PLANE = ("y", "x")
DEPTH = ("dp", "zh")
BF = jnp.bfloat16
F32 = jnp.float32
WIDE = 256
NOWHERE = 255.0


def dot(a, b, contract=(1, 0), exact=False):
    return lax.dot_general(
        a,
        b,
        (((contract[0],), (contract[1],)), ((), ())),
        preferred_element_type=F32,
        precision=lax.Precision.HIGHEST if exact else None,
    )


def iota(shape, dim):
    return lax.broadcasted_iota(jnp.int32, shape, dim).astype(F32)


def live_rows(counts_ref, sites):
    return lax.broadcasted_iota(jnp.int32, (sites, 1), 0) < counts_ref[0]


def face_sites(row, sites):
    return (iota((sites, row.shape[1]), 0) == row).astype(F32)


def pick_matrix(columns, k):
    sites = columns.shape[0]
    return jnp.where(iota((sites, WIDE), 1) == columns[:, k : k + 1], 1.0, 0.0).astype(BF)


def gather_conv(extended, picks, w_ref):
    total = jnp.zeros((w_ref.shape[1], w_ref.shape[2]), F32)
    for k in range(w_ref.shape[0]):
        total = total + dot(dot(picks(k), extended).astype(BF), w_ref[k])
    return total


def extend(values, below, above):
    rim = below.shape[0]
    pad = jnp.zeros((WIDE - values.shape[0] - 2 * rim, values.shape[1]), F32)
    return jnp.concatenate([values, below, above, pad], 0).astype(BF)


def fetch(sources, targets, sems):
    copies = [
        pltpu.make_async_copy(s, t, sems.at[i])
        for i, (s, t) in enumerate(zip(sources, targets))
    ]
    for copy in copies:
        copy.start()
    return copies


def near_is_above():
    return lax.axis_index("core") == 0


def near_and_far(faces):
    above = near_is_above()
    low, high = faces[0:1], faces[1:2]
    return jnp.where(above, high, low), jnp.where(above, low, high)


def pack_kernel(
    counts, feat_h, cot_h, map_h, low_h, high_h, near, far, faces,
    feat, cot, table, low_s, high_s, sems,
):
    for copy in fetch(
        (feat_h, cot_h, map_h, low_h, high_h), (feat, cot, table, low_s, high_s), sems
    ):
        copy.wait()
    sites, rim = feat.shape[0], low_s.shape[1]
    live = live_rows(counts, sites)
    masked = jnp.where(live, feat[...].astype(F32), 0.0).astype(BF)
    grad = jnp.where(live, cot[...].astype(F32), 0.0).astype(BF)
    offsets = table.shape[0]
    names = jnp.concatenate(
        [table[...].astype(F32), jnp.full((rim - offsets, sites), NOWHERE, F32)], 0
    ).astype(BF)
    faces[0:1] = low_s[...].astype(F32)
    faces[1:2] = high_s[...].astype(F32)
    for out, row in zip((near, far), near_and_far(faces)):
        out[:sites] = grad
        picks = face_sites(row, sites).T.astype(BF)
        out[sites : sites + rim] = dot(picks, masked).astype(BF)
        out[sites + rim :] = names


def stage_kernel(
    counts, feat, own, faces_in, w_one_in, w_two_in,
    masked, grad, names, faces, picks, w_one, w_two, sems,
):
    sites, rim = feat.shape[0], faces.shape[1]
    live = live_rows(counts, sites)
    masked[...] = jnp.where(live, feat[...].astype(F32), 0.0).astype(BF)
    grad[...] = own[:sites]
    names[...] = own[sites + rim :].astype(F32)
    faces[...] = faces_in[...]
    columns = names[...].T
    for k in range(picks.shape[0]):
        picks[k] = pick_matrix(columns, k)
        w_one[k] = w_one_in[k]
        w_two[k] = w_two_in[k]


def sites_of(names, first, row):
    found = jnp.full(names.shape, NOWHERE, F32)
    for j in range(row.shape[1]):
        found = jnp.where(names == first + j, row[:, j : j + 1], found)
    return found


def lanes(k, width, n=1):
    return slice(k * width, (k + n) * width)


def back(held, w_ref, rows):
    offsets, channels = w_ref.shape[0], w_ref.shape[1]
    total = jnp.zeros((rows, channels), F32)
    for k in range(0, offsets, 2):
        n = min(2, offsets - k)
        weight = jnp.concatenate([w_ref[k + j] for j in range(n)], 1)
        total = total + dot(held[:, lanes(k, w_ref.shape[2], n)], weight, (1, 1))
    return total


def main_kernel(
    counts, masked, own_grads, own_names, faces, picks, w_one, w_two, near, far,
    near_out, far_out, own_grad, hidden_ref, mine, theirs,
    picked, held, kept, sems,
):
    offsets, channels = w_one.shape[0], w_one.shape[1]
    sites, rim = masked.shape[0], faces.shape[1]
    live = live_rows(counts, sites)
    above = near_is_above()
    near_row, far_row = near_and_far(faces)
    rims = slice(sites, sites + rim)
    near_rim, far_rim = near[rims].astype(F32), far[rims].astype(F32)
    extended = extend(
        masked[...].astype(F32),
        jnp.where(above, far_rim, near_rim),
        jnp.where(above, near_rim, far_rim),
    )
    for k in range(offsets):
        picked[:, lanes(k, channels)] = dot(picks[k], extended).astype(BF)
    x = dot(picked[...], w_one[...].reshape(offsets * channels, channels))

    up_first, down_first = float(sites), float(sites + rim)
    near_first = jnp.where(above, up_first, down_first)
    far_first = jnp.where(above, down_first, up_first)
    names = jnp.concatenate(
        [
            own_names[...],
            sites_of(near[sites + rim :].astype(F32), near_first, near_row),
            sites_of(far[sites + rim :].astype(F32), far_first, far_row),
        ],
        1,
    )
    grads = jnp.concatenate([own_grads[...], near[:sites], far[:sites]], 0)
    rows = iota((sites, 3 * sites), 0)
    for k in range(offsets):
        hits = jnp.where(rows == names[k : k + 1], 1.0, 0.0).astype(BF)
        held[:, lanes(k, channels)] = dot(hits, grads).astype(BF)
    hidden_grad = back(held, w_two, sites)

    slope = math.sqrt(2.0 / math.pi)
    t = jnp.tanh(slope * (x + 0.044715 * (x * x * x)))
    cdf = 0.5 * (1.0 + t)
    hidden = jnp.where(live, x * cdf, 0.0)
    hidden_ref[...] = hidden.astype(BF)
    bend = cdf + 0.5 * x * (1.0 - t * t) * (slope * (1.0 + 3 * 0.044715 * (x * x)))
    pre_grad = jnp.where(live, bend * hidden_grad, 0.0).astype(BF)

    extended_t = extended.astype(F32).T.astype(BF)
    hidden_t = hidden.T.astype(BF)
    rows = iota((WIDE, sites), 0)
    for k in range(offsets):
        hits = jnp.where(rows == names[k : k + 1, :sites], 1.0, 0.0).astype(BF)
        kept[:, lanes(k, channels)] = dot(hits, pre_grad).astype(BF)
    ext_grad = back(kept, w_one, WIDE)
    own_grad[...] = ext_grad[:sites]
    to_above, to_below = ext_grad[sites + rim : sites + 2 * rim], ext_grad[rims]
    near_pick = face_sites(near_row, sites).T.astype(BF)
    far_pick = face_sites(far_row, sites).T.astype(BF)
    near_out[:rim] = dot(near_pick, hidden.astype(BF))
    near_out[rim:] = jnp.where(above, to_above, to_below)
    far_out[:rim] = dot(far_pick, hidden.astype(BF))
    far_out[rim:] = jnp.where(above, to_below, to_above)
    first_is_mine = lax.axis_index("core") == 0
    for k in range(0, offsets, 2):
        n = min(2, offsets - k)
        first = dot(extended_t, kept[:, lanes(k, channels, n)])
        second = dot(hidden_t, held[:, lanes(k, channels, n)])
        for j in range(n):
            a, b = first[:, lanes(j, channels)], second[:, lanes(j, channels)]
            mine[k + j] = jnp.where(first_is_mine, a, b).astype(BF)
            theirs[k + j] = jnp.where(first_is_mine, b, a).astype(BF)
    mine[offsets] = jnp.zeros((channels, channels), BF)
    theirs[offsets] = jnp.zeros((channels, channels), BF)


def last_kernel(
    counts, hidden, faces, near, far, own_grad, picks, w_two,
    response, input_grad, picked, sems,
):
    sites, rim = hidden.shape[0], faces.shape[1]
    offsets, channels = w_two.shape[0], w_two.shape[1]
    live = live_rows(counts, sites)
    above = near_is_above()
    near_row, far_row = near_and_far(faces)
    grad = own_grad[...] + dot(face_sites(near_row, sites), near[rim:], exact=True)
    grad = grad + dot(face_sites(far_row, sites), far[rim:], exact=True)
    input_grad[...] = jnp.where(live, grad, 0.0).astype(BF)
    extended = extend(
        hidden[...].astype(F32),
        jnp.where(above, far[:rim], near[:rim]),
        jnp.where(above, near[:rim], far[:rim]),
    )
    for k in range(offsets):
        picked[:, lanes(k, channels)] = dot(picks[k], extended).astype(BF)
    second_pre = dot(picked[...], w_two[...].reshape(offsets * channels, channels))
    response[...] = jnp.where(live, second_pre, 0.0).astype(BF)


def call(kernel, places, outs, scratch, copies, us, limit=32):
    memory = {"s": pltpu.SMEM, "v": pltpu.VMEM, "h": pltpu.HBM}
    return pl.pallas_call(
        kernel,
        out_shape=[jax.ShapeDtypeStruct(s, d) for s, d in outs],
        in_specs=[pl.BlockSpec(memory_space=memory[p]) for p in places],
        out_specs=[pl.BlockSpec(memory_space=pltpu.VMEM)] * len(outs),
        scratch_shapes=[pltpu.VMEM(s, d) for s, d in scratch]
        + [pltpu.SemaphoreType.DMA((copies,))],
        compiler_params=pltpu.CompilerParams(vmem_limit_bytes=limit * 2**20),
        cost_estimate=pl.CostEstimate(
            flops=0, bytes_accessed=int(us * 3e6), transcendentals=0
        ),
    )


def exchange(near, far):
    last = lax.axis_size(SLAB) - 1
    pairs = [p for i in range(1, last, 2) for p in ((i, i + 1), (i + 1, i))]
    from_far = lax.ppermute(far, SLAB, pairs)
    return other_core(near), from_far


def swap(block, axis):
    return lax.all_to_all(block, axis, 0, 0, tiled=True)


def other_core(block):
    return lax.ppermute(block, "core", [(0, 1), (1, 0)])


def on_device(feat, counts, nb, low, high, w_one, w_two, cot):
    sites, channels = feat.shape
    offsets, rim = nb.shape[1], low.shape[0]
    scaling = 1.0 / math.sqrt(lax.axis_size(AXES) * sites)
    flat = ((sites, channels), BF)
    field = ((sites, channels), F32)
    letter = ((sites + 2 * rim, channels), BF)
    ends = ((2 * rim, channels), F32)
    weight = ((offsets, channels, channels), BF)
    sums = ((offsets + 1, channels, channels), BF)
    row = ((1, rim), jnp.int32)
    faces = ((2, rim), F32)
    picks = ((offsets, sites, WIDE), BF)
    broad = ((sites, offsets * channels), BF)
    near, far, sides = call(
        pack_kernel, "shhhhh", (letter, letter, faces),
        (flat, flat, ((offsets, sites), jnp.int32), row, row), 5, 1, limit=60,
    )(counts, feat, cot, nb.T, low.reshape(1, rim), high.reshape(1, rim))
    masked, grad, names, faces, picks, w_one, w_two = call(
        stage_kernel, "svvvvv",
        (flat, flat, ((rim, sites), F32), faces, picks, weight, weight), (), 1, 2,
    )(counts, feat, near, sides, w_one, w_two)
    near, far = exchange(near, far)
    near_two, far_two, own_grad, hidden, mine, theirs = call(
        main_kernel, "svvvvvvvvv", (ends, ends, field, flat, sums, sums),
        (broad, broad, ((WIDE, offsets * channels), BF)), 1, 5,
    )(counts, masked, grad, names, faces, picks, w_one, w_two, near, far)

    depth, plane = lax.axis_size(DEPTH), lax.axis_size(PLANE)
    share = (mine.astype(F32) + other_core(theirs).astype(F32)).astype(BF)
    share, near_two, far_two = lax.optimization_barrier((share, near_two, far_two))
    parts = swap(share.reshape(plane, -1, channels), PLANE)
    near, far = exchange(near_two, far_two)
    parts = jnp.sum(parts.astype(F32), 0).reshape(depth, -1, channels)
    parts, near, far = lax.optimization_barrier((parts, near, far))
    total = jnp.sum(swap(parts, DEPTH), 0) * scaling
    response, input_grad = call(
        last_kernel, "svvvvvvv", (flat, flat), (broad,), 1, 3
    )(counts, hidden, faces, near, far, own_grad, picks, w_two)
    total, response, input_grad = lax.optimization_barrier((total, response, input_grad))

    total = total.astype(BF)
    column = swap(jnp.broadcast_to(total, (depth, *total.shape)), DEPTH)
    column = column.reshape(-1, channels)
    whole = swap(jnp.broadcast_to(column, (plane, *column.shape)), PLANE)
    whole = whole.reshape(offsets + 1, channels, channels)
    other = other_core(whole)
    first_is_mine = lax.axis_index("core") == 0
    first = jnp.where(first_is_mine, whole, other)[:offsets]
    second = jnp.where(first_is_mine, other, whole)[:offsets]
    return response, input_grad, first, second


def solution(mesh):
    groups, slabs = mesh.devices.shape
    side = {64: 4, 16: 2, 4: 1}[slabs]
    fine = Mesh(mesh.devices.reshape(groups, side, side, 2, 2), AXES)
    rows, row = P(AXES, None), P(AXES)
    return jax.shard_map(
        on_device,
        mesh=fine,
        in_specs=(rows, row, rows, row, row, P(), P(), rows),
        out_specs=(rows, rows, P(), P()),
        check_vma=False,
    )
```

time: 156 us -> 133 us (0.85)
  blocking collectives: 85.7 us -> 35.5 us
  starting transfers between devices: 30.8 us -> 61 us
  Pallas kernels: 13.6 us -> 7.8 us
  other arithmetic: 1.86 us -> 4 us
    all_to_all x4 -> x2, blocking collectives: 85.7 us -> 35.5 us  [swap(): return lax.all_to_all(block, axis, 0, 0, tiled=True)]
    all_to_all x0 -> x2, starting transfers between devices: none -> 21 us  [swap(): return lax.all_to_all(block, axis, 0, 0, tiled=True)]
    ppermute x4 -> x2, waiting for transfers between devices: 13.2 us -> 0.01 us  [exchange(): from_far = lax.ppermute(far, SLAB, pairs)]
    all_to_all x0 -> x2, waiting for transfers between devices: none -> 12.5 us  [swap(): return lax.all_to_all(block, axis, 0, 0, tiled=True)]
    ppermute x2 -> x4, starting transfers between devices: 7.67 us -> 18.3 us  [other_core(): return lax.ppermute(block, 'core', [(0, 1), (1, 0)])]
    pallas_call x3 -> x4, Pallas kernels: 13.6 us -> 7.8 us  [the longest x1 3.95 us: on_device(): call(main_kernel, 'svvvvvvvvv', (ends, ends, field, flat, sums, sums), (b...]
    ppermute x2 -> x4, waiting for transfers between devices: 2.44 us -> 4.52 us  [other_core(): return lax.ppermute(block, 'core', [(0, 1), (1, 0)])]
    ppermute x4 -> x2, starting transfers between devices: 23.1 us -> 21.7 us  [exchange(): from_far = lax.ppermute(far, SLAB, pairs)]
  transfers between devices with their start and end apart: 6 -> 8, of which waited for: 3 -> 4; matrix products, arithmetic and copies ran while one was open for 0% -> 1% of each run, Pallas kernels for 2% -> 2%
where the time goes in v3:
time: 133 us; the launch traced here: 132 us
  starting transfers between devices  61 us (46%)
  blocking collectives  35.5 us (27%)
  waiting for transfers between devices  17 us (13%)
  Pallas kernels  7.8 us (6%)
  local copies, waits for them, and re-layouts  5.39 us (4%)
  other arithmetic  4 us (3%)
  between operations  1.43 us (1%)
    all_to_all x2, blocking collectives, swap(): return lax.all_to_all(block, axis, 0, 0, tiled=True)  35.5 us
    ppermute x2, starting transfers between devices, exchange(): from_far = lax.ppermute(far, SLAB, pairs)  21.7 us
    all_to_all x2, starting transfers between devices, swap(): return lax.all_to_all(block, axis, 0, 0, tiled=True)  21 us
    ppermute x4, starting transfers between devices, other_core(): return lax.ppermute(block, 'core', [(0, 1), (1, 0)])  18.3 us
    all_to_all x2, waiting for transfers between devices, swap(): return lax.all_to_all(block, axis, 0, 0, tiled=True)  12.5 us
    unnamed x10, local copies, waits for them, and re-layouts  4.56 us
    ppermute x4, waiting for transfers between devices, other_core(): return lax.ppermute(block, 'core', [(0, 1), (1, 0)])  4.52 us
    pallas_call x1, Pallas kernels, on_device(): call(main_kernel, 'svvvvvvvvv', (ends, ends, field, flat, sums, sums), (b...  3.95 us
  transfers between devices with their start and end apart: 8, of which 4 were waited for; matrix products, arithmetic and copies ran while one was open for 1% of the time, Pallas kernels for 2%

profile of v3, /device:TPU:1, one launch (start us, length us, event | category | flops | bytes accessed | tf_op | source)
XLA Modules:
  0.0 132.2 jit_solution(2605660048238982328)
XLA Ops:
  1.3 1.7 %shard_map.111 = (bf16[192,128]{1,0:T(8,128)(2,1)}, bf16[192,128]{1,0:T(8,128)(2,1)}, f32[2,32]{1,0:T(2,128)}) custom-call(s32[1]{0:T(128)S(6)} %copy.12.counts, bf16[128,128]{1,0:T(8,128)(2,1)} %feat.1, bf16[128,128]{1,0:T(8,128)(2,1)} %cot_h.1, s32[27,128]{1,0:T(8,128)} %bitcast.8, s32[1,32]{1,0:T(1,128)} %bitcast.9, s32[1,32]{1,0:T(1,128)} %bitcast.10), custom_call_target="tpu_custom_call" | custom-call | bytes 3000000 | tf_op jit(solution)/shard_map/pallas_call | solution.py:286
  3.0 8.8 %collective-permute-start = (bf16[192,128]{1,0:T(8,128)(2,1)}, bf16[192,128]{1,0:T(8,128)(2,1)S(1)}, u32[]{:S(2)}, u32[]{:S(2)}) collective-permute-start(bf16[192,128]{1,0:T(8,128)(2,1)} %get-tuple-element.31.own), channel_id=1, source_target_pairs={{0,1},{1,0},{2,3},{3,2},{4,5},{5,4},{6,7},{7,6},{8,9},{9,8},{10,11... | collective-permute-start | bytes 147464 | tf_op jit(solution)/shard_map/ppermute | solution.py:269
  11.7 10.0 %collective-permute-start.1 = (bf16[192,128]{1,0:T(8,128)(2,1)}, bf16[192,128]{1,0:T(8,128)(2,1)S(1)}, u32[]{:S(2)}, u32[]{:S(2)}) collective-permute-start(bf16[192,128]{1,0:T(8,128)(2,1)} %get-tuple-element.40), channel_id=1, source_target_pairs={{1,2},{2,1},{3,4},{4,3},{5,6},{6,5},{7,8},{8,7},{9,10},{10,9},{11,... | collective-permute-start | bytes 147464 | tf_op jit(solution)/shard_map/ppermute | solution.py:260
  21.7 0.0 copy-start
  21.7 1.2 copy-done
  22.9 0.0 copy-start.1
  22.9 1.2 copy-done.1
  24.1 0.0 copy-start.2
  24.1 0.8 copy-done.2
  24.8 0.0 copy-start.3
  24.8 0.8 copy-done.3
  25.6 0.0 copy-start.4
  25.6 0.7 copy-done.4
  26.3 0.6 shard_map.112
  26.9 0.0 collective-permute-done.near
  26.9 0.0 collective-permute-done.1.far
  26.9 3.9 %shard_map.113 = (f32[64,128]{1,0:T(8,128)S(1)}, f32[64,128]{1,0:T(8,128)S(1)}, f32[128,128]{1,0:T(8,128)S(1)}, bf16[128,128]{1,0:T(8,128)(2,1)S(1)}, bf16[28,12...) custom-call(s32[1]{0:T(128)S(6)} %copy.12.counts, bf16[128,128]{1,0:T(8,128)(2,1)S(1)} %get-tuple-element.33.masked, ...), custom_call_target="tpu_custom_call" | custom-call | bytes 15000000 | tf_op jit(solution)/shard_map/pallas_call | solution.py:295
  30.9 1.9 %collective-permute-start.2 = (bf16[28,128,128]{2,1,0:T(8,128)(2,1)S(1)}, bf16[28,128,128]{2,1,0:T(8,128)(2,1)S(1)}, u32[]{:S(2)}, u32[]{:S(2)}) collective-permute-start(bf16[28,128,128]{2,1,0:T(8,128)(2,1)S(1)} %get-tuple-element.42), channel_id=1, source_target_pairs={{0,1},{1,0},{2,3},{3,2},{4,5},{5,4},{6,7},{7,6},{8,9},{9,8},{10,11... | collective-permute-start | bytes 2752520 | tf_op jit(solution)/shard_map/ppermute | solution.py:269
  32.8 2.4 %collective-permute-done.2 = bf16[28,128,128]{2,1,0:T(8,128)(2,1)S(1)} collective-permute-done((bf16[28,128,128]{2,1,0:T(8,128)(2,1)S(1)}, bf16[28,128,128]{2,1,0:T(8,128)(2,1)S(1)}, u32[]{:S(2)}, u32[]{:S(2)}) %collective-permute-start.2) | collective-permute-done | bytes 917536 | tf_op jit(solution)/shard_map/ppermute | solution.py:269
  35.2 1.3 %add_convert_fusion = bf16[28,128,128]{2,1,0:T(8,128)(2,1)} fusion(bf16[28,128,128]{2,1,0:T(8,128)(2,1)S(1)} %collective-permute-done.2, bf16[28,128,128]{2,1,0:T(8,128)(2,1)S(1)} %get-tuple-element.41), kind=kLoop, calls=%fused_computation.1 | loop fusion | flops 1835008 | bytes 2752512 | tf_op jit(solution)/shard_map/convert_element_type | solution.py:301
  36.6 6.9 %all-to-all-start = ((bf16[16,224,128]{2,1,0:T(8,128)(2,1)}), bf16[16,224,128]{2,1,0:T(8,128)(2,1)}, u32[]{:S(2)}, u32[]{:S(2)}) async-start(bf16[16,224,128]{2,1,0:T(8,128)(2,1)} %bitcast.5), calls=%async_computation | async-start | bytes 1835008 | tf_op jit(solution)/shard_map/all_to_all | solution.py:265
  43.5 2.6 %collective-permute-start.3 = (f32[64,128]{1,0:T(8,128)S(1)}, f32[64,128]{1,0:T(8,128)S(1)}, u32[]{:S(2)}, u32[]{:S(2)}) collective-permute-start(f32[64,128]{1,0:T(8,128)S(1)} %get-tuple-element.46), channel_id=1, source_target_pairs={{0,1},{1,0},{2,3},{3,2},{4,5},{5,4},{6,7},{7,6},{8,9},{9,8},{10,11... | collective-permute-start | bytes 98312 | tf_op jit(solution)/shard_map/ppermute | solution.py:269
  46.1 11.7 %collective-permute-start.4 = (f32[64,128]{1,0:T(8,128)S(1)}, f32[64,128]{1,0:T(8,128)S(1)}, u32[]{:S(2)}, u32[]{:S(2)}) collective-permute-start(f32[64,128]{1,0:T(8,128)S(1)} %get-tuple-element.47), channel_id=1, source_target_pairs={{1,2},{2,1},{3,4},{4,3},{5,6},{6,5},{7,8},{8,7},{9,10},{10,9},{11,... | collective-permute-start | bytes 98312 | tf_op jit(solution)/shard_map/ppermute | solution.py:260
  57.8 0.7 all-to-all-done
  58.5 1.3 convert_reduce_fusion
  59.8 0.7 reshape.29
  60.5 0.0 collective-permute-done.3.near
  60.5 0.0 collective-permute-done.4.far
  60.5 14.1 %all-to-all-start.1 = ((f32[16,14,128]{2,1,0:T(8,128)}), f32[16,14,128]{2,1,0:T(8,128)S(1)}, u32[]{:S(2)}, u32[]{:S(2)}) async-start(f32[16,14,128]{2,1,0:T(8,128)} %reshape.29), calls=%async_computation.1 | async-start | bytes 262144 | tf_op jit(solution)/shard_map/all_to_all | solution.py:265
  74.6 1.6 %shard_map.114 = (bf16[128,128]{1,0:T(8,128)(2,1)}, bf16[128,128]{1,0:T(8,128)(2,1)}) custom-call(s32[1]{0:T(128)S(6)} %copy.12.counts, bf16[128,128]{1,0:T(8,128)(2,1)S(1)} %get-tuple-element.49.hidden, f32[2,32]{1,0:T(2,128)S(1)} %get-tuple-element.36.faces, f32[64,128]{1,0:T(8,128)S(1)} %collective-permute-done.3.near, ...), custom_call_target="tpu_custom_call" | custom-call | bytes 9000000 | tf_op jit(solution)/shard_map/pallas_call | solution.py:308
  76.2 11.8 %all-to-all-done.1 = f32[16,14,128]{2,1,0:T(8,128)S(1)} async-done(((f32[16,14,128]{2,1,0:T(8,128)}), f32[16,14,128]{2,1,0:T(8,128)S(1)}, u32[]{:S(2)}, u32[]{:S(2)}) %all-to-all-start.1) | async-done | bytes 114720 | tf_op jit(solution)/shard_map/all_to_all | solution.py:265
  88.0 16.7 %all_to_all.20 = bf16[16,14,128]{2,1,0:T(8,128)(2,1)S(1)} all-to-all(bf16[16,14,128]{2,1,0:T(8,128)(2,1)S(1)} %broadcast_in_dim.6), channel_id=1, replica_groups=mesh['dp'=8,'y'=4,'x'=4,'zh'=2,'core'=2] {'dp','zh'}, dimensions={0} | all-to-all | bytes 114688 | tf_op jit(solution)/shard_map/all_to_all | solution.py:265
  104.8 0.1 broadcast_in_dim.7
  104.9 18.8 %all_to_all.21 = bf16[16,224,128]{2,1,0:T(8,128)(2,1)S(1)} all-to-all(bf16[16,224,128]{2,1,0:T(8,128)(2,1)S(1)} %broadcast_in_dim.7), channel_id=1, replica_groups=mesh['dp'=8,'y'=4,'x'=4,'zh'=2,'core'=2] {'y','x'}, dimensions={0} | all-to-all | bytes 1835008 | tf_op jit(solution)/shard_map/all_to_all | solution.py:265
  123.7 5.1 %collective-permute-start.5 = (bf16[28,128,128]{2,1,0:T(8,128)(2,1)S(1)}, bf16[28,128,128]{2,1,0:T(8,128)(2,1)S(1)}, u32[]{:S(2)}, u32[]{:S(2)}) collective-permute-start(bf16[28,128,128]{2,1,0:T(8,128)(2,1)S(1)} %bitcast.6), channel_id=1, source_target_pairs={{0,1},{1,0},{2,3},{3,2},{4,5},{5,4},{6,7},{7,6},{8,9},{9,8},{10,11... | collective-permute-start | bytes 2752520 | tf_op jit(solution)/shard_map/ppermute | solution.py:269
  128.8 2.1 %collective-permute-done.5 = bf16[28,128,128]{2,1,0:T(8,128)(2,1)S(1)} collective-permute-done((bf16[28,128,128]{2,1,0:T(8,128)(2,1)S(1)}, bf16[28,128,128]{2,1,0:T(8,128)(2,1)S(1)}, u32[]{:S(2)}, u32[]{:S(2)}) %collective-permute-start.5) | collective-permute-done | bytes 917536 | tf_op jit(solution)/shard_map/ppermute | solution.py:269
  130.9 1.3 broadcast_select_fusion
  (4 shorter events, 0.1 us)
Async XLA Ops:
  3.0 23.9 %collective-permute-start = (bf16[192,128]{1,0:T(8,128)(2,1)}, bf16[192,128]{1,0:T(8,128)(2,1)S(1)}, u32[]{:S(2)}, u32[]{:S(2)}) collective-permute-start(bf16[192,128]{1,0:T(8,128)(2,1)} %get-tuple-element.31.own), channel_id=1, source_target_pairs={{0,1},{1,0},{2,3},{3,2},{4,5},{5,4},{6,7},{7,6},{8,9},{9,8},{10,11... | collective-permute-start | bytes 147464 | tf_op jit(solution)/shard_map/ppermute | solution.py:269
  11.7 15.2 %collective-permute-start.1 = (bf16[192,128]{1,0:T(8,128)(2,1)}, bf16[192,128]{1,0:T(8,128)(2,1)S(1)}, u32[]{:S(2)}, u32[]{:S(2)}) collective-permute-start(bf16[192,128]{1,0:T(8,128)(2,1)} %get-tuple-element.40), channel_id=1, source_target_pairs={{1,2},{2,1},{3,4},{4,3},{5,6},{6,5},{7,8},{8,7},{9,10},{10,9},{11,... | collective-permute-start | bytes 147464 | tf_op jit(solution)/shard_map/ppermute | solution.py:260
  21.7 1.2 copy-start
  22.9 1.2 copy-start.1
  24.1 0.8 copy-start.2
  24.8 0.8 copy-start.3
  25.6 0.7 copy-start.4
  30.9 4.4 %collective-permute-start.2 = (bf16[28,128,128]{2,1,0:T(8,128)(2,1)S(1)}, bf16[28,128,128]{2,1,0:T(8,128)(2,1)S(1)}, u32[]{:S(2)}, u32[]{:S(2)}) collective-permute-start(bf16[28,128,128]{2,1,0:T(8,128)(2,1)S(1)} %get-tuple-element.42), channel_id=1, source_target_pairs={{0,1},{1,0},{2,3},{3,2},{4,5},{5,4},{6,7},{7,6},{8,9},{9,8},{10,11... | collective-permute-start | bytes 2752520 | tf_op jit(solution)/shard_map/ppermute | solution.py:269
  36.6 21.9 %all-to-all-start = ((bf16[16,224,128]{2,1,0:T(8,128)(2,1)}), bf16[16,224,128]{2,1,0:T(8,128)(2,1)}, u32[]{:S(2)}, u32[]{:S(2)}) async-start(bf16[16,224,128]{2,1,0:T(8,128)(2,1)} %bitcast.5), calls=%async_computation | async-start | bytes 1835008 | tf_op jit(solution)/shard_map/all_to_all | solution.py:265
  43.5 17.0 %collective-permute-start.3 = (f32[64,128]{1,0:T(8,128)S(1)}, f32[64,128]{1,0:T(8,128)S(1)}, u32[]{:S(2)}, u32[]{:S(2)}) collective-permute-start(f32[64,128]{1,0:T(8,128)S(1)} %get-tuple-element.46), channel_id=1, source_target_pairs={{0,1},{1,0},{2,3},{3,2},{4,5},{5,4},{6,7},{7,6},{8,9},{9,8},{10,11... | collective-permute-start | bytes 98312 | tf_op jit(solution)/shard_map/ppermute | solution.py:269
  46.1 14.4 %collective-permute-start.4 = (f32[64,128]{1,0:T(8,128)S(1)}, f32[64,128]{1,0:T(8,128)S(1)}, u32[]{:S(2)}, u32[]{:S(2)}) collective-permute-start(f32[64,128]{1,0:T(8,128)S(1)} %get-tuple-element.47), channel_id=1, source_target_pairs={{1,2},{2,1},{3,4},{4,3},{5,6},{6,5},{7,8},{8,7},{9,10},{10,9},{11,... | collective-permute-start | bytes 98312 | tf_op jit(solution)/shard_map/ppermute | solution.py:260
  60.5 27.5 %all-to-all-start.1 = ((f32[16,14,128]{2,1,0:T(8,128)}), f32[16,14,128]{2,1,0:T(8,128)S(1)}, u32[]{:S(2)}, u32[]{:S(2)}) async-start(f32[16,14,128]{2,1,0:T(8,128)} %reshape.29), calls=%async_computation.1 | async-start | bytes 262144 | tf_op jit(solution)/shard_map/all_to_all | solution.py:265
  123.7 7.2 %collective-permute-start.5 = (bf16[28,128,128]{2,1,0:T(8,128)(2,1)S(1)}, bf16[28,128,128]{2,1,0:T(8,128)(2,1)S(1)}, u32[]{:S(2)}, u32[]{:S(2)}) collective-permute-start(bf16[28,128,128]{2,1,0:T(8,128)(2,1)S(1)} %bitcast.6), channel_id=1, source_target_pairs={{0,1},{1,0},{2,3},{3,2},{4,5},{5,4},{6,7},{7,6},{8,9},{9,8},{10,11... | collective-permute-start | bytes 2752520 | tf_op jit(solution)/shard_map/ppermute | solution.py:269

commit v4 on v3

--- a/solution.py
+++ b/solution.py
@@ -71,31 +71,29 @@
     return lax.axis_index("core") == 0
 
 
-def near_and_far(faces):
+def near_and_far(low, high):
     above = near_is_above()
-    low, high = faces[0:1], faces[1:2]
     return jnp.where(above, high, low), jnp.where(above, low, high)
 
 
 def pack_kernel(
     counts, feat_h, cot_h, map_h, low_h, high_h, near, far, faces,
-    feat, cot, table, low_s, high_s, sems,
+    feat, cot, table, low, high, sems,
 ):
     for copy in fetch(
-        (feat_h, cot_h, map_h, low_h, high_h), (feat, cot, table, low_s, high_s), sems
+        (feat_h, cot_h, map_h, low_h, high_h), (feat, cot, table, low, high), sems
     ):
         copy.wait()
-    sites, rim = feat.shape[0], low_s.shape[1]
-    live = live_rows(counts, sites)
+    live = live_rows(counts, feat.shape[0])
+    faces[0:1] = low[...].astype(F32)
+    faces[1:2] = high[...].astype(F32)
+    offsets, sites = table.shape
+    rim = low.shape[1]
     masked = jnp.where(live, feat[...].astype(F32), 0.0).astype(BF)
     grad = jnp.where(live, cot[...].astype(F32), 0.0).astype(BF)
-    offsets = table.shape[0]
-    names = jnp.concatenate(
-        [table[...].astype(F32), jnp.full((rim - offsets, sites), NOWHERE, F32)], 0
-    ).astype(BF)
-    faces[0:1] = low_s[...].astype(F32)
-    faces[1:2] = high_s[...].astype(F32)
-    for out, row in zip((near, far), near_and_far(faces)):
+    blank = jnp.full((rim - offsets, sites), NOWHERE, F32)
+    names = jnp.concatenate([table[...].astype(F32), blank], 0).astype(BF)
+    for out, row in zip((far, near), near_and_far(faces[1:2], faces[0:1])):
         out[:sites] = grad
         picks = face_sites(row, sites).T.astype(BF)
         out[sites : sites + rim] = dot(picks, masked).astype(BF)
@@ -103,15 +101,15 @@
 
 
 def stage_kernel(
-    counts, feat, own, faces_in, w_one_in, w_two_in,
+    counts, feat, own, sides, w_one_in, w_two_in,
     masked, grad, names, faces, picks, w_one, w_two, sems,
 ):
-    sites, rim = feat.shape[0], faces.shape[1]
+    sites, rim = feat.shape[0], sides.shape[1]
     live = live_rows(counts, sites)
     masked[...] = jnp.where(live, feat[...].astype(F32), 0.0).astype(BF)
     grad[...] = own[:sites]
     names[...] = own[sites + rim :].astype(F32)
-    faces[...] = faces_in[...]
+    faces[...] = sides[...]
     columns = names[...].T
     for k in range(picks.shape[0]):
         picks[k] = pick_matrix(columns, k)
@@ -141,15 +139,15 @@
 
 
 def main_kernel(
-    counts, masked, own_grads, own_names, faces, picks, w_one, w_two, near, far,
-    near_out, far_out, own_grad, hidden_ref, mine, theirs,
+    counts, masked, own_grads, own_names, faces, picks, w_one, w_two, far, near,
+    far_out, own_grad, hidden_ref, mine, theirs,
     picked, held, kept, sems,
 ):
     offsets, channels = w_one.shape[0], w_one.shape[1]
     sites, rim = masked.shape[0], faces.shape[1]
     live = live_rows(counts, sites)
     above = near_is_above()
-    near_row, far_row = near_and_far(faces)
+    near_row, far_row = near_and_far(faces[0:1], faces[1:2])
     rims = slice(sites, sites + rim)
     near_rim, far_rim = near[rims].astype(F32), far[rims].astype(F32)
     extended = extend(
@@ -198,8 +196,12 @@
     to_above, to_below = ext_grad[sites + rim : sites + 2 * rim], ext_grad[rims]
     near_pick = face_sites(near_row, sites).T.astype(BF)
     far_pick = face_sites(far_row, sites).T.astype(BF)
-    near_out[:rim] = dot(near_pick, hidden.astype(BF))
-    near_out[rim:] = jnp.where(above, to_above, to_below)
+    to_near = jnp.where(above, to_above, to_below)
+    coarse = to_near.astype(BF)
+    theirs[offsets, :rim] = dot(near_pick, hidden.astype(BF)).astype(BF)
+    theirs[offsets, rim : 2 * rim] = coarse
+    theirs[offsets, 2 * rim : 3 * rim] = (to_near - coarse.astype(F32)).astype(BF)
+    theirs[offsets, 3 * rim :] = jnp.zeros((channels - 3 * rim, channels), BF)
     far_out[:rim] = dot(far_pick, hidden.astype(BF))
     far_out[rim:] = jnp.where(above, to_below, to_above)
     first_is_mine = lax.axis_index("core") == 0
@@ -212,7 +214,6 @@
             mine[k + j] = jnp.where(first_is_mine, a, b).astype(BF)
             theirs[k + j] = jnp.where(first_is_mine, b, a).astype(BF)
     mine[offsets] = jnp.zeros((channels, channels), BF)
-    theirs[offsets] = jnp.zeros((channels, channels), BF)
 
 
 def last_kernel(
@@ -223,14 +224,16 @@
     offsets, channels = w_two.shape[0], w_two.shape[1]
     live = live_rows(counts, sites)
     above = near_is_above()
-    near_row, far_row = near_and_far(faces)
-    grad = own_grad[...] + dot(face_sites(near_row, sites), near[rim:], exact=True)
+    near_row, far_row = near_and_far(faces[0:1], faces[1:2])
+    near_grad = near[rim : 2 * rim].astype(F32) + near[2 * rim : 3 * rim].astype(F32)
+    grad = own_grad[...] + dot(face_sites(near_row, sites), near_grad, exact=True)
     grad = grad + dot(face_sites(far_row, sites), far[rim:], exact=True)
     input_grad[...] = jnp.where(live, grad, 0.0).astype(BF)
+    near_rim = near[:rim].astype(F32)
     extended = extend(
         hidden[...].astype(F32),
-        jnp.where(above, far[:rim], near[:rim]),
-        jnp.where(above, near[:rim], far[:rim]),
+        jnp.where(above, far[:rim], near_rim),
+        jnp.where(above, near_rim, far[:rim]),
     )
     for k in range(offsets):
         picked[:, lanes(k, channels)] = dot(picks[k], extended).astype(BF)
@@ -238,12 +241,16 @@
     response[...] = jnp.where(live, second_pre, 0.0).astype(BF)
 
 
-def call(kernel, places, outs, scratch, copies, us, limit=32):
-    memory = {"s": pltpu.SMEM, "v": pltpu.VMEM, "h": pltpu.HBM}
+def call(kernel, places, outs, scratch, copies, us, limit=16):
+    spec = {
+        "s": pl.BlockSpec(memory_space=pltpu.SMEM),
+        "v": pl.BlockSpec(memory_space=pltpu.VMEM),
+        "h": pl.BlockSpec(memory_space=pltpu.HBM),
+    }
     return pl.pallas_call(
         kernel,
         out_shape=[jax.ShapeDtypeStruct(s, d) for s, d in outs],
-        in_specs=[pl.BlockSpec(memory_space=memory[p]) for p in places],
+        in_specs=[spec[p] for p in places],
         out_specs=[pl.BlockSpec(memory_space=pltpu.VMEM)] * len(outs),
         scratch_shapes=[pltpu.VMEM(s, d) for s, d in scratch]
         + [pltpu.SemaphoreType.DMA((copies,))],
@@ -254,11 +261,10 @@
     )
 
 
-def exchange(near, far):
+def far_slab(block):
     last = lax.axis_size(SLAB) - 1
     pairs = [p for i in range(1, last, 2) for p in ((i, i + 1), (i + 1, i))]
-    from_far = lax.ppermute(far, SLAB, pairs)
-    return other_core(near), from_far
+    return lax.ppermute(block, SLAB, pairs)
 
 
 def swap(block, axis):
@@ -275,7 +281,7 @@
     scaling = 1.0 / math.sqrt(lax.axis_size(AXES) * sites)
     flat = ((sites, channels), BF)
     field = ((sites, channels), F32)
-    letter = ((sites + 2 * rim, channels), BF)
+    message = ((sites + 2 * rim, channels), BF)
     ends = ((2 * rim, channels), F32)
     weight = ((offsets, channels, channels), BF)
     sums = ((offsets + 1, channels, channels), BF)
@@ -283,39 +289,39 @@
     faces = ((2, rim), F32)
     picks = ((offsets, sites, WIDE), BF)
     broad = ((sites, offsets * channels), BF)
-    near, far, sides = call(
-        pack_kernel, "shhhhh", (letter, letter, faces),
+    low, high, table = low.reshape(1, rim), high.reshape(1, rim), nb.T
+    letters = call(
+        pack_kernel, "shhhhh", (message, message, faces),
         (flat, flat, ((offsets, sites), jnp.int32), row, row), 5, 1, limit=60,
-    )(counts, feat, cot, nb.T, low.reshape(1, rim), high.reshape(1, rim))
+    )(counts, feat, cot, table, low, high)
     masked, grad, names, faces, picks, w_one, w_two = call(
         stage_kernel, "svvvvv",
         (flat, flat, ((rim, sites), F32), faces, picks, weight, weight), (), 1, 2,
-    )(counts, feat, near, sides, w_one, w_two)
-    near, far = exchange(near, far)
-    near_two, far_two, own_grad, hidden, mine, theirs = call(
-        main_kernel, "svvvvvvvvv", (ends, ends, field, flat, sums, sums),
+    )(counts, feat, letters[1], letters[2], w_one, w_two)
+    near, far = other_core(letters[0]), far_slab(letters[1])
+    far_two, own_grad, hidden, mine, theirs = call(
+        main_kernel, "svvvvvvvvv", (ends, field, flat, sums, sums),
         (broad, broad, ((WIDE, offsets * channels), BF)), 1, 5,
-    )(counts, masked, grad, names, faces, picks, w_one, w_two, near, far)
+    )(counts, masked, grad, names, faces, picks, w_one, w_two, far, near)
 
     depth, plane = lax.axis_size(DEPTH), lax.axis_size(PLANE)
-    share = (mine.astype(F32) + other_core(theirs).astype(F32)).astype(BF)
-    share, near_two, far_two = lax.optimization_barrier((share, near_two, far_two))
+    near = other_core(theirs)
+    share = (mine.astype(F32) + near.astype(F32)).astype(BF)
     parts = swap(share.reshape(plane, -1, channels), PLANE)
-    near, far = exchange(near_two, far_two)
     parts = jnp.sum(parts.astype(F32), 0).reshape(depth, -1, channels)
-    parts, near, far = lax.optimization_barrier((parts, near, far))
     total = jnp.sum(swap(parts, DEPTH), 0) * scaling
-    response, input_grad = call(
-        last_kernel, "svvvvvvv", (flat, flat), (broad,), 1, 3
-    )(counts, hidden, faces, near, far, own_grad, picks, w_two)
-    total, response, input_grad = lax.optimization_barrier((total, response, input_grad))
 
     total = total.astype(BF)
     column = swap(jnp.broadcast_to(total, (depth, *total.shape)), DEPTH)
     column = column.reshape(-1, channels)
+    column, far_two = lax.optimization_barrier((column, far_two))
     whole = swap(jnp.broadcast_to(column, (plane, *column.shape)), PLANE)
+    whole, far = lax.optimization_barrier((whole, far_slab(far_two)))
     whole = whole.reshape(offsets + 1, channels, channels)
     other = other_core(whole)
+    response, input_grad = call(
+        last_kernel, "svvvvvvv", (flat, flat), (broad,), 1, 3
+    )(counts, hidden, faces, near[offsets], far, own_grad, picks, w_two)
     first_is_mine = lax.axis_index("core") == 0
     first = jnp.where(first_is_mine, whole, other)[:offsets]
     second = jnp.where(first_is_mine, other, whole)[:offsets]

time: 133 us -> 130 us (0.977)
  the two profiles are of different devices: /device:TPU:1 before, /device:TPU:9 now
where the time goes in v4:
time: 130 us
  blocking collectives  57.4 us (44%)
  starting transfers between devices  42.2 us (32%)
  waiting for transfers between devices  11 us (8%)
  Pallas kernels  7.81 us (6%)
  local copies, waits for them, and re-layouts  6.44 us (5%)
  other arithmetic  3.29 us (3%)
  between operations  1.42 us (1%)
    all_to_all x3, blocking collectives, swap(): return lax.all_to_all(block, axis, 0, 0, tiled=True)  57.4 us
    ppermute x2, starting transfers between devices, far_slab(): return lax.ppermute(block, SLAB, pairs)  21.4 us
    ppermute x3, starting transfers between devices, other_core(): return lax.ppermute(block, 'core', [(0, 1), (1, 0)])  14.8 us
    ppermute x2, waiting for transfers between devices, far_slab(): return lax.ppermute(block, SLAB, pairs)  8.53 us
    all_to_all x1, starting transfers between devices, swap(): return lax.all_to_all(block, axis, 0, 0, tiled=True)  5.93 us
    unnamed x12, local copies, waits for them, and re-layouts  4.57 us
    pallas_call x1, Pallas kernels, on_device(): call(main_kernel, 'svvvvvvvvv', (ends, field, flat, sums, sums), (broad,...  3.95 us
    select_n x1, other arithmetic, on_device(): second = jnp.where(first_is_mine, other, whole)[:offsets]  2.75 us
  transfers between devices with their start and end apart: 6, of which 3 were waited for; matrix products, arithmetic and copies ran while one was open for 1% of the time, Pallas kernels for 2%

profile of v4, /device:TPU:9, one launch (start us, length us, event | category | flops | bytes accessed | tf_op | source)
XLA Modules:
  0.0 129.6 jit_solution(1037935417976153841)
XLA Ops:
  1.3 1.7 %shard_map.111 = (bf16[192,128]{1,0:T(8,128)(2,1)}, bf16[192,128]{1,0:T(8,128)(2,1)}, f32[2,32]{1,0:T(2,128)}) custom-call(s32[1]{0:T(128)S(6)} %copy.12.counts, bf16[128,128]{1,0:T(8,128)(2,1)} %feat.1, bf16[128,128]{1,0:T(8,128)(2,1)} %cot_h.1, s32[27,128]{1,0:T(8,128)} %bitcast.8, s32[1,32]{1,0:T(1,128)} %bitcast.9, s32[1,32]{1,0:T(1,128)} %bitcast.10), custom_call_target="tpu_custom_call" | custom-call | bytes 3000000 | tf_op jit(solution)/shard_map/pallas_call | solution.py:293
  3.0 16.0 %collective-permute-start = (bf16[192,128]{1,0:T(8,128)(2,1)}, bf16[192,128]{1,0:T(8,128)(2,1)S(1)}, u32[]{:S(2)}, u32[]{:S(2)}) collective-permute-start(bf16[192,128]{1,0:T(8,128)(2,1)} %get-tuple-element.25.own), channel_id=1, source_target_pairs={{1,2},{2,1},{3,4},{4,3},{5,6},{6,5},{7,8},{8,7},{9,10},{10,9},{11,... | collective-permute-start | bytes 147464 | tf_op jit(solution)/shard_map/ppermute | solution.py:267
  19.0 3.8 %collective-permute-start.1 = (bf16[192,128]{1,0:T(8,128)(2,1)}, bf16[192,128]{1,0:T(8,128)(2,1)S(1)}, u32[]{:S(2)}, u32[]{:S(2)}) collective-permute-start(bf16[192,128]{1,0:T(8,128)(2,1)} %get-tuple-element.34), channel_id=1, source_target_pairs={{0,1},{1,0},{2,3},{3,2},{4,5},{5,4},{6,7},{7,6},{8,9},{9,8},{10,11... | collective-permute-start | bytes 147464 | tf_op jit(solution)/shard_map/ppermute | solution.py:275
  22.8 0.0 copy-start
  22.8 1.2 copy-done
  24.0 0.0 copy-start.1
  24.0 1.2 copy-done.1
  25.1 0.0 copy-start.2
  25.1 0.8 copy-done.2
  25.9 0.0 copy-start.3
  25.9 0.8 copy-done.3
  26.7 0.0 copy-start.4
  26.7 0.7 copy-done.4
  27.4 0.6 shard_map.112
  28.0 0.0 collective-permute-done.far
  28.0 0.0 collective-permute-done.1.near
  28.0 4.0 %shard_map.113 = (f32[64,128]{1,0:T(8,128)S(1)}, f32[128,128]{1,0:T(8,128)S(1)}, bf16[128,128]{1,0:T(8,128)(2,1)S(1)}, bf16[28,128,128]{2,1,0:T(8,128)(2,1)S(1)}, bf16[28,128,128]{2,1,0:T(8,128)(2,1)S(1)}) custom-call(s32[1]{0:T(128)S(6)} %copy.12.counts, bf16[128,128]{1,0:T(8,128)(2,1)S(1)} %get-tuple-element.27.masked, ...), custom_call_target="tpu_custom_call" | custom-call | bytes 15000000 | tf_op jit(solution)/shard_map/pallas_call | solution.py:302
  32.0 1.9 %collective-permute-start.2 = (bf16[28,128,128]{2,1,0:T(8,128)(2,1)S(1)}, bf16[28,128,128]{2,1,0:T(8,128)(2,1)S(1)}, u32[]{:S(2)}, u32[]{:S(2)}) collective-permute-start(bf16[28,128,128]{2,1,0:T(8,128)(2,1)S(1)} %get-tuple-element.36), channel_id=1, source_target_pairs={{0,1},{1,0},{2,3},{3,2},{4,5},{5,4},{6,7},{7,6},{8,9},{9,8},{10,11... | collective-permute-start | bytes 2752520 | tf_op jit(solution)/shard_map/ppermute | solution.py:275
  33.9 2.4 %collective-permute-done.2 = bf16[28,128,128]{2,1,0:T(8,128)(2,1)S(1)} collective-permute-done((bf16[28,128,128]{2,1,0:T(8,128)(2,1)S(1)}, bf16[28,128,128]{2,1,0:T(8,128)(2,1)S(1)}, u32[]{:S(2)}, u32[]{:S(2)}) %collective-permute-start.2) | collective-permute-done | bytes 917536 | tf_op jit(solution)/shard_map/ppermute | solution.py:275
  36.3 0.0 copy-start.5
  36.3 0.4 add_convert_fusion
  36.7 17.9 %all_to_all.20 = bf16[16,224,128]{2,1,0:T(8,128)(2,1)S(1)} all-to-all(bf16[16,224,128]{2,1,0:T(8,128)(2,1)S(1)} %bitcast.7), channel_id=1, replica_groups=mesh['dp'=8,'y'=4,'x'=4,'zh'=2,'core'=2] {'y','x'}, dimensions={0} | all-to-all | bytes 1835008 | tf_op jit(solution)/shard_map/all_to_all | solution.py:271
  54.6 0.0 copy-done.5
  54.6 0.1 convert_reduce_fusion
  54.7 23.1 %all_to_all.21 = f32[16,14,128]{2,1,0:T(8,128)S(1)} all-to-all(f32[16,14,128]{2,1,0:T(8,128)S(1)} %reshape.29), channel_id=1, replica_groups=mesh['dp'=8,'y'=4,'x'=4,'zh'=2,'core'=2] {'dp','zh'}, dimensions={0} | all-to-all | bytes 229376 | tf_op jit(solution)/shard_map/all_to_all | solution.py:271
  77.9 16.4 %all_to_all.22 = bf16[16,14,128]{2,1,0:T(8,128)(2,1)S(1)} all-to-all(bf16[16,14,128]{2,1,0:T(8,128)(2,1)S(1)} %broadcast_in_dim.6), channel_id=1, replica_groups=mesh['dp'=8,'y'=4,'x'=4,'zh'=2,'core'=2] {'dp','zh'}, dimensions={0} | all-to-all | bytes 114688 | tf_op jit(solution)/shard_map/all_to_all | solution.py:271
  94.4 1.1 broadcast_in_dim.7
  95.4 5.9 %all-to-all-start.3 = ((bf16[16,224,128]{2,1,0:T(8,128)(2,1)}), bf16[16,224,128]{2,1,0:T(8,128)(2,1)}, u32[]{:S(2)}, u32[]{:S(2)}) async-start(bf16[16,224,128]{2,1,0:T(8,128)(2,1)} %broadcast_in_dim.7), calls=%async_computation.3 | async-start | bytes 1835008 | tf_op jit(solution)/shard_map/all_to_all | solution.py:271
  101.4 5.4 %collective-permute-start.3 = (f32[64,128]{1,0:T(8,128)S(1)}, f32[64,128]{1,0:T(8,128)S(1)}, u32[]{:S(2)}, u32[]{:S(2)}) collective-permute-start(f32[64,128]{1,0:T(8,128)S(1)} %get-tuple-element.40), channel_id=1, source_target_pairs={{1,2},{2,1},{3,4},{4,3},{5,6},{6,5},{7,8},{8,7},{9,10},{10,9},{11,... | collective-permute-start | bytes 98312 | tf_op jit(solution)/shard_map/ppermute | solution.py:267
  106.8 8.5 %collective-permute-done.3.far = f32[64,128]{1,0:T(8,128)S(1)} collective-permute-done((f32[64,128]{1,0:T(8,128)S(1)}, f32[64,128]{1,0:T(8,128)S(1)}, u32[]{:S(2)}, u32[]{:S(2)}) %collective-permute-start.3) | collective-permute-done | bytes 32800 | tf_op jit(solution)/shard_map/ppermute | solution.py:267
  115.3 0.0 all-to-all-done.3
  115.3 9.1 %collective-permute-start.4 = (bf16[28,128,128]{2,1,0:T(8,128)(2,1)}, bf16[28,128,128]{2,1,0:T(8,128)(2,1)}, u32[]{:S(2)}, u32[]{:S(2)}) collective-permute-start(bf16[28,128,128]{2,1,0:T(8,128)(2,1)} %bitcast.5), channel_id=1, source_target_pairs={{0,1},{1,0},{2,3},{3,2},{4,5},{5,4},{6,7},{7,6},{8,9},{9,8},{10,11... | collective-permute-start | bytes 2752520 | tf_op jit(solution)/shard_map/ppermute | solution.py:275
  124.4 0.8 slice_bitcast_fusion.near
  125.2 1.6 %shard_map.114 = (bf16[128,128]{1,0:T(8,128)(2,1)}, bf16[128,128]{1,0:T(8,128)(2,1)}) custom-call(s32[1]{0:T(128)S(6)} %copy.12.counts, bf16[128,128]{1,0:T(8,128)(2,1)S(1)} %get-tuple-element.35.hidden, f32[2,32]{1,0:T(2,128)S(1)} %get-tuple-element.30.faces, bf16[128,128]{1,0:T(8,128)(2,1)S(1)} %slice_bitcast_fusion.near, ...), custom_call_target="tpu_custom_call" | custom-call | bytes 9000000 | tf_op jit(solution)/shard_map/pallas_call | solution.py:322
  126.8 0.1 collective-permute-done.4
  126.8 2.8 %broadcast_select_fusion = (bf16[27,128,128]{2,1,0:T(8,128)(2,1)}, bf16[27,128,128]{2,1,0:T(8,128)(2,1)}) fusion(pred[]{:T(512)S(6)} %eq.3, bf16[28,128,128]{2,1,0:T(8,128)(2,1)} %collective-permute-done.4, bf16[28,128,128]{2,1,0:T(8,128)(2,1)} %bitcast.5), kind=kLoop, calls=%fused_computation.2 | loop fusion | flops 884736 | bytes 3538945 | tf_op jit(solution)/shard_map/jit(_where)/select_n | solution.py:327
  (5 shorter events, 0.1 us)
Async XLA Ops:
  3.0 25.0 %collective-permute-start = (bf16[192,128]{1,0:T(8,128)(2,1)}, bf16[192,128]{1,0:T(8,128)(2,1)S(1)}, u32[]{:S(2)}, u32[]{:S(2)}) collective-permute-start(bf16[192,128]{1,0:T(8,128)(2,1)} %get-tuple-element.25.own), channel_id=1, source_target_pairs={{1,2},{2,1},{3,4},{4,3},{5,6},{6,5},{7,8},{8,7},{9,10},{10,9},{11,... | collective-permute-start | bytes 147464 | tf_op jit(solution)/shard_map/ppermute | solution.py:267
  19.0 9.0 %collective-permute-start.1 = (bf16[192,128]{1,0:T(8,128)(2,1)}, bf16[192,128]{1,0:T(8,128)(2,1)S(1)}, u32[]{:S(2)}, u32[]{:S(2)}) collective-permute-start(bf16[192,128]{1,0:T(8,128)(2,1)} %get-tuple-element.34), channel_id=1, source_target_pairs={{0,1},{1,0},{2,3},{3,2},{4,5},{5,4},{6,7},{7,6},{8,9},{9,8},{10,11... | collective-permute-start | bytes 147464 | tf_op jit(solution)/shard_map/ppermute | solution.py:275
  22.8 1.2 copy-start
  24.0 1.2 copy-start.1
  25.1 0.8 copy-start.2
  25.9 0.8 copy-start.3
  26.7 0.7 copy-start.4
  32.0 4.4 %collective-permute-start.2 = (bf16[28,128,128]{2,1,0:T(8,128)(2,1)S(1)}, bf16[28,128,128]{2,1,0:T(8,128)(2,1)S(1)}, u32[]{:S(2)}, u32[]{:S(2)}) collective-permute-start(bf16[28,128,128]{2,1,0:T(8,128)(2,1)S(1)} %get-tuple-element.36), channel_id=1, source_target_pairs={{0,1},{1,0},{2,3},{3,2},{4,5},{5,4},{6,7},{7,6},{8,9},{9,8},{10,11... | collective-permute-start | bytes 2752520 | tf_op jit(solution)/shard_map/ppermute | solution.py:275
  36.3 18.3 %copy-start.5 = (bf16[28,128,128]{2,1,0:T(8,128)(2,1)}, bf16[28,128,128]{2,1,0:T(8,128)(2,1)S(1)}, u32[]{:S(2)}) copy-start(bf16[28,128,128]{2,1,0:T(8,128)(2,1)S(1)} %collective-permute-done.2) | copy-start | bytes 2752516
  95.4 19.9 %all-to-all-start.3 = ((bf16[16,224,128]{2,1,0:T(8,128)(2,1)}), bf16[16,224,128]{2,1,0:T(8,128)(2,1)}, u32[]{:S(2)}, u32[]{:S(2)}) async-start(bf16[16,224,128]{2,1,0:T(8,128)(2,1)} %broadcast_in_dim.7), calls=%async_computation.3 | async-start | bytes 1835008 | tf_op jit(solution)/shard_map/all_to_all | solution.py:271
  101.4 13.9 %collective-permute-start.3 = (f32[64,128]{1,0:T(8,128)S(1)}, f32[64,128]{1,0:T(8,128)S(1)}, u32[]{:S(2)}, u32[]{:S(2)}) collective-permute-start(f32[64,128]{1,0:T(8,128)S(1)} %get-tuple-element.40), channel_id=1, source_target_pairs={{1,2},{2,1},{3,4},{4,3},{5,6},{6,5},{7,8},{8,7},{9,10},{10,9},{11,... | collective-permute-start | bytes 98312 | tf_op jit(solution)/shard_map/ppermute | solution.py:267
  115.3 11.5 %collective-permute-start.4 = (bf16[28,128,128]{2,1,0:T(8,128)(2,1)}, bf16[28,128,128]{2,1,0:T(8,128)(2,1)}, u32[]{:S(2)}, u32[]{:S(2)}) collective-permute-start(bf16[28,128,128]{2,1,0:T(8,128)(2,1)} %bitcast.5), channel_id=1, source_target_pairs={{0,1},{1,0},{2,3},{3,2},{4,5},{5,4},{6,7},{7,6},{8,9},{9,8},{10,11... | collective-permute-start | bytes 2752520 | tf_op jit(solution)/shard_map/ppermute | solution.py:275

commit v5 on v4

--- a/solution.py
+++ b/solution.py
@@ -7,10 +7,10 @@
 from jax.experimental.pallas import tpu as pltpu
 from jax.sharding import Mesh, PartitionSpec as P
 
-AXES = ("dp", "y", "x", "zh", "core")
+AXES = ("column", "pair", "y", "x", "zh", "core")
 SLAB = ("y", "x", "zh", "core")
-PLANE = ("y", "x")
-DEPTH = ("dp", "zh")
+BLOCK = ("pair", "y", "x")
+COLUMN = ("column", "zh")
 BF = jnp.bfloat16
 F32 = jnp.float32
 WIDE = 256
@@ -279,6 +279,7 @@
     sites, channels = feat.shape
     offsets, rim = nb.shape[1], low.shape[0]
     scaling = 1.0 / math.sqrt(lax.axis_size(AXES) * sites)
+    half = math.sqrt(scaling)
     flat = ((sites, channels), BF)
     field = ((sites, channels), F32)
     message = ((sites + 2 * rim, channels), BF)
@@ -304,24 +305,24 @@
         (broad, broad, ((WIDE, offsets * channels), BF)), 1, 5,
     )(counts, masked, grad, names, faces, picks, w_one, w_two, far, near)
 
-    depth, plane = lax.axis_size(DEPTH), lax.axis_size(PLANE)
+    column, block = lax.axis_size(COLUMN), lax.axis_size(BLOCK)
     near = other_core(theirs)
     share = (mine.astype(F32) + near.astype(F32)).astype(BF)
-    parts = swap(share.reshape(plane, -1, channels), PLANE)
-    parts = jnp.sum(parts.astype(F32), 0).reshape(depth, -1, channels)
-    total = jnp.sum(swap(parts, DEPTH), 0) * scaling
-
-    total = total.astype(BF)
-    column = swap(jnp.broadcast_to(total, (depth, *total.shape)), DEPTH)
-    column = column.reshape(-1, channels)
-    column, far_two = lax.optimization_barrier((column, far_two))
-    whole = swap(jnp.broadcast_to(column, (plane, *column.shape)), PLANE)
-    whole, far = lax.optimization_barrier((whole, far_slab(far_two)))
-    whole = whole.reshape(offsets + 1, channels, channels)
-    other = other_core(whole)
+    share, far_two = lax.optimization_barrier((share, far_two))
+    parts = swap(share.reshape(block, -1, channels), BLOCK)
+    far = far_slab(far_two)
+    parts = (jnp.sum(parts.astype(F32), 0) * half).astype(BF)
+    parts, far = lax.optimization_barrier((parts, far))
+    parts = swap(jnp.broadcast_to(parts, (column, *parts.shape)), COLUMN)
     response, input_grad = call(
         last_kernel, "svvvvvvv", (flat, flat), (broad,), 1, 3
     )(counts, hidden, faces, near[offsets], far, own_grad, picks, w_two)
+    total = (jnp.sum(parts.astype(F32), 0) * half).astype(BF)
+    total, response, input_grad = lax.optimization_barrier((total, response, input_grad))
+
+    whole = swap(jnp.broadcast_to(total, (block, *total.shape)), BLOCK)
+    whole = whole.reshape(offsets + 1, channels, channels)
+    other = other_core(whole)
     first_is_mine = lax.axis_index("core") == 0
     first = jnp.where(first_is_mine, whole, other)[:offsets]
     second = jnp.where(first_is_mine, other, whole)[:offsets]
@@ -331,7 +332,8 @@
 def solution(mesh):
     groups, slabs = mesh.devices.shape
     side = {64: 4, 16: 2, 4: 1}[slabs]
-    fine = Mesh(mesh.devices.reshape(groups, side, side, 2, 2), AXES)
+    pair = 2 if groups % 2 == 0 else 1
+    fine = Mesh(mesh.devices.reshape(groups // pair, pair, side, side, 2, 2), AXES)
     rows, row = P(AXES, None), P(AXES)
     return jax.shard_map(
         on_device,

time: 130 us -> 119 us (0.915)
  the two profiles are of different devices: /device:TPU:9 before, /device:TPU:1 now
where the time goes in v5:
time: 119 us; the launch traced here: 118 us
  starting transfers between devices  48.7 us (41%)
  blocking collectives  27.4 us (23%)
  waiting for transfers between devices  22.5 us (19%)
  Pallas kernels  7.8 us (7%)
  local copies, waits for them, and re-layouts  6.16 us (5%)
  other arithmetic  3.94 us (3%)
  between operations  1.42 us (1%)
    ppermute x2, starting transfers between devices, far_slab(): return lax.ppermute(block, SLAB, pairs)  28 us
    all_to_all x1, blocking collectives, swap(): return lax.all_to_all(block, axis, 0, 0, tiled=True)  27.4 us
    all_to_all x2, waiting for transfers between devices, swap(): return lax.all_to_all(block, axis, 0, 0, tiled=True)  12.1 us
    all_to_all x2, starting transfers between devices, swap(): return lax.all_to_all(block, axis, 0, 0, tiled=True)  11.8 us
    ppermute x3, starting transfers between devices, other_core(): return lax.ppermute(block, 'core', [(0, 1), (1, 0)])  8.91 us
    ppermute x2, waiting for transfers between devices, far_slab(): return lax.ppermute(block, SLAB, pairs)  6.29 us
    unnamed x12, local copies, waits for them, and re-layouts  4.57 us
    ppermute x3, waiting for transfers between devices, other_core(): return lax.ppermute(block, 'core', [(0, 1), (1, 0)])  4.15 us
  transfers between devices with their start and end apart: 7, of which 5 were waited for; matrix products, arithmetic and copies ran while one was open for 2% of the time, Pallas kernels for 2%

profile of v5, /device:TPU:1, one launch (start us, length us, event | category | flops | bytes accessed | tf_op | source)
XLA Modules:
  0.0 117.9 jit_solution(17378658958084953973)
XLA Ops:
  1.3 1.7 %shard_map.111 = (bf16[192,128]{1,0:T(8,128)(2,1)}, bf16[192,128]{1,0:T(8,128)(2,1)}, f32[2,32]{1,0:T(2,128)}) custom-call(s32[1]{0:T(128)S(6)} %copy.12.counts, bf16[128,128]{1,0:T(8,128)(2,1)} %feat.1, bf16[128,128]{1,0:T(8,128)(2,1)} %cot_h.1, s32[27,128]{1,0:T(8,128)} %bitcast.10, s32[1,32]{1,0:T(1,128)} %bitcast.11, s32[1,32]{1,0:T(1,128)} %bitcast.12), custom_call_target="tpu_custom_call" | custom-call | bytes 3000000 | tf_op jit(solution)/shard_map/pallas_call | solution.py:294
  3.0 16.8 %collective-permute-start = (bf16[192,128]{1,0:T(8,128)(2,1)}, bf16[192,128]{1,0:T(8,128)(2,1)S(1)}, u32[]{:S(2)}, u32[]{:S(2)}) collective-permute-start(bf16[192,128]{1,0:T(8,128)(2,1)} %get-tuple-element.28.own), channel_id=1, source_target_pairs={{1,2},{2,1},{3,4},{4,3},{5,6},{6,5},{7,8},{8,7},{9,10},{10,9},{11,... | collective-permute-start | bytes 147464 | tf_op jit(solution)/shard_map/ppermute | solution.py:267
  19.8 1.9 %collective-permute-start.1 = (bf16[192,128]{1,0:T(8,128)(2,1)}, bf16[192,128]{1,0:T(8,128)(2,1)S(1)}, u32[]{:S(2)}, u32[]{:S(2)}) collective-permute-start(bf16[192,128]{1,0:T(8,128)(2,1)} %get-tuple-element.37), channel_id=1, source_target_pairs={{0,1},{1,0},{2,3},{3,2},{4,5},{5,4},{6,7},{7,6},{8,9},{9,8},{10,11... | collective-permute-start | bytes 147464 | tf_op jit(solution)/shard_map/ppermute | solution.py:275
  21.7 0.0 copy-start
  21.7 1.2 copy-done
  22.9 0.0 copy-start.1
  22.9 1.2 copy-done.1
  24.1 0.0 copy-start.2
  24.1 0.8 copy-done.2
  24.8 0.0 copy-start.3
  24.8 0.8 copy-done.3
  25.6 0.0 copy-start.4
  25.6 0.7 copy-done.4
  26.3 0.6 shard_map.112
  26.9 0.0 collective-permute-done.far
  26.9 0.0 collective-permute-done.1.near
  26.9 3.9 %shard_map.113 = (f32[64,128]{1,0:T(8,128)S(1)}, f32[128,128]{1,0:T(8,128)S(1)}, bf16[128,128]{1,0:T(8,128)(2,1)S(1)}, bf16[28,128,128]{2,1,0:T(8,128)(2,1)S(1)}, bf16[28,128,128]{2,1,0:T(8,128)(2,1)S(1)}) custom-call(s32[1]{0:T(128)S(6)} %copy.12.counts, bf16[128,128]{1,0:T(8,128)(2,1)S(1)} %get-tuple-element.30.masked, ...), custom_call_target="tpu_custom_call" | custom-call | bytes 15000000 | tf_op jit(solution)/shard_map/pallas_call | solution.py:303
  30.9 2.4 %collective-permute-start.2 = (bf16[28,128,128]{2,1,0:T(8,128)(2,1)S(1)}, bf16[28,128,128]{2,1,0:T(8,128)(2,1)S(1)}, u32[]{:S(2)}, u32[]{:S(2)}) collective-permute-start(bf16[28,128,128]{2,1,0:T(8,128)(2,1)S(1)} %get-tuple-element.39), channel_id=1, source_target_pairs={{0,1},{1,0},{2,3},{3,2},{4,5},{5,4},{6,7},{7,6},{8,9},{9,8},{10,11... | collective-permute-start | bytes 2752520 | tf_op jit(solution)/shard_map/ppermute | solution.py:275
  33.3 2.1 %collective-permute-done.2 = bf16[28,128,128]{2,1,0:T(8,128)(2,1)S(1)} collective-permute-done((bf16[28,128,128]{2,1,0:T(8,128)(2,1)S(1)}, bf16[28,128,128]{2,1,0:T(8,128)(2,1)S(1)}, u32[]{:S(2)}, u32[]{:S(2)}) %collective-permute-start.2) | collective-permute-done | bytes 917536 | tf_op jit(solution)/shard_map/ppermute | solution.py:275
  35.4 0.0 copy-start.5
  35.4 1.3 %add_convert_fusion = bf16[28,128,128]{2,1,0:T(8,128)(2,1)} fusion(bf16[28,128,128]{2,1,0:T(8,128)(2,1)S(1)} %collective-permute-done.2, bf16[28,128,128]{2,1,0:T(8,128)(2,1)S(1)} %get-tuple-element.38), kind=kLoop, calls=%fused_computation.1 | loop fusion | flops 1835008 | bytes 2752512 | tf_op jit(solution)/shard_map/convert_element_type | solution.py:310
  36.6 0.0 copy-done.5
  36.6 7.6 %all-to-all-start = ((bf16[32,112,128]{2,1,0:T(8,128)(2,1)}), bf16[32,112,128]{2,1,0:T(8,128)(2,1)}, u32[]{:S(2)}, u32[]{:S(2)}) async-start(bf16[32,112,128]{2,1,0:T(8,128)(2,1)} %bitcast.7), calls=%async_computation | async-start | bytes 1835008 | tf_op jit(solution)/shard_map/all_to_all | solution.py:271
  44.2 11.1 %collective-permute-start.3 = (f32[64,128]{1,0:T(8,128)S(1)}, f32[64,128]{1,0:T(8,128)S(1)}, u32[]{:S(2)}, u32[]{:S(2)}) collective-permute-start(f32[64,128]{1,0:T(8,128)S(1)} %get-tuple-element.42), channel_id=1, source_target_pairs={{1,2},{2,1},{3,4},{4,3},{5,6},{6,5},{7,8},{8,7},{9,10},{10,9},{11,... | collective-permute-start | bytes 98312 | tf_op jit(solution)/shard_map/ppermute | solution.py:267
  55.4 2.6 %all-to-all-done = bf16[32,112,128]{2,1,0:T(8,128)(2,1)} async-done(((bf16[32,112,128]{2,1,0:T(8,128)(2,1)}), bf16[32,112,128]{2,1,0:T(8,128)(2,1)}, u32[]{:S(2)}, u32[]{:S(2)}) %all-to-all-start) | async-done | bytes 917536 | tf_op jit(solution)/shard_map/all_to_all | solution.py:271
  58.0 1.3 %convert_reduce_fusion = f32[112,128]{1,0:T(8,128)S(1)} fusion(bf16[32,112,128]{2,1,0:T(8,128)(2,1)} %all-to-all-done), kind=kLoop, calls=%fused_computation | loop fusion | flops 903168 | bytes 974848 | tf_op jit(solution)/shard_map/reduce_sum | solution.py:314
  59.3 6.3 %collective-permute-done.3.far = f32[64,128]{1,0:T(8,128)S(1)} collective-permute-done((f32[64,128]{1,0:T(8,128)S(1)}, f32[64,128]{1,0:T(8,128)S(1)}, u32[]{:S(2)}, u32[]{:S(2)}) %collective-permute-start.3) | collective-permute-done | bytes 32800 | tf_op jit(solution)/shard_map/ppermute | solution.py:267
  65.6 0.7 broadcast_in_dim.6
  66.3 4.2 %all-to-all-start.1 = ((bf16[8,112,128]{2,1,0:T(8,128)(2,1)}), bf16[8,112,128]{2,1,0:T(8,128)(2,1)S(1)}, u32[]{:S(2)}, u32[]{:S(2)}) async-start(bf16[8,112,128]{2,1,0:T(8,128)(2,1)} %broadcast_in_dim.6), calls=%async_computation.1 | async-start | bytes 458752 | tf_op jit(solution)/shard_map/all_to_all | solution.py:271
  70.5 0.8 slice_bitcast_fusion.near
  71.3 1.6 %shard_map.114 = (bf16[128,128]{1,0:T(8,128)(2,1)}, bf16[128,128]{1,0:T(8,128)(2,1)}) custom-call(s32[1]{0:T(128)S(6)} %copy.12.counts, bf16[128,128]{1,0:T(8,128)(2,1)S(1)} %get-tuple-element.44.hidden, f32[2,32]{1,0:T(2,128)S(1)} %get-tuple-element.33.faces, bf16[128,128]{1,0:T(8,128)(2,1)S(1)} %slice_bitcast_fusion.near, ...), custom_call_target="tpu_custom_call" | custom-call | bytes 9000000 | tf_op jit(solution)/shard_map/pallas_call | solution.py:317
  72.9 9.5 %all-to-all-done.1 = bf16[8,112,128]{2,1,0:T(8,128)(2,1)S(1)} async-done(((bf16[8,112,128]{2,1,0:T(8,128)(2,1)}), bf16[8,112,128]{2,1,0:T(8,128)(2,1)S(1)}, u32[]{:S(2)}, u32[]{:S(2)}) %all-to-all-start.1) | async-done | bytes 229408 | tf_op jit(solution)/shard_map/all_to_all | solution.py:271
  82.4 0.1 broadcast_in_dim.7
  82.6 27.4 %all_to_all.15 = bf16[32,112,128]{2,1,0:T(8,128)(2,1)S(1)} all-to-all(bf16[32,112,128]{2,1,0:T(8,128)(2,1)S(1)} %broadcast_in_dim.7), channel_id=1, replica_groups=mesh['column'=4,'pair'=2,'y'=4,'x'=4,'zh'=2,'core'=2] {'pair','y','x'}, dimensions={0} | all-to-all | bytes 1835008 | tf_op jit(solution)/shard_map/all_to_all | solution.py:271
  110.0 4.6 %collective-permute-start.4 = (bf16[28,128,128]{2,1,0:T(8,128)(2,1)S(1)}, bf16[28,128,128]{2,1,0:T(8,128)(2,1)S(1)}, u32[]{:S(2)}, u32[]{:S(2)}) collective-permute-start(bf16[28,128,128]{2,1,0:T(8,128)(2,1)S(1)} %bitcast.8), channel_id=1, source_target_pairs={{0,1},{1,0},{2,3},{3,2},{4,5},{5,4},{6,7},{7,6},{8,9},{9,8},{10,11... | collective-permute-start | bytes 2752520 | tf_op jit(solution)/shard_map/ppermute | solution.py:275
  114.5 2.1 %collective-permute-done.4 = bf16[28,128,128]{2,1,0:T(8,128)(2,1)S(1)} collective-permute-done((bf16[28,128,128]{2,1,0:T(8,128)(2,1)S(1)}, bf16[28,128,128]{2,1,0:T(8,128)(2,1)S(1)}, u32[]{:S(2)}, u32[]{:S(2)}) %collective-permute-start.4) | collective-permute-done | bytes 917536 | tf_op jit(solution)/shard_map/ppermute | solution.py:275
  116.6 1.3 %broadcast_select_fusion = (bf16[27,128,128]{2,1,0:T(8,128)(2,1)}, bf16[27,128,128]{2,1,0:T(8,128)(2,1)}) fusion(pred[]{:T(512)S(6)} %eq.3, bf16[28,128,128]{2,1,0:T(8,128)(2,1)S(1)} %collective-permute-done.4, bf16[28,128,128]{2,1,0:T(8,128)(2,1)S(1)} %bitcast.9), kind=kLoop, calls=%fused_computation.2 | loop fusion | flops 884736 | bytes 3538945 | tf_op jit(solution)/shard_map/jit(_where)/select_n | solution.py:328
  (3 shorter events, 0.0 us)
Async XLA Ops:
  3.0 23.9 %collective-permute-start = (bf16[192,128]{1,0:T(8,128)(2,1)}, bf16[192,128]{1,0:T(8,128)(2,1)S(1)}, u32[]{:S(2)}, u32[]{:S(2)}) collective-permute-start(bf16[192,128]{1,0:T(8,128)(2,1)} %get-tuple-element.28.own), channel_id=1, source_target_pairs={{1,2},{2,1},{3,4},{4,3},{5,6},{6,5},{7,8},{8,7},{9,10},{10,9},{11,... | collective-permute-start | bytes 147464 | tf_op jit(solution)/shard_map/ppermute | solution.py:267
  19.8 7.1 %collective-permute-start.1 = (bf16[192,128]{1,0:T(8,128)(2,1)}, bf16[192,128]{1,0:T(8,128)(2,1)S(1)}, u32[]{:S(2)}, u32[]{:S(2)}) collective-permute-start(bf16[192,128]{1,0:T(8,128)(2,1)} %get-tuple-element.37), channel_id=1, source_target_pairs={{0,1},{1,0},{2,3},{3,2},{4,5},{5,4},{6,7},{7,6},{8,9},{9,8},{10,11... | collective-permute-start | bytes 147464 | tf_op jit(solution)/shard_map/ppermute | solution.py:275
  21.7 1.2 copy-start
  22.9 1.2 copy-start.1
  24.1 0.8 copy-start.2
  24.8 0.8 copy-start.3
  25.6 0.7 copy-start.4
  30.9 4.5 %collective-permute-start.2 = (bf16[28,128,128]{2,1,0:T(8,128)(2,1)S(1)}, bf16[28,128,128]{2,1,0:T(8,128)(2,1)S(1)}, u32[]{:S(2)}, u32[]{:S(2)}) collective-permute-start(bf16[28,128,128]{2,1,0:T(8,128)(2,1)S(1)} %get-tuple-element.39), channel_id=1, source_target_pairs={{0,1},{1,0},{2,3},{3,2},{4,5},{5,4},{6,7},{7,6},{8,9},{9,8},{10,11... | collective-permute-start | bytes 2752520 | tf_op jit(solution)/shard_map/ppermute | solution.py:275
  35.4 1.3 %copy-start.5 = (bf16[28,128,128]{2,1,0:T(8,128)(2,1)}, bf16[28,128,128]{2,1,0:T(8,128)(2,1)S(1)}, u32[]{:S(2)}) copy-start(bf16[28,128,128]{2,1,0:T(8,128)(2,1)S(1)} %collective-permute-done.2) | copy-start | bytes 2752516
  36.6 21.4 %all-to-all-start = ((bf16[32,112,128]{2,1,0:T(8,128)(2,1)}), bf16[32,112,128]{2,1,0:T(8,128)(2,1)}, u32[]{:S(2)}, u32[]{:S(2)}) async-start(bf16[32,112,128]{2,1,0:T(8,128)(2,1)} %bitcast.7), calls=%async_computation | async-start | bytes 1835008 | tf_op jit(solution)/shard_map/all_to_all | solution.py:271
  44.2 21.3 %collective-permute-start.3 = (f32[64,128]{1,0:T(8,128)S(1)}, f32[64,128]{1,0:T(8,128)S(1)}, u32[]{:S(2)}, u32[]{:S(2)}) collective-permute-start(f32[64,128]{1,0:T(8,128)S(1)} %get-tuple-element.42), channel_id=1, source_target_pairs={{1,2},{2,1},{3,4},{4,3},{5,6},{6,5},{7,8},{8,7},{9,10},{10,9},{11,... | collective-permute-start | bytes 98312 | tf_op jit(solution)/shard_map/ppermute | solution.py:267
  66.3 16.1 %all-to-all-start.1 = ((bf16[8,112,128]{2,1,0:T(8,128)(2,1)}), bf16[8,112,128]{2,1,0:T(8,128)(2,1)S(1)}, u32[]{:S(2)}, u32[]{:S(2)}) async-start(bf16[8,112,128]{2,1,0:T(8,128)(2,1)} %broadcast_in_dim.6), calls=%async_computation.1 | async-start | bytes 458752 | tf_op jit(solution)/shard_map/all_to_all | solution.py:271
  110.0 6.7 %collective-permute-start.4 = (bf16[28,128,128]{2,1,0:T(8,128)(2,1)S(1)}, bf16[28,128,128]{2,1,0:T(8,128)(2,1)S(1)}, u32[]{:S(2)}, u32[]{:S(2)}) collective-permute-start(bf16[28,128,128]{2,1,0:T(8,128)(2,1)S(1)} %bitcast.8), channel_id=1, source_target_pairs={{0,1},{1,0},{2,3},{3,2},{4,5},{5,4},{6,7},{7,6},{8,9},{9,8},{10,11... | collective-permute-start | bytes 2752520 | tf_op jit(solution)/shard_map/ppermute | solution.py:275

commit v6 on v5

--- a/solution.py
+++ b/solution.py
@@ -308,11 +308,10 @@
     column, block = lax.axis_size(COLUMN), lax.axis_size(BLOCK)
     near = other_core(theirs)
     share = (mine.astype(F32) + near.astype(F32)).astype(BF)
-    share, far_two = lax.optimization_barrier((share, far_two))
     parts = swap(share.reshape(block, -1, channels), BLOCK)
+    parts = (jnp.sum(parts.astype(F32), 0) * half).astype(BF)
+    parts, far_two = lax.optimization_barrier((parts, far_two))
     far = far_slab(far_two)
-    parts = (jnp.sum(parts.astype(F32), 0) * half).astype(BF)
-    parts, far = lax.optimization_barrier((parts, far))
     parts = swap(jnp.broadcast_to(parts, (column, *parts.shape)), COLUMN)
     response, input_grad = call(
         last_kernel, "svvvvvvv", (flat, flat), (broad,), 1, 3

time: 119 us -> 121 us (1.017)
  blocking collectives: 27.4 us -> 39.9 us
  waiting for transfers between devices: 22.5 us -> 11.3 us
  starting transfers between devices: 48.7 us -> 51.4 us
  other arithmetic: 3.94 us -> 1.88 us
    all_to_all x1 -> x2, blocking collectives: 27.4 us -> 39.9 us  [swap(): return lax.all_to_all(block, axis, 0, 0, tiled=True)]
    all_to_all x2 -> x1, waiting for transfers between devices: 12.1 us -> 0.01 us  [swap(): return lax.all_to_all(block, axis, 0, 0, tiled=True)]
    ppermute x2, starting transfers between devices: 28 us -> 31.5 us  [far_slab(): return lax.ppermute(block, SLAB, pairs)]
    all_to_all x2 -> x1, starting transfers between devices: 11.8 us -> 10.5 us  [swap(): return lax.all_to_all(block, axis, 0, 0, tiled=True)]
  transfers between devices with their start and end apart: 7 -> 6, of which waited for: 5 -> 3; matrix products, arithmetic and copies ran while one was open for 2% -> 1% of each run, Pallas kernels for 2% -> 2%
where the time goes in v6:
time: 121 us; the launch traced here: 120 us
  starting transfers between devices  51.4 us (42%)
  blocking collectives  39.9 us (33%)
  waiting for transfers between devices  11.3 us (9%)
  Pallas kernels  7.81 us (6%)
  local copies, waits for them, and re-layouts  6.17 us (5%)
  other arithmetic  1.88 us (2%)
  between operations  1.43 us (1%)
    all_to_all x2, blocking collectives, swap(): return lax.all_to_all(block, axis, 0, 0, tiled=True)  39.9 us
    ppermute x2, starting transfers between devices, far_slab(): return lax.ppermute(block, SLAB, pairs)  31.5 us
    all_to_all x1, starting transfers between devices, swap(): return lax.all_to_all(block, axis, 0, 0, tiled=True)  10.5 us
    ppermute x3, starting transfers between devices, other_core(): return lax.ppermute(block, 'core', [(0, 1), (1, 0)])  9.44 us
    ppermute x2, waiting for transfers between devices, far_slab(): return lax.ppermute(block, SLAB, pairs)  7.16 us
    unnamed x12, local copies, waits for them, and re-layouts  4.57 us
    ppermute x3, waiting for transfers between devices, other_core(): return lax.ppermute(block, 'core', [(0, 1), (1, 0)])  4.15 us
    pallas_call x1, Pallas kernels, on_device(): call(main_kernel, 'svvvvvvvvv', (ends, field, flat, sums, sums), (broad,...  3.96 us
  transfers between devices with their start and end apart: 6, of which 3 were waited for; matrix products, arithmetic and copies ran while one was open for 1% of the time, Pallas kernels for 2%

profile of v6, /device:TPU:1, one launch (start us, length us, event | category | flops | bytes accessed | tf_op | source)
XLA Modules:
  0.0 119.9 jit_solution(14426845713445515763)
XLA Ops:
  1.3 1.7 %shard_map.111 = (bf16[192,128]{1,0:T(8,128)(2,1)}, bf16[192,128]{1,0:T(8,128)(2,1)}, f32[2,32]{1,0:T(2,128)}) custom-call(s32[1]{0:T(128)S(6)} %copy.12.counts, bf16[128,128]{1,0:T(8,128)(2,1)} %feat.1, bf16[128,128]{1,0:T(8,128)(2,1)} %cot_h.1, s32[27,128]{1,0:T(8,128)} %bitcast.10, s32[1,32]{1,0:T(1,128)} %bitcast.11, s32[1,32]{1,0:T(1,128)} %bitcast.12), custom_call_target="tpu_custom_call" | custom-call | bytes 3000000 | tf_op jit(solution)/shard_map/pallas_call | solution.py:294
  3.0 16.8 %collective-permute-start = (bf16[192,128]{1,0:T(8,128)(2,1)}, bf16[192,128]{1,0:T(8,128)(2,1)S(1)}, u32[]{:S(2)}, u32[]{:S(2)}) collective-permute-start(bf16[192,128]{1,0:T(8,128)(2,1)} %get-tuple-element.26.own), channel_id=1, source_target_pairs={{1,2},{2,1},{3,4},{4,3},{5,6},{6,5},{7,8},{8,7},{9,10},{10,9},{11,... | collective-permute-start | bytes 147464 | tf_op jit(solution)/shard_map/ppermute | solution.py:267
  19.8 1.9 %collective-permute-start.1 = (bf16[192,128]{1,0:T(8,128)(2,1)}, bf16[192,128]{1,0:T(8,128)(2,1)S(1)}, u32[]{:S(2)}, u32[]{:S(2)}) collective-permute-start(bf16[192,128]{1,0:T(8,128)(2,1)} %get-tuple-element.35), channel_id=1, source_target_pairs={{0,1},{1,0},{2,3},{3,2},{4,5},{5,4},{6,7},{7,6},{8,9},{9,8},{10,11... | collective-permute-start | bytes 147464 | tf_op jit(solution)/shard_map/ppermute | solution.py:275
  21.7 0.0 copy-start
  21.7 1.2 copy-done
  22.9 0.0 copy-start.1
  22.9 1.2 copy-done.1
  24.1 0.0 copy-start.2
  24.1 0.8 copy-done.2
  24.8 0.0 copy-start.3
  24.8 0.8 copy-done.3
  25.6 0.0 copy-start.4
  25.6 0.7 copy-done.4
  26.3 0.6 shard_map.112
  26.9 0.0 collective-permute-done.far
  26.9 0.0 collective-permute-done.1.near
  26.9 4.0 %shard_map.113 = (f32[64,128]{1,0:T(8,128)S(1)}, f32[128,128]{1,0:T(8,128)S(1)}, bf16[128,128]{1,0:T(8,128)(2,1)S(1)}, bf16[28,128,128]{2,1,0:T(8,128)(2,1)S(1)}, bf16[28,128,128]{2,1,0:T(8,128)(2,1)S(1)}) custom-call(s32[1]{0:T(128)S(6)} %copy.12.counts, bf16[128,128]{1,0:T(8,128)(2,1)S(1)} %get-tuple-element.28.masked, ...), custom_call_target="tpu_custom_call" | custom-call | bytes 15000000 | tf_op jit(solution)/shard_map/pallas_call | solution.py:303
  30.9 2.4 %collective-permute-start.2 = (bf16[28,128,128]{2,1,0:T(8,128)(2,1)S(1)}, bf16[28,128,128]{2,1,0:T(8,128)(2,1)S(1)}, u32[]{:S(2)}, u32[]{:S(2)}) collective-permute-start(bf16[28,128,128]{2,1,0:T(8,128)(2,1)S(1)} %get-tuple-element.37), channel_id=1, source_target_pairs={{0,1},{1,0},{2,3},{3,2},{4,5},{5,4},{6,7},{7,6},{8,9},{9,8},{10,11... | collective-permute-start | bytes 2752520 | tf_op jit(solution)/shard_map/ppermute | solution.py:275
  33.3 2.1 %collective-permute-done.2 = bf16[28,128,128]{2,1,0:T(8,128)(2,1)S(1)} collective-permute-done((bf16[28,128,128]{2,1,0:T(8,128)(2,1)S(1)}, bf16[28,128,128]{2,1,0:T(8,128)(2,1)S(1)}, u32[]{:S(2)}, u32[]{:S(2)}) %collective-permute-start.2) | collective-permute-done | bytes 917536 | tf_op jit(solution)/shard_map/ppermute | solution.py:275
  35.4 0.0 copy-start.5
  35.4 0.4 add_convert_fusion
  35.8 21.0 %all_to_all.15 = bf16[32,112,128]{2,1,0:T(8,128)(2,1)S(1)} all-to-all(bf16[32,112,128]{2,1,0:T(8,128)(2,1)S(1)} %bitcast.7), channel_id=1, replica_groups=mesh['column'=4,'pair'=2,'y'=4,'x'=4,'zh'=2,'core'=2] {'pair','y','x'}, dimensions={0} | all-to-all | bytes 1835008 | tf_op jit(solution)/shard_map/all_to_all | solution.py:271
  56.8 0.0 copy-done.5
  56.8 0.1 convert_reduce_fusion
  57.0 0.7 broadcast_in_dim.6
  57.7 10.5 %all-to-all-start.1 = ((bf16[8,112,128]{2,1,0:T(8,128)(2,1)}), bf16[8,112,128]{2,1,0:T(8,128)(2,1)S(1)}, u32[]{:S(2)}, u32[]{:S(2)}) async-start(bf16[8,112,128]{2,1,0:T(8,128)(2,1)} %broadcast_in_dim.6), calls=%async_computation.1 | async-start | bytes 458752 | tf_op jit(solution)/shard_map/all_to_all | solution.py:271
  68.2 14.6 %collective-permute-start.3 = (f32[64,128]{1,0:T(8,128)S(1)}, f32[64,128]{1,0:T(8,128)S(1)}, u32[]{:S(2)}, u32[]{:S(2)}) collective-permute-start(f32[64,128]{1,0:T(8,128)S(1)} %get-tuple-element.41), channel_id=1, source_target_pairs={{1,2},{2,1},{3,4},{4,3},{5,6},{6,5},{7,8},{8,7},{9,10},{10,9},{11,... | collective-permute-start | bytes 98312 | tf_op jit(solution)/shard_map/ppermute | solution.py:267
  82.8 0.8 slice_bitcast_fusion.near
  83.6 7.2 %collective-permute-done.3.far = f32[64,128]{1,0:T(8,128)S(1)} collective-permute-done((f32[64,128]{1,0:T(8,128)S(1)}, f32[64,128]{1,0:T(8,128)S(1)}, u32[]{:S(2)}, u32[]{:S(2)}) %collective-permute-start.3) | collective-permute-done | bytes 32800 | tf_op jit(solution)/shard_map/ppermute | solution.py:267
  90.7 1.6 %shard_map.114 = (bf16[128,128]{1,0:T(8,128)(2,1)}, bf16[128,128]{1,0:T(8,128)(2,1)}) custom-call(s32[1]{0:T(128)S(6)} %copy.12.counts, bf16[128,128]{1,0:T(8,128)(2,1)S(1)} %get-tuple-element.40.hidden, f32[2,32]{1,0:T(2,128)S(1)} %get-tuple-element.31.faces, bf16[128,128]{1,0:T(8,128)(2,1)S(1)} %slice_bitcast_fusion.near, ...), custom_call_target="tpu_custom_call" | custom-call | bytes 9000000 | tf_op jit(solution)/shard_map/pallas_call | solution.py:316
  92.3 0.0 all-to-all-done.1
  92.4 0.1 broadcast_in_dim.7
  92.5 18.9 %all_to_all.16 = bf16[32,112,128]{2,1,0:T(8,128)(2,1)S(1)} all-to-all(bf16[32,112,128]{2,1,0:T(8,128)(2,1)S(1)} %broadcast_in_dim.7), channel_id=1, replica_groups=mesh['column'=4,'pair'=2,'y'=4,'x'=4,'zh'=2,'core'=2] {'pair','y','x'}, dimensions={0} | all-to-all | bytes 1835008 | tf_op jit(solution)/shard_map/all_to_all | solution.py:271
  111.4 5.1 %collective-permute-start.4 = (bf16[28,128,128]{2,1,0:T(8,128)(2,1)S(1)}, bf16[28,128,128]{2,1,0:T(8,128)(2,1)S(1)}, u32[]{:S(2)}, u32[]{:S(2)}) collective-permute-start(bf16[28,128,128]{2,1,0:T(8,128)(2,1)S(1)} %bitcast.8), channel_id=1, source_target_pairs={{0,1},{1,0},{2,3},{3,2},{4,5},{5,4},{6,7},{7,6},{8,9},{9,8},{10,11... | collective-permute-start | bytes 2752520 | tf_op jit(solution)/shard_map/ppermute | solution.py:275
  116.5 2.1 %collective-permute-done.4 = bf16[28,128,128]{2,1,0:T(8,128)(2,1)S(1)} collective-permute-done((bf16[28,128,128]{2,1,0:T(8,128)(2,1)S(1)}, bf16[28,128,128]{2,1,0:T(8,128)(2,1)S(1)}, u32[]{:S(2)}, u32[]{:S(2)}) %collective-permute-start.4) | collective-permute-done | bytes 917536 | tf_op jit(solution)/shard_map/ppermute | solution.py:275
  118.6 1.3 %broadcast_select_fusion = (bf16[27,128,128]{2,1,0:T(8,128)(2,1)}, bf16[27,128,128]{2,1,0:T(8,128)(2,1)}) fusion(pred[]{:T(512)S(6)} %eq.3, bf16[28,128,128]{2,1,0:T(8,128)(2,1)S(1)} %collective-permute-done.4, bf16[28,128,128]{2,1,0:T(8,128)(2,1)S(1)} %bitcast.9), kind=kLoop, calls=%fused_computation.2 | loop fusion | flops 884736 | bytes 3538945 | tf_op jit(solution)/shard_map/jit(_where)/select_n | solution.py:327
  (3 shorter events, 0.0 us)
Async XLA Ops:
  3.0 23.9 %collective-permute-start = (bf16[192,128]{1,0:T(8,128)(2,1)}, bf16[192,128]{1,0:T(8,128)(2,1)S(1)}, u32[]{:S(2)}, u32[]{:S(2)}) collective-permute-start(bf16[192,128]{1,0:T(8,128)(2,1)} %get-tuple-element.26.own), channel_id=1, source_target_pairs={{1,2},{2,1},{3,4},{4,3},{5,6},{6,5},{7,8},{8,7},{9,10},{10,9},{11,... | collective-permute-start | bytes 147464 | tf_op jit(solution)/shard_map/ppermute | solution.py:267
  19.8 7.1 %collective-permute-start.1 = (bf16[192,128]{1,0:T(8,128)(2,1)}, bf16[192,128]{1,0:T(8,128)(2,1)S(1)}, u32[]{:S(2)}, u32[]{:S(2)}) collective-permute-start(bf16[192,128]{1,0:T(8,128)(2,1)} %get-tuple-element.35), channel_id=1, source_target_pairs={{0,1},{1,0},{2,3},{3,2},{4,5},{5,4},{6,7},{7,6},{8,9},{9,8},{10,11... | collective-permute-start | bytes 147464 | tf_op jit(solution)/shard_map/ppermute | solution.py:275
  21.7 1.2 copy-start
  22.9 1.2 copy-start.1
  24.1 0.8 copy-start.2
  24.8 0.8 copy-start.3
  25.6 0.7 copy-start.4
  30.9 4.5 %collective-permute-start.2 = (bf16[28,128,128]{2,1,0:T(8,128)(2,1)S(1)}, bf16[28,128,128]{2,1,0:T(8,128)(2,1)S(1)}, u32[]{:S(2)}, u32[]{:S(2)}) collective-permute-start(bf16[28,128,128]{2,1,0:T(8,128)(2,1)S(1)} %get-tuple-element.37), channel_id=1, source_target_pairs={{0,1},{1,0},{2,3},{3,2},{4,5},{5,4},{6,7},{7,6},{8,9},{9,8},{10,11... | collective-permute-start | bytes 2752520 | tf_op jit(solution)/shard_map/ppermute | solution.py:275
  35.4 21.4 %copy-start.5 = (bf16[28,128,128]{2,1,0:T(8,128)(2,1)}, bf16[28,128,128]{2,1,0:T(8,128)(2,1)S(1)}, u32[]{:S(2)}) copy-start(bf16[28,128,128]{2,1,0:T(8,128)(2,1)S(1)} %collective-permute-done.2) | copy-start | bytes 2752516
  57.7 34.7 %all-to-all-start.1 = ((bf16[8,112,128]{2,1,0:T(8,128)(2,1)}), bf16[8,112,128]{2,1,0:T(8,128)(2,1)S(1)}, u32[]{:S(2)}, u32[]{:S(2)}) async-start(bf16[8,112,128]{2,1,0:T(8,128)(2,1)} %broadcast_in_dim.6), calls=%async_computation.1 | async-start | bytes 458752 | tf_op jit(solution)/shard_map/all_to_all | solution.py:271
  68.2 22.6 %collective-permute-start.3 = (f32[64,128]{1,0:T(8,128)S(1)}, f32[64,128]{1,0:T(8,128)S(1)}, u32[]{:S(2)}, u32[]{:S(2)}) collective-permute-start(f32[64,128]{1,0:T(8,128)S(1)} %get-tuple-element.41), channel_id=1, source_target_pairs={{1,2},{2,1},{3,4},{4,3},{5,6},{6,5},{7,8},{8,7},{9,10},{10,9},{11,... | collective-permute-start | bytes 98312 | tf_op jit(solution)/shard_map/ppermute | solution.py:267
  111.4 7.2 %collective-permute-start.4 = (bf16[28,128,128]{2,1,0:T(8,128)(2,1)S(1)}, bf16[28,128,128]{2,1,0:T(8,128)(2,1)S(1)}, u32[]{:S(2)}, u32[]{:S(2)}) collective-permute-start(bf16[28,128,128]{2,1,0:T(8,128)(2,1)S(1)} %bitcast.8), channel_id=1, source_target_pairs={{0,1},{1,0},{2,3},{3,2},{4,5},{5,4},{6,7},{7,6},{8,9},{9,8},{10,11... | collective-permute-start | bytes 2752520 | tf_op jit(solution)/shard_map/ppermute | solution.py:275

commit v7 on v6

--- a/solution.py
+++ b/solution.py
@@ -313,13 +313,14 @@
     parts, far_two = lax.optimization_barrier((parts, far_two))
     far = far_slab(far_two)
     parts = swap(jnp.broadcast_to(parts, (column, *parts.shape)), COLUMN)
+    total = (jnp.sum(parts.astype(F32), 0) * half).astype(BF)
+    total, far = lax.optimization_barrier((total, far))
     response, input_grad = call(
         last_kernel, "svvvvvvv", (flat, flat), (broad,), 1, 3
     )(counts, hidden, faces, near[offsets], far, own_grad, picks, w_two)
-    total = (jnp.sum(parts.astype(F32), 0) * half).astype(BF)
-    total, response, input_grad = lax.optimization_barrier((total, response, input_grad))
 
     whole = swap(jnp.broadcast_to(total, (block, *total.shape)), BLOCK)
+    whole, response, input_grad = lax.optimization_barrier((whole, response, input_grad))
     whole = whole.reshape(offsets + 1, channels, channels)
     other = other_core(whole)
     first_is_mine = lax.axis_index("core") == 0

time: 121 us -> 122 us (level)
  blocking collectives: 39.9 us -> 21 us
  waiting for transfers between devices: 11.3 us -> 23.1 us
  starting transfers between devices: 51.4 us -> 57.3 us
    all_to_all x2 -> x1, blocking collectives: 39.9 us -> 21 us  [swap(): return lax.all_to_all(block, axis, 0, 0, tiled=True)]
    all_to_all x1 -> x2, waiting for transfers between devices: 0.01 us -> 10.9 us  [swap(): return lax.all_to_all(block, axis, 0, 0, tiled=True)]
    all_to_all x1 -> x2, starting transfers between devices: 10.5 us -> 16.4 us  [swap(): return lax.all_to_all(block, axis, 0, 0, tiled=True)]
  transfers between devices with their start and end apart: 6 -> 7, of which waited for: 3 -> 4; matrix products, arithmetic and copies ran while one was open for 1% -> 1% of each run, Pallas kernels for 2% -> 2%
where the time goes in v7:
time: 122 us; the launch traced here: 121 us
  starting transfers between devices  57.3 us (47%)
  waiting for transfers between devices  23.1 us (19%)
  blocking collectives  21 us (17%)
  Pallas kernels  7.8 us (6%)
  local copies, waits for them, and re-layouts  7.1 us (6%)
  other arithmetic  3.05 us (2%)
  between operations  1.43 us (1%)
    ppermute x2, starting transfers between devices, far_slab(): return lax.ppermute(block, SLAB, pairs)  31.5 us
    all_to_all x1, blocking collectives, swap(): return lax.all_to_all(block, axis, 0, 0, tiled=True)  21 us
    all_to_all x2, starting transfers between devices, swap(): return lax.all_to_all(block, axis, 0, 0, tiled=True)  16.4 us
    all_to_all x2, waiting for transfers between devices, swap(): return lax.all_to_all(block, axis, 0, 0, tiled=True)  10.9 us
    ppermute x3, starting transfers between devices, other_core(): return lax.ppermute(block, 'core', [(0, 1), (1, 0)])  9.44 us
    ppermute x2, waiting for transfers between devices, far_slab(): return lax.ppermute(block, SLAB, pairs)  7.86 us
    unnamed x12, local copies, waits for them, and re-layouts  4.57 us
    ppermute x3, waiting for transfers between devices, other_core(): return lax.ppermute(block, 'core', [(0, 1), (1, 0)])  4.36 us
  transfers between devices with their start and end apart: 7, of which 4 were waited for; matrix products, arithmetic and copies ran while one was open for 1% of the time, Pallas kernels for 2%

profile of v7, /device:TPU:1, one launch (start us, length us, event | category | flops | bytes accessed | tf_op | source)
XLA Modules:
  0.0 120.8 jit_solution(12306764106689769310)
XLA Ops:
  1.3 1.7 %shard_map.111 = (bf16[192,128]{1,0:T(8,128)(2,1)}, bf16[192,128]{1,0:T(8,128)(2,1)}, f32[2,32]{1,0:T(2,128)}) custom-call(s32[1]{0:T(128)S(6)} %copy.12.counts, bf16[128,128]{1,0:T(8,128)(2,1)} %feat.1, bf16[128,128]{1,0:T(8,128)(2,1)} %cot_h.1, s32[27,128]{1,0:T(8,128)} %bitcast.8, s32[1,32]{1,0:T(1,128)} %bitcast.9, s32[1,32]{1,0:T(1,128)} %bitcast.10), custom_call_target="tpu_custom_call" | custom-call | bytes 3000000 | tf_op jit(solution)/shard_map/pallas_call | solution.py:294
  3.0 16.8 %collective-permute-start = (bf16[192,128]{1,0:T(8,128)(2,1)}, bf16[192,128]{1,0:T(8,128)(2,1)S(1)}, u32[]{:S(2)}, u32[]{:S(2)}) collective-permute-start(bf16[192,128]{1,0:T(8,128)(2,1)} %get-tuple-element.28.own), channel_id=1, source_target_pairs={{1,2},{2,1},{3,4},{4,3},{5,6},{6,5},{7,8},{8,7},{9,10},{10,9},{11,... | collective-permute-start | bytes 147464 | tf_op jit(solution)/shard_map/ppermute | solution.py:267
  19.8 1.9 %collective-permute-start.1 = (bf16[192,128]{1,0:T(8,128)(2,1)}, bf16[192,128]{1,0:T(8,128)(2,1)S(1)}, u32[]{:S(2)}, u32[]{:S(2)}) collective-permute-start(bf16[192,128]{1,0:T(8,128)(2,1)} %get-tuple-element.37), channel_id=1, source_target_pairs={{0,1},{1,0},{2,3},{3,2},{4,5},{5,4},{6,7},{7,6},{8,9},{9,8},{10,11... | collective-permute-start | bytes 147464 | tf_op jit(solution)/shard_map/ppermute | solution.py:275
  21.7 0.0 copy-start
  21.7 1.2 copy-done
  22.9 0.0 copy-start.1
  22.9 1.2 copy-done.1
  24.1 0.0 copy-start.2
  24.1 0.8 copy-done.2
  24.8 0.0 copy-start.3
  24.8 0.8 copy-done.3
  25.6 0.0 copy-start.4
  25.6 0.7 copy-done.4
  26.3 0.6 shard_map.112
  26.9 0.0 collective-permute-done.far
  26.9 0.0 collective-permute-done.1.near
  26.9 3.9 %shard_map.113 = (f32[64,128]{1,0:T(8,128)S(1)}, f32[128,128]{1,0:T(8,128)S(1)}, bf16[128,128]{1,0:T(8,128)(2,1)S(1)}, bf16[28,128,128]{2,1,0:T(8,128)(2,1)S(1)}, bf16[28,128,128]{2,1,0:T(8,128)(2,1)S(1)}) custom-call(s32[1]{0:T(128)S(6)} %copy.12.counts, bf16[128,128]{1,0:T(8,128)(2,1)S(1)} %get-tuple-element.30.masked, ...), custom_call_target="tpu_custom_call" | custom-call | bytes 15000000 | tf_op jit(solution)/shard_map/pallas_call | solution.py:303
  30.9 2.4 %collective-permute-start.2 = (bf16[28,128,128]{2,1,0:T(8,128)(2,1)S(1)}, bf16[28,128,128]{2,1,0:T(8,128)(2,1)S(1)}, u32[]{:S(2)}, u32[]{:S(2)}) collective-permute-start(bf16[28,128,128]{2,1,0:T(8,128)(2,1)S(1)} %get-tuple-element.39), channel_id=1, source_target_pairs={{0,1},{1,0},{2,3},{3,2},{4,5},{5,4},{6,7},{7,6},{8,9},{9,8},{10,11... | collective-permute-start | bytes 2752520 | tf_op jit(solution)/shard_map/ppermute | solution.py:275
  33.3 2.1 %collective-permute-done.2 = bf16[28,128,128]{2,1,0:T(8,128)(2,1)S(1)} collective-permute-done((bf16[28,128,128]{2,1,0:T(8,128)(2,1)S(1)}, bf16[28,128,128]{2,1,0:T(8,128)(2,1)S(1)}, u32[]{:S(2)}, u32[]{:S(2)}) %collective-permute-start.2) | collective-permute-done | bytes 917536 | tf_op jit(solution)/shard_map/ppermute | solution.py:275
  35.4 0.0 copy-start.5
  35.4 0.4 add_convert_fusion
  35.8 21.0 %all_to_all.15 = bf16[32,112,128]{2,1,0:T(8,128)(2,1)S(1)} all-to-all(bf16[32,112,128]{2,1,0:T(8,128)(2,1)S(1)} %bitcast.7), channel_id=1, replica_groups=mesh['column'=4,'pair'=2,'y'=4,'x'=4,'zh'=2,'core'=2] {'pair','y','x'}, dimensions={0} | all-to-all | bytes 1835008 | tf_op jit(solution)/shard_map/all_to_all | solution.py:271
  56.8 0.0 copy-done.5
  56.8 0.1 convert_reduce_fusion
  56.9 0.7 broadcast_in_dim.6
  57.7 10.5 %all-to-all-start.1 = ((bf16[8,112,128]{2,1,0:T(8,128)(2,1)}), bf16[8,112,128]{2,1,0:T(8,128)(2,1)S(1)}, u32[]{:S(2)}, u32[]{:S(2)}) async-start(bf16[8,112,128]{2,1,0:T(8,128)(2,1)} %broadcast_in_dim.6), calls=%async_computation.1 | async-start | bytes 458752 | tf_op jit(solution)/shard_map/all_to_all | solution.py:271
  68.2 14.6 %collective-permute-start.3 = (f32[64,128]{1,0:T(8,128)S(1)}, f32[64,128]{1,0:T(8,128)S(1)}, u32[]{:S(2)}, u32[]{:S(2)}) collective-permute-start(f32[64,128]{1,0:T(8,128)S(1)} %get-tuple-element.42), channel_id=1, source_target_pairs={{1,2},{2,1},{3,4},{4,3},{5,6},{6,5},{7,8},{8,7},{9,10},{10,9},{11,... | collective-permute-start | bytes 98312 | tf_op jit(solution)/shard_map/ppermute | solution.py:267
  82.8 0.0 all-to-all-done.1
  82.9 7.9 %collective-permute-done.3.far = f32[64,128]{1,0:T(8,128)S(1)} collective-permute-done((f32[64,128]{1,0:T(8,128)S(1)}, f32[64,128]{1,0:T(8,128)S(1)}, u32[]{:S(2)}, u32[]{:S(2)}) %collective-permute-start.3) | collective-permute-done | bytes 32800 | tf_op jit(solution)/shard_map/ppermute | solution.py:267
  90.7 1.1 broadcast_in_dim.7
  91.8 5.9 %all-to-all-start.2 = ((bf16[32,112,128]{2,1,0:T(8,128)(2,1)}), bf16[32,112,128]{2,1,0:T(8,128)(2,1)}, u32[]{:S(2)}, u32[]{:S(2)}) async-start(bf16[32,112,128]{2,1,0:T(8,128)(2,1)} %broadcast_in_dim.7), calls=%async_computation.2 | async-start | bytes 1835008 | tf_op jit(solution)/shard_map/all_to_all | solution.py:271
  97.7 0.8 slice_bitcast_fusion.near
  98.4 1.6 %shard_map.114 = (bf16[128,128]{1,0:T(8,128)(2,1)}, bf16[128,128]{1,0:T(8,128)(2,1)}) custom-call(s32[1]{0:T(128)S(6)} %copy.12.counts, bf16[128,128]{1,0:T(8,128)(2,1)S(1)} %get-tuple-element.44.hidden, f32[2,32]{1,0:T(2,128)S(1)} %get-tuple-element.33.faces, bf16[128,128]{1,0:T(8,128)(2,1)S(1)} %slice_bitcast_fusion.near, ...), custom_call_target="tpu_custom_call" | custom-call | bytes 9000000 | tf_op jit(solution)/shard_map/pallas_call | solution.py:318
  100.0 10.9 %all-to-all-done.2 = bf16[32,112,128]{2,1,0:T(8,128)(2,1)} async-done(((bf16[32,112,128]{2,1,0:T(8,128)(2,1)}), bf16[32,112,128]{2,1,0:T(8,128)(2,1)}, u32[]{:S(2)}, u32[]{:S(2)}) %all-to-all-start.2) | async-done | bytes 917536 | tf_op jit(solution)/shard_map/all_to_all | solution.py:271
  110.9 5.1 %collective-permute-start.4 = (bf16[28,128,128]{2,1,0:T(8,128)(2,1)}, bf16[28,128,128]{2,1,0:T(8,128)(2,1)S(1)}, u32[]{:S(2)}, u32[]{:S(2)}) collective-permute-start(bf16[28,128,128]{2,1,0:T(8,128)(2,1)} %bitcast.5), channel_id=1, source_target_pairs={{0,1},{1,0},{2,3},{3,2},{4,5},{5,4},{6,7},{7,6},{8,9},{9,8},{10,11... | collective-permute-start | bytes 2752520 | tf_op jit(solution)/shard_map/ppermute | solution.py:275
  116.1 2.3 %collective-permute-done.4 = bf16[28,128,128]{2,1,0:T(8,128)(2,1)S(1)} collective-permute-done((bf16[28,128,128]{2,1,0:T(8,128)(2,1)}, bf16[28,128,128]{2,1,0:T(8,128)(2,1)S(1)}, u32[]{:S(2)}, u32[]{:S(2)}) %collective-permute-start.4) | collective-permute-done | bytes 917536 | tf_op jit(solution)/shard_map/ppermute | solution.py:275
  118.3 2.5 %broadcast_select_fusion = (bf16[27,128,128]{2,1,0:T(8,128)(2,1)}, bf16[27,128,128]{2,1,0:T(8,128)(2,1)}) fusion(pred[]{:T(512)S(6)} %eq.3, bf16[28,128,128]{2,1,0:T(8,128)(2,1)S(1)} %collective-permute-done.4, bf16[28,128,128]{2,1,0:T(8,128)(2,1)} %bitcast.5), kind=kLoop, calls=%fused_computation.2 | loop fusion | flops 884736 | bytes 3538945 | tf_op jit(solution)/shard_map/jit(_where)/select_n | solution.py:328
  (3 shorter events, 0.0 us)
Async XLA Ops:
  3.0 23.9 %collective-permute-start = (bf16[192,128]{1,0:T(8,128)(2,1)}, bf16[192,128]{1,0:T(8,128)(2,1)S(1)}, u32[]{:S(2)}, u32[]{:S(2)}) collective-permute-start(bf16[192,128]{1,0:T(8,128)(2,1)} %get-tuple-element.28.own), channel_id=1, source_target_pairs={{1,2},{2,1},{3,4},{4,3},{5,6},{6,5},{7,8},{8,7},{9,10},{10,9},{11,... | collective-permute-start | bytes 147464 | tf_op jit(solution)/shard_map/ppermute | solution.py:267
  19.8 7.1 %collective-permute-start.1 = (bf16[192,128]{1,0:T(8,128)(2,1)}, bf16[192,128]{1,0:T(8,128)(2,1)S(1)}, u32[]{:S(2)}, u32[]{:S(2)}) collective-permute-start(bf16[192,128]{1,0:T(8,128)(2,1)} %get-tuple-element.37), channel_id=1, source_target_pairs={{0,1},{1,0},{2,3},{3,2},{4,5},{5,4},{6,7},{7,6},{8,9},{9,8},{10,11... | collective-permute-start | bytes 147464 | tf_op jit(solution)/shard_map/ppermute | solution.py:275
  21.7 1.2 copy-start
  22.9 1.2 copy-start.1
  24.1 0.8 copy-start.2
  24.8 0.8 copy-start.3
  25.6 0.7 copy-start.4
  30.9 4.5 %collective-permute-start.2 = (bf16[28,128,128]{2,1,0:T(8,128)(2,1)S(1)}, bf16[28,128,128]{2,1,0:T(8,128)(2,1)S(1)}, u32[]{:S(2)}, u32[]{:S(2)}) collective-permute-start(bf16[28,128,128]{2,1,0:T(8,128)(2,1)S(1)} %get-tuple-element.39), channel_id=1, source_target_pairs={{0,1},{1,0},{2,3},{3,2},{4,5},{5,4},{6,7},{7,6},{8,9},{9,8},{10,11... | collective-permute-start | bytes 2752520 | tf_op jit(solution)/shard_map/ppermute | solution.py:275
  35.4 21.4 %copy-start.5 = (bf16[28,128,128]{2,1,0:T(8,128)(2,1)}, bf16[28,128,128]{2,1,0:T(8,128)(2,1)S(1)}, u32[]{:S(2)}) copy-start(bf16[28,128,128]{2,1,0:T(8,128)(2,1)S(1)} %collective-permute-done.2) | copy-start | bytes 2752516
  57.7 25.1 %all-to-all-start.1 = ((bf16[8,112,128]{2,1,0:T(8,128)(2,1)}), bf16[8,112,128]{2,1,0:T(8,128)(2,1)S(1)}, u32[]{:S(2)}, u32[]{:S(2)}) async-start(bf16[8,112,128]{2,1,0:T(8,128)(2,1)} %broadcast_in_dim.6), calls=%async_computation.1 | async-start | bytes 458752 | tf_op jit(solution)/shard_map/all_to_all | solution.py:271
  68.2 22.6 %collective-permute-start.3 = (f32[64,128]{1,0:T(8,128)S(1)}, f32[64,128]{1,0:T(8,128)S(1)}, u32[]{:S(2)}, u32[]{:S(2)}) collective-permute-start(f32[64,128]{1,0:T(8,128)S(1)} %get-tuple-element.42), channel_id=1, source_target_pairs={{1,2},{2,1},{3,4},{4,3},{5,6},{6,5},{7,8},{8,7},{9,10},{10,9},{11,... | collective-permute-start | bytes 98312 | tf_op jit(solution)/shard_map/ppermute | solution.py:267
  91.8 19.2 %all-to-all-start.2 = ((bf16[32,112,128]{2,1,0:T(8,128)(2,1)}), bf16[32,112,128]{2,1,0:T(8,128)(2,1)}, u32[]{:S(2)}, u32[]{:S(2)}) async-start(bf16[32,112,128]{2,1,0:T(8,128)(2,1)} %broadcast_in_dim.7), calls=%async_computation.2 | async-start | bytes 1835008 | tf_op jit(solution)/shard_map/all_to_all | solution.py:271
  110.9 7.4 %collective-permute-start.4 = (bf16[28,128,128]{2,1,0:T(8,128)(2,1)}, bf16[28,128,128]{2,1,0:T(8,128)(2,1)S(1)}, u32[]{:S(2)}, u32[]{:S(2)}) collective-permute-start(bf16[28,128,128]{2,1,0:T(8,128)(2,1)} %bitcast.5), channel_id=1, source_target_pairs={{0,1},{1,0},{2,3},{3,2},{4,5},{5,4},{6,7},{7,6},{8,9},{9,8},{10,11... | collective-permute-start | bytes 2752520 | tf_op jit(solution)/shard_map/ppermute | solution.py:275

commit v8 on v6

--- a/solution.py
+++ b/solution.py
@@ -307,11 +307,11 @@
 
     column, block = lax.axis_size(COLUMN), lax.axis_size(BLOCK)
     near = other_core(theirs)
+    far = far_slab(far_two)
     share = (mine.astype(F32) + near.astype(F32)).astype(BF)
+    far, share = lax.optimization_barrier((far, share))
     parts = swap(share.reshape(block, -1, channels), BLOCK)
     parts = (jnp.sum(parts.astype(F32), 0) * half).astype(BF)
-    parts, far_two = lax.optimization_barrier((parts, far_two))
-    far = far_slab(far_two)
     parts = swap(jnp.broadcast_to(parts, (column, *parts.shape)), COLUMN)
     response, input_grad = call(
         last_kernel, "svvvvvvv", (flat, flat), (broad,), 1, 3

time: 121 us -> 127 us (1.050)
  waiting for transfers between devices: 11.3 us -> 15.5 us
  blocking collectives: 39.9 us -> 42.6 us
    all_to_all x1, waiting for transfers between devices: 0.01 us -> 9.7 us  [swap(): return lax.all_to_all(block, axis, 0, 0, tiled=True)]
    ppermute x2, starting transfers between devices: 31.5 us -> 26.7 us  [far_slab(): return lax.ppermute(block, SLAB, pairs)]
    all_to_all x1, starting transfers between devices: 10.5 us -> 14.3 us  [swap(): return lax.all_to_all(block, axis, 0, 0, tiled=True)]
    ppermute x2, waiting for transfers between devices: 7.16 us -> 3.73 us  [far_slab(): return lax.ppermute(block, SLAB, pairs)]
    all_to_all x2, blocking collectives: 39.9 us -> 42.6 us  [swap(): return lax.all_to_all(block, axis, 0, 0, tiled=True)]
    ppermute x3, waiting for transfers between devices: 4.15 us -> 2.08 us  [other_core(): return lax.ppermute(block, 'core', [(0, 1), (1, 0)])]
where the time goes in v8:
time: 127 us; the launch traced here: 126 us
  starting transfers between devices  50.6 us (40%)
  blocking collectives  42.6 us (34%)
  waiting for transfers between devices  15.5 us (12%)
  Pallas kernels  7.8 us (6%)
  local copies, waits for them, and re-layouts  6.17 us (5%)
  other arithmetic  1.89 us (1%)
  between operations  1.43 us (1%)
    all_to_all x2, blocking collectives, swap(): return lax.all_to_all(block, axis, 0, 0, tiled=True)  42.6 us
    ppermute x2, starting transfers between devices, far_slab(): return lax.ppermute(block, SLAB, pairs)  26.7 us
    all_to_all x1, starting transfers between devices, swap(): return lax.all_to_all(block, axis, 0, 0, tiled=True)  14.3 us
    all_to_all x1, waiting for transfers between devices, swap(): return lax.all_to_all(block, axis, 0, 0, tiled=True)  9.7 us
    ppermute x3, starting transfers between devices, other_core(): return lax.ppermute(block, 'core', [(0, 1), (1, 0)])  9.58 us
    unnamed x12, local copies, waits for them, and re-layouts  4.57 us
    pallas_call x1, Pallas kernels, on_device(): call(main_kernel, 'svvvvvvvvv', (ends, field, flat, sums, sums), (broad,...  3.95 us
    ppermute x2, waiting for transfers between devices, far_slab(): return lax.ppermute(block, SLAB, pairs)  3.73 us
  transfers between devices with their start and end apart: 6, of which 3 were waited for; matrix products, arithmetic and copies ran while one was open for 1% of the time, Pallas kernels for 2%

profile of v8, /device:TPU:1, one launch (start us, length us, event | category | flops | bytes accessed | tf_op | source)
XLA Modules:
  0.0 126.0 jit_solution(452796320964481448)
XLA Ops:
  1.3 1.7 %shard_map.111 = (bf16[192,128]{1,0:T(8,128)(2,1)}, bf16[192,128]{1,0:T(8,128)(2,1)}, f32[2,32]{1,0:T(2,128)}) custom-call(s32[1]{0:T(128)S(6)} %copy.12.counts, bf16[128,128]{1,0:T(8,128)(2,1)} %feat.1, bf16[128,128]{1,0:T(8,128)(2,1)} %cot_h.1, s32[27,128]{1,0:T(8,128)} %bitcast.10, s32[1,32]{1,0:T(1,128)} %bitcast.11, s32[1,32]{1,0:T(1,128)} %bitcast.12), custom_call_target="tpu_custom_call" | custom-call | bytes 3000000 | tf_op jit(solution)/shard_map/pallas_call | solution.py:294
  3.0 16.8 %collective-permute-start = (bf16[192,128]{1,0:T(8,128)(2,1)}, bf16[192,128]{1,0:T(8,128)(2,1)S(1)}, u32[]{:S(2)}, u32[]{:S(2)}) collective-permute-start(bf16[192,128]{1,0:T(8,128)(2,1)} %get-tuple-element.26.own), channel_id=1, source_target_pairs={{1,2},{2,1},{3,4},{4,3},{5,6},{6,5},{7,8},{8,7},{9,10},{10,9},{11,... | collective-permute-start | bytes 147464 | tf_op jit(solution)/shard_map/ppermute | solution.py:267
  19.8 1.9 %collective-permute-start.1 = (bf16[192,128]{1,0:T(8,128)(2,1)}, bf16[192,128]{1,0:T(8,128)(2,1)S(1)}, u32[]{:S(2)}, u32[]{:S(2)}) collective-permute-start(bf16[192,128]{1,0:T(8,128)(2,1)} %get-tuple-element.35), channel_id=1, source_target_pairs={{0,1},{1,0},{2,3},{3,2},{4,5},{5,4},{6,7},{7,6},{8,9},{9,8},{10,11... | collective-permute-start | bytes 147464 | tf_op jit(solution)/shard_map/ppermute | solution.py:275
  21.7 0.0 copy-start
  21.7 1.2 copy-done
  22.9 0.0 copy-start.1
  22.9 1.2 copy-done.1
  24.1 0.0 copy-start.2
  24.1 0.8 copy-done.2
  24.8 0.0 copy-start.3
  24.8 0.8 copy-done.3
  25.6 0.0 copy-start.4
  25.6 0.7 copy-done.4
  26.3 0.6 shard_map.112
  26.9 0.0 collective-permute-done.far
  26.9 0.0 collective-permute-done.1.near
  26.9 3.9 %shard_map.113 = (f32[64,128]{1,0:T(8,128)S(1)}, f32[128,128]{1,0:T(8,128)S(1)}, bf16[128,128]{1,0:T(8,128)(2,1)S(1)}, bf16[28,128,128]{2,1,0:T(8,128)(2,1)S(1)}, bf16[28,128,128]{2,1,0:T(8,128)(2,1)S(1)}) custom-call(s32[1]{0:T(128)S(6)} %copy.12.counts, bf16[128,128]{1,0:T(8,128)(2,1)S(1)} %get-tuple-element.28.masked, ...), custom_call_target="tpu_custom_call" | custom-call | bytes 15000000 | tf_op jit(solution)/shard_map/pallas_call | solution.py:303
  30.9 2.4 %collective-permute-start.3 = (bf16[28,128,128]{2,1,0:T(8,128)(2,1)S(1)}, bf16[28,128,128]{2,1,0:T(8,128)(2,1)S(1)}, u32[]{:S(2)}, u32[]{:S(2)}) collective-permute-start(bf16[28,128,128]{2,1,0:T(8,128)(2,1)S(1)} %get-tuple-element.38), channel_id=1, source_target_pairs={{0,1},{1,0},{2,3},{3,2},{4,5},{5,4},{6,7},{7,6},{8,9},{9,8},{10,11... | collective-permute-start | bytes 2752520 | tf_op jit(solution)/shard_map/ppermute | solution.py:275
  33.3 9.9 %collective-permute-start.2 = (f32[64,128]{1,0:T(8,128)S(1)}, f32[64,128]{1,0:T(8,128)S(1)}, u32[]{:S(2)}, u32[]{:S(2)}) collective-permute-start(f32[64,128]{1,0:T(8,128)S(1)} %get-tuple-element.36), channel_id=1, source_target_pairs={{1,2},{2,1},{3,4},{4,3},{5,6},{6,5},{7,8},{8,7},{9,10},{10,9},{11,... | collective-permute-start | bytes 98312 | tf_op jit(solution)/shard_map/ppermute | solution.py:267
  43.2 0.0 collective-permute-done.3
  43.2 0.0 copy-start.5
  43.2 0.4 add_convert_fusion
  43.6 3.7 %collective-permute-done.2.far = f32[64,128]{1,0:T(8,128)S(1)} collective-permute-done((f32[64,128]{1,0:T(8,128)S(1)}, f32[64,128]{1,0:T(8,128)S(1)}, u32[]{:S(2)}, u32[]{:S(2)}) %collective-permute-start.2) | collective-permute-done | bytes 32800 | tf_op jit(solution)/shard_map/ppermute | solution.py:267
  47.3 20.2 %all_to_all.15 = bf16[32,112,128]{2,1,0:T(8,128)(2,1)S(1)} all-to-all(bf16[32,112,128]{2,1,0:T(8,128)(2,1)S(1)} %bitcast.7), channel_id=1, replica_groups=mesh['column'=4,'pair'=2,'y'=4,'x'=4,'zh'=2,'core'=2] {'pair','y','x'}, dimensions={0} | all-to-all | bytes 1835008 | tf_op jit(solution)/shard_map/all_to_all | solution.py:271
  67.5 0.0 copy-done.5
  67.5 0.1 convert_reduce_fusion
  67.6 0.7 broadcast_in_dim.6
  68.3 14.3 %all-to-all-start.1 = ((bf16[8,112,128]{2,1,0:T(8,128)(2,1)}), bf16[8,112,128]{2,1,0:T(8,128)(2,1)S(1)}, u32[]{:S(2)}, u32[]{:S(2)}) async-start(bf16[8,112,128]{2,1,0:T(8,128)(2,1)} %broadcast_in_dim.6), calls=%async_computation.1 | async-start | bytes 458752 | tf_op jit(solution)/shard_map/all_to_all | solution.py:271
  82.6 0.8 slice_bitcast_fusion.near
  83.4 1.6 %shard_map.114 = (bf16[128,128]{1,0:T(8,128)(2,1)}, bf16[128,128]{1,0:T(8,128)(2,1)}) custom-call(s32[1]{0:T(128)S(6)} %copy.12.counts, bf16[128,128]{1,0:T(8,128)(2,1)S(1)} %get-tuple-element.40.hidden, f32[2,32]{1,0:T(2,128)S(1)} %get-tuple-element.31.faces, bf16[128,128]{1,0:T(8,128)(2,1)S(1)} %slice_bitcast_fusion.near, ...), custom_call_target="tpu_custom_call" | custom-call | bytes 9000000 | tf_op jit(solution)/shard_map/pallas_call | solution.py:316
  85.0 9.7 %all-to-all-done.1 = bf16[8,112,128]{2,1,0:T(8,128)(2,1)S(1)} async-done(((bf16[8,112,128]{2,1,0:T(8,128)(2,1)}), bf16[8,112,128]{2,1,0:T(8,128)(2,1)S(1)}, u32[]{:S(2)}, u32[]{:S(2)}) %all-to-all-start.1) | async-done | bytes 229408 | tf_op jit(solution)/shard_map/all_to_all | solution.py:271
  94.7 0.1 broadcast_in_dim.7
  94.8 22.5 %all_to_all.16 = bf16[32,112,128]{2,1,0:T(8,128)(2,1)S(1)} all-to-all(bf16[32,112,128]{2,1,0:T(8,128)(2,1)S(1)} %broadcast_in_dim.7), channel_id=1, replica_groups=mesh['column'=4,'pair'=2,'y'=4,'x'=4,'zh'=2,'core'=2] {'pair','y','x'}, dimensions={0} | all-to-all | bytes 1835008 | tf_op jit(solution)/shard_map/all_to_all | solution.py:271
  117.3 5.3 %collective-permute-start.4 = (bf16[28,128,128]{2,1,0:T(8,128)(2,1)S(1)}, bf16[28,128,128]{2,1,0:T(8,128)(2,1)S(1)}, u32[]{:S(2)}, u32[]{:S(2)}) collective-permute-start(bf16[28,128,128]{2,1,0:T(8,128)(2,1)S(1)} %bitcast.8), channel_id=1, source_target_pairs={{0,1},{1,0},{2,3},{3,2},{4,5},{5,4},{6,7},{7,6},{8,9},{9,8},{10,11... | collective-permute-start | bytes 2752520 | tf_op jit(solution)/shard_map/ppermute | solution.py:275
  122.6 2.1 %collective-permute-done.4 = bf16[28,128,128]{2,1,0:T(8,128)(2,1)S(1)} collective-permute-done((bf16[28,128,128]{2,1,0:T(8,128)(2,1)S(1)}, bf16[28,128,128]{2,1,0:T(8,128)(2,1)S(1)}, u32[]{:S(2)}, u32[]{:S(2)}) %collective-permute-start.4) | collective-permute-done | bytes 917536 | tf_op jit(solution)/shard_map/ppermute | solution.py:275
  124.7 1.3 %broadcast_select_fusion = (bf16[27,128,128]{2,1,0:T(8,128)(2,1)}, bf16[27,128,128]{2,1,0:T(8,128)(2,1)}) fusion(pred[]{:T(512)S(6)} %eq.3, bf16[28,128,128]{2,1,0:T(8,128)(2,1)S(1)} %collective-permute-done.4, bf16[28,128,128]{2,1,0:T(8,128)(2,1)S(1)} %bitcast.9), kind=kLoop, calls=%fused_computation.2 | loop fusion | flops 884736 | bytes 3538945 | tf_op jit(solution)/shard_map/jit(_where)/select_n | solution.py:327
  (3 shorter events, 0.0 us)
Async XLA Ops:
  3.0 23.9 %collective-permute-start = (bf16[192,128]{1,0:T(8,128)(2,1)}, bf16[192,128]{1,0:T(8,128)(2,1)S(1)}, u32[]{:S(2)}, u32[]{:S(2)}) collective-permute-start(bf16[192,128]{1,0:T(8,128)(2,1)} %get-tuple-element.26.own), channel_id=1, source_target_pairs={{1,2},{2,1},{3,4},{4,3},{5,6},{6,5},{7,8},{8,7},{9,10},{10,9},{11,... | collective-permute-start | bytes 147464 | tf_op jit(solution)/shard_map/ppermute | solution.py:267
  19.8 7.1 %collective-permute-start.1 = (bf16[192,128]{1,0:T(8,128)(2,1)}, bf16[192,128]{1,0:T(8,128)(2,1)S(1)}, u32[]{:S(2)}, u32[]{:S(2)}) collective-permute-start(bf16[192,128]{1,0:T(8,128)(2,1)} %get-tuple-element.35), channel_id=1, source_target_pairs={{0,1},{1,0},{2,3},{3,2},{4,5},{5,4},{6,7},{7,6},{8,9},{9,8},{10,11... | collective-permute-start | bytes 147464 | tf_op jit(solution)/shard_map/ppermute | solution.py:275
  21.7 1.2 copy-start
  22.9 1.2 copy-start.1
  24.1 0.8 copy-start.2
  24.8 0.8 copy-start.3
  25.6 0.7 copy-start.4
  30.9 12.3 %collective-permute-start.3 = (bf16[28,128,128]{2,1,0:T(8,128)(2,1)S(1)}, bf16[28,128,128]{2,1,0:T(8,128)(2,1)S(1)}, u32[]{:S(2)}, u32[]{:S(2)}) collective-permute-start(bf16[28,128,128]{2,1,0:T(8,128)(2,1)S(1)} %get-tuple-element.38), channel_id=1, source_target_pairs={{0,1},{1,0},{2,3},{3,2},{4,5},{5,4},{6,7},{7,6},{8,9},{9,8},{10,11... | collective-permute-start | bytes 2752520 | tf_op jit(solution)/shard_map/ppermute | solution.py:275
  33.3 14.0 %collective-permute-start.2 = (f32[64,128]{1,0:T(8,128)S(1)}, f32[64,128]{1,0:T(8,128)S(1)}, u32[]{:S(2)}, u32[]{:S(2)}) collective-permute-start(f32[64,128]{1,0:T(8,128)S(1)} %get-tuple-element.36), channel_id=1, source_target_pairs={{1,2},{2,1},{3,4},{4,3},{5,6},{6,5},{7,8},{8,7},{9,10},{10,9},{11,... | collective-permute-start | bytes 98312 | tf_op jit(solution)/shard_map/ppermute | solution.py:267
  43.2 24.3 %copy-start.5 = (bf16[28,128,128]{2,1,0:T(8,128)(2,1)}, bf16[28,128,128]{2,1,0:T(8,128)(2,1)S(1)}, u32[]{:S(2)}) copy-start(bf16[28,128,128]{2,1,0:T(8,128)(2,1)S(1)} %collective-permute-done.3) | copy-start | bytes 2752516
  68.3 26.3 %all-to-all-start.1 = ((bf16[8,112,128]{2,1,0:T(8,128)(2,1)}), bf16[8,112,128]{2,1,0:T(8,128)(2,1)S(1)}, u32[]{:S(2)}, u32[]{:S(2)}) async-start(bf16[8,112,128]{2,1,0:T(8,128)(2,1)} %broadcast_in_dim.6), calls=%async_computation.1 | async-start | bytes 458752 | tf_op jit(solution)/shard_map/all_to_all | solution.py:271
  117.3 7.3 %collective-permute-start.4 = (bf16[28,128,128]{2,1,0:T(8,128)(2,1)S(1)}, bf16[28,128,128]{2,1,0:T(8,128)(2,1)S(1)}, u32[]{:S(2)}, u32[]{:S(2)}) collective-permute-start(bf16[28,128,128]{2,1,0:T(8,128)(2,1)S(1)} %bitcast.8), channel_id=1, source_target_pairs={{0,1},{1,0},{2,3},{3,2},{4,5},{5,4},{6,7},{7,6},{8,9},{9,8},{10,11... | collective-permute-start | bytes 2752520 | tf_op jit(solution)/shard_map/ppermute | solution.py:275

commit v9 on v5

--- a/solution.py
+++ b/solution.py
@@ -9,7 +9,7 @@
 
 AXES = ("column", "pair", "y", "x", "zh", "core")
 SLAB = ("y", "x", "zh", "core")
-BLOCK = ("pair", "y", "x")
+PLANE = ("y", "x")
 COLUMN = ("column", "zh")
 BF = jnp.bfloat16
 F32 = jnp.float32
@@ -275,6 +275,10 @@
     return lax.ppermute(block, "core", [(0, 1), (1, 0)])
 
 
+def other_plane(block):
+    return lax.ppermute(block, "pair", [(0, 1), (1, 0)])
+
+
 def on_device(feat, counts, nb, low, high, w_one, w_two, cot):
     sites, channels = feat.shape
     offsets, rim = nb.shape[1], low.shape[0]
@@ -305,14 +309,19 @@
         (broad, broad, ((WIDE, offsets * channels), BF)), 1, 5,
     )(counts, masked, grad, names, faces, picks, w_one, w_two, far, near)
 
-    column, block = lax.axis_size(COLUMN), lax.axis_size(BLOCK)
+    column, plane = lax.axis_size(COLUMN), lax.axis_size(PLANE)
+    side = lax.axis_index("pair")
     near = other_core(theirs)
     share = (mine.astype(F32) + near.astype(F32)).astype(BF)
     share, far_two = lax.optimization_barrier((share, far_two))
-    parts = swap(share.reshape(block, -1, channels), BLOCK)
+    parts = swap(share.reshape(plane, -1, channels), PLANE)
     far = far_slab(far_two)
-    parts = (jnp.sum(parts.astype(F32), 0) * half).astype(BF)
+    parts = jnp.sum(parts.astype(F32), 0)
     parts, far = lax.optimization_barrier((parts, far))
+    rows = parts.shape[0] // 2
+    keep = lax.dynamic_slice_in_dim(parts, side * rows, rows)
+    give = lax.dynamic_slice_in_dim(parts, (1 - side) * rows, rows)
+    parts = ((keep + other_plane(give)) * half).astype(BF)
     parts = swap(jnp.broadcast_to(parts, (column, *parts.shape)), COLUMN)
     response, input_grad = call(
         last_kernel, "svvvvvvv", (flat, flat), (broad,), 1, 3
@@ -320,7 +329,11 @@
     total = (jnp.sum(parts.astype(F32), 0) * half).astype(BF)
     total, response, input_grad = lax.optimization_barrier((total, response, input_grad))
 
-    whole = swap(jnp.broadcast_to(total, (block, *total.shape)), BLOCK)
+    other = other_plane(total)
+    both = jnp.where(
+        side == 0, jnp.concatenate([total, other]), jnp.concatenate([other, total])
+    )
+    whole = swap(jnp.broadcast_to(both, (plane, *both.shape)), PLANE)
     whole = whole.reshape(offsets + 1, channels, channels)
     other = other_core(whole)
     first_is_mine = lax.axis_index("core") == 0

time: 119 us -> 127 us (1.067)
  starting transfers between devices: 48.7 us -> 61.3 us
  blocking collectives: 27.4 us -> 23.3 us
    ppermute x0 -> x2, starting transfers between devices: none -> 7.81 us  [other_plane(): return lax.ppermute(block, 'pair', [(0, 1), (1, 0)])]
    ppermute x2, waiting for transfers between devices: 6.29 us -> 0.01 us  [far_slab(): return lax.ppermute(block, SLAB, pairs)]
    all_to_all x2, starting transfers between devices: 11.8 us -> 17.2 us  [swap(): return lax.all_to_all(block, axis, 0, 0, tiled=True)]
    all_to_all x1, blocking collectives: 27.4 us -> 23.3 us  [swap(): return lax.all_to_all(block, axis, 0, 0, tiled=True)]
    ppermute x0 -> x2, waiting for transfers between devices: none -> 3.5 us  [other_plane(): return lax.ppermute(block, 'pair', [(0, 1), (1, 0)])]
    all_to_all x2, waiting for transfers between devices: 12.1 us -> 14.7 us  [swap(): return lax.all_to_all(block, axis, 0, 0, tiled=True)]
    ppermute x2, starting transfers between devices: 28 us -> 26.7 us  [far_slab(): return lax.ppermute(block, SLAB, pairs)]
  transfers between devices with their start and end apart: 7 -> 9, of which waited for: 5 -> 6; matrix products, arithmetic and copies ran while one was open for 2% -> 2% of each run, Pallas kernels for 2% -> 2%
where the time goes in v9:
time: 127 us; the launch traced here: 126 us
  starting transfers between devices  61.3 us (48%)
  blocking collectives  23.3 us (18%)
  waiting for transfers between devices  22.4 us (18%)
  Pallas kernels  7.81 us (6%)
  local copies, waits for them, and re-layouts  6.18 us (5%)
  other arithmetic  3.97 us (3%)
  between operations  1.47 us (1%)
    ppermute x2, starting transfers between devices, far_slab(): return lax.ppermute(block, SLAB, pairs)  26.7 us
    all_to_all x1, blocking collectives, swap(): return lax.all_to_all(block, axis, 0, 0, tiled=True)  23.3 us
    all_to_all x2, starting transfers between devices, swap(): return lax.all_to_all(block, axis, 0, 0, tiled=True)  17.2 us
    all_to_all x2, waiting for transfers between devices, swap(): return lax.all_to_all(block, axis, 0, 0, tiled=True)  14.7 us
    ppermute x3, starting transfers between devices, other_core(): return lax.ppermute(block, 'core', [(0, 1), (1, 0)])  9.67 us
    ppermute x2, starting transfers between devices, other_plane(): return lax.ppermute(block, 'pair', [(0, 1), (1, 0)])  7.81 us
    unnamed x12, local copies, waits for them, and re-layouts  4.57 us
    ppermute x3, waiting for transfers between devices, other_core(): return lax.ppermute(block, 'core', [(0, 1), (1, 0)])  4.15 us
  transfers between devices with their start and end apart: 9, of which 6 were waited for; matrix products, arithmetic and copies ran while one was open for 2% of the time, Pallas kernels for 2%

profile of v9, /device:TPU:1, one launch (start us, length us, event | category | flops | bytes accessed | tf_op | source)
XLA Modules:
  0.0 126.4 jit_solution(6939331205553445673)
XLA Ops:
  1.3 1.7 %shard_map.111 = (bf16[192,128]{1,0:T(8,128)(2,1)}, bf16[192,128]{1,0:T(8,128)(2,1)}, f32[2,32]{1,0:T(2,128)}) custom-call(s32[1]{0:T(128)S(6)} %copy.12.counts, bf16[128,128]{1,0:T(8,128)(2,1)} %feat.1, bf16[128,128]{1,0:T(8,128)(2,1)} %cot_h.1, s32[27,128]{1,0:T(8,128)} %bitcast.10, s32[1,32]{1,0:T(1,128)} %bitcast.11, s32[1,32]{1,0:T(1,128)} %bitcast.12), custom_call_target="tpu_custom_call" | custom-call | bytes 3000000 | tf_op jit(solution)/shard_map/pallas_call | solution.py:298
  3.0 16.8 %collective-permute-start = (bf16[192,128]{1,0:T(8,128)(2,1)}, bf16[192,128]{1,0:T(8,128)(2,1)S(1)}, u32[]{:S(2)}, u32[]{:S(2)}) collective-permute-start(bf16[192,128]{1,0:T(8,128)(2,1)} %get-tuple-element.28.own), channel_id=1, source_target_pairs={{1,2},{2,1},{3,4},{4,3},{5,6},{6,5},{7,8},{8,7},{9,10},{10,9},{11,... | collective-permute-start | bytes 147464 | tf_op jit(solution)/shard_map/ppermute | solution.py:267
  19.8 1.9 %collective-permute-start.1 = (bf16[192,128]{1,0:T(8,128)(2,1)}, bf16[192,128]{1,0:T(8,128)(2,1)S(1)}, u32[]{:S(2)}, u32[]{:S(2)}) collective-permute-start(bf16[192,128]{1,0:T(8,128)(2,1)} %get-tuple-element.37), channel_id=1, source_target_pairs={{0,1},{1,0},{2,3},{3,2},{4,5},{5,4},{6,7},{7,6},{8,9},{9,8},{10,11... | collective-permute-start | bytes 147464 | tf_op jit(solution)/shard_map/ppermute | solution.py:275
  21.7 0.0 copy-start
  21.7 1.2 copy-done
  22.9 0.0 copy-start.1
  22.9 1.2 copy-done.1
  24.1 0.0 copy-start.2
  24.1 0.8 copy-done.2
  24.8 0.0 copy-start.3
  24.8 0.8 copy-done.3
  25.6 0.0 copy-start.4
  25.6 0.7 copy-done.4
  26.3 0.6 shard_map.112
  26.9 0.0 collective-permute-done.far
  26.9 0.0 collective-permute-done.1.near
  26.9 4.0 %shard_map.113 = (f32[64,128]{1,0:T(8,128)S(1)}, f32[128,128]{1,0:T(8,128)S(1)}, bf16[128,128]{1,0:T(8,128)(2,1)S(1)}, bf16[28,128,128]{2,1,0:T(8,128)(2,1)S(1)}, bf16[28,128,128]{2,1,0:T(8,128)(2,1)S(1)}) custom-call(s32[1]{0:T(128)S(6)} %copy.12.counts, bf16[128,128]{1,0:T(8,128)(2,1)S(1)} %get-tuple-element.30.masked, ...), custom_call_target="tpu_custom_call" | custom-call | bytes 15000000 | tf_op jit(solution)/shard_map/pallas_call | solution.py:307
  30.9 2.4 %collective-permute-start.2 = (bf16[28,128,128]{2,1,0:T(8,128)(2,1)S(1)}, bf16[28,128,128]{2,1,0:T(8,128)(2,1)S(1)}, u32[]{:S(2)}, u32[]{:S(2)}) collective-permute-start(bf16[28,128,128]{2,1,0:T(8,128)(2,1)S(1)} %get-tuple-element.39), channel_id=1, source_target_pairs={{0,1},{1,0},{2,3},{3,2},{4,5},{5,4},{6,7},{7,6},{8,9},{9,8},{10,11... | collective-permute-start | bytes 2752520 | tf_op jit(solution)/shard_map/ppermute | solution.py:275
  33.3 2.1 %collective-permute-done.2 = bf16[28,128,128]{2,1,0:T(8,128)(2,1)S(1)} collective-permute-done((bf16[28,128,128]{2,1,0:T(8,128)(2,1)S(1)}, bf16[28,128,128]{2,1,0:T(8,128)(2,1)S(1)}, u32[]{:S(2)}, u32[]{:S(2)}) %collective-permute-start.2) | collective-permute-done | bytes 917536 | tf_op jit(solution)/shard_map/ppermute | solution.py:275
  35.4 0.0 copy-start.5
  35.4 1.3 %add_convert_fusion = bf16[28,128,128]{2,1,0:T(8,128)(2,1)} fusion(bf16[28,128,128]{2,1,0:T(8,128)(2,1)S(1)} %collective-permute-done.2, bf16[28,128,128]{2,1,0:T(8,128)(2,1)S(1)} %get-tuple-element.38), kind=kLoop, calls=%fused_computation.1 | loop fusion | flops 1835008 | bytes 2752512 | tf_op jit(solution)/shard_map/convert_element_type | solution.py:315
  36.6 0.0 copy-done.5
  36.6 6.8 %all-to-all-start = ((bf16[16,224,128]{2,1,0:T(8,128)(2,1)}), bf16[16,224,128]{2,1,0:T(8,128)(2,1)}, u32[]{:S(2)}, u32[]{:S(2)}) async-start(bf16[16,224,128]{2,1,0:T(8,128)(2,1)} %bitcast.7), calls=%async_computation | async-start | bytes 1835008 | tf_op jit(solution)/shard_map/all_to_all | solution.py:271
  43.5 9.9 %collective-permute-start.3 = (f32[64,128]{1,0:T(8,128)S(1)}, f32[64,128]{1,0:T(8,128)S(1)}, u32[]{:S(2)}, u32[]{:S(2)}) collective-permute-start(f32[64,128]{1,0:T(8,128)S(1)} %get-tuple-element.42), channel_id=1, source_target_pairs={{1,2},{2,1},{3,4},{4,3},{5,6},{6,5},{7,8},{8,7},{9,10},{10,9},{11,... | collective-permute-start | bytes 98312 | tf_op jit(solution)/shard_map/ppermute | solution.py:267
  53.3 5.1 %all-to-all-done = bf16[16,224,128]{2,1,0:T(8,128)(2,1)} async-done(((bf16[16,224,128]{2,1,0:T(8,128)(2,1)}), bf16[16,224,128]{2,1,0:T(8,128)(2,1)}, u32[]{:S(2)}, u32[]{:S(2)}) %all-to-all-start) | async-done | bytes 917536 | tf_op jit(solution)/shard_map/all_to_all | solution.py:271
  58.4 1.3 %convert_reduce_fusion = f32[224,128]{1,0:T(8,128)S(1)} fusion(bf16[16,224,128]{2,1,0:T(8,128)(2,1)} %all-to-all-done), kind=kLoop, calls=%fused_computation | loop fusion | flops 888832 | bytes 1032192 | tf_op jit(solution)/shard_map/reduce_sum | solution.py:319
  59.8 0.0 collective-permute-done.3.far
  59.8 2.7 %collective-permute-start.4 = (f32[112,128]{1,0:T(8,128)S(1)}, f32[112,128]{1,0:T(8,128)S(1)}, u32[]{:S(2)}, u32[]{:S(2)}) collective-permute-start(f32[112,128]{1,0:T(8,128)S(1)} %constant_dynamic-slice_fusion), channel_id=1, source_target_pairs={{0,64},{64,0},{1,65},{65,1},{2,66},{66,2},{3,67},{67,3},{4,68},{68... | collective-permute-start | bytes 172040 | tf_op jit(solution)/shard_map/ppermute | solution.py:279
  62.4 2.3 %collective-permute-done.4 = f32[112,128]{1,0:T(8,128)S(1)} collective-permute-done((f32[112,128]{1,0:T(8,128)S(1)}, f32[112,128]{1,0:T(8,128)S(1)}, u32[]{:S(2)}, u32[]{:S(2)}) %collective-permute-start.4) | collective-permute-done | bytes 57376 | tf_op jit(solution)/shard_map/ppermute | solution.py:279
  64.7 0.7 broadcast_in_dim.6
  65.4 10.4 %all-to-all-start.1 = ((bf16[8,112,128]{2,1,0:T(8,128)(2,1)}), bf16[8,112,128]{2,1,0:T(8,128)(2,1)S(1)}, u32[]{:S(2)}, u32[]{:S(2)}) async-start(bf16[8,112,128]{2,1,0:T(8,128)(2,1)} %broadcast_in_dim.6), calls=%async_computation.1 | async-start | bytes 458752 | tf_op jit(solution)/shard_map/all_to_all | solution.py:271
  75.8 0.8 slice_bitcast_fusion.near
  76.6 1.6 %shard_map.114 = (bf16[128,128]{1,0:T(8,128)(2,1)}, bf16[128,128]{1,0:T(8,128)(2,1)}) custom-call(s32[1]{0:T(128)S(6)} %copy.12.counts, bf16[128,128]{1,0:T(8,128)(2,1)S(1)} %get-tuple-element.44.hidden, f32[2,32]{1,0:T(2,128)S(1)} %get-tuple-element.33.faces, bf16[128,128]{1,0:T(8,128)(2,1)S(1)} %slice_bitcast_fusion.near, ...), custom_call_target="tpu_custom_call" | custom-call | bytes 9000000 | tf_op jit(solution)/shard_map/pallas_call | solution.py:326
  78.2 9.6 %all-to-all-done.1 = bf16[8,112,128]{2,1,0:T(8,128)(2,1)S(1)} async-done(((bf16[8,112,128]{2,1,0:T(8,128)(2,1)}), bf16[8,112,128]{2,1,0:T(8,128)(2,1)S(1)}, u32[]{:S(2)}, u32[]{:S(2)}) %all-to-all-start.1) | async-done | bytes 229408 | tf_op jit(solution)/shard_map/all_to_all | solution.py:271
  87.8 5.2 %collective-permute-start.5 = (bf16[112,128]{1,0:T(8,128)(2,1)S(1)}, bf16[112,128]{1,0:T(8,128)(2,1)S(1)}, u32[]{:S(2)}, u32[]{:S(2)}) collective-permute-start(bf16[112,128]{1,0:T(8,128)(2,1)S(1)} %multiply_convert_fusion), channel_id=1, source_target_pairs={{0,64},{64,0},{1,65},{65,1},{2,66},{66,2},{3,67},{67,3},{4,68},{68... | collective-permute-start | bytes 86024 | tf_op jit(solution)/shard_map/ppermute | solution.py:279
  93.0 1.2 collective-permute-done.5
  94.2 0.1 broadcast_in_dim.7
  94.4 23.3 %all_to_all.15 = bf16[16,224,128]{2,1,0:T(8,128)(2,1)S(1)} all-to-all(bf16[16,224,128]{2,1,0:T(8,128)(2,1)S(1)} %broadcast_in_dim.7), channel_id=1, replica_groups=mesh['column'=4,'pair'=2,'y'=4,'x'=4,'zh'=2,'core'=2] {'y','x'}, dimensions={0} | all-to-all | bytes 1835008 | tf_op jit(solution)/shard_map/all_to_all | solution.py:271
  117.7 5.3 %collective-permute-start.6 = (bf16[28,128,128]{2,1,0:T(8,128)(2,1)S(1)}, bf16[28,128,128]{2,1,0:T(8,128)(2,1)S(1)}, u32[]{:S(2)}, u32[]{:S(2)}) collective-permute-start(bf16[28,128,128]{2,1,0:T(8,128)(2,1)S(1)} %bitcast.8), channel_id=1, source_target_pairs={{0,1},{1,0},{2,3},{3,2},{4,5},{5,4},{6,7},{7,6},{8,9},{9,8},{10,11... | collective-permute-start | bytes 2752520 | tf_op jit(solution)/shard_map/ppermute | solution.py:275
  123.0 2.1 %collective-permute-done.6 = bf16[28,128,128]{2,1,0:T(8,128)(2,1)S(1)} collective-permute-done((bf16[28,128,128]{2,1,0:T(8,128)(2,1)S(1)}, bf16[28,128,128]{2,1,0:T(8,128)(2,1)S(1)}, u32[]{:S(2)}, u32[]{:S(2)}) %collective-permute-start.6) | collective-permute-done | bytes 917536 | tf_op jit(solution)/shard_map/ppermute | solution.py:275
  125.1 1.3 %broadcast_select_fusion = (bf16[27,128,128]{2,1,0:T(8,128)(2,1)}, bf16[27,128,128]{2,1,0:T(8,128)(2,1)}) fusion(pred[]{:T(512)S(6)} %eq.6, bf16[28,128,128]{2,1,0:T(8,128)(2,1)S(1)} %collective-permute-done.6, bf16[28,128,128]{2,1,0:T(8,128)(2,1)S(1)} %bitcast.9), kind=kLoop, calls=%fused_computation.2 | loop fusion | flops 884736 | bytes 3538945 | tf_op jit(solution)/shard_map/jit(_where)/select_n | solution.py:341
  (5 shorter events, 0.1 us)
Async XLA Ops:
  3.0 23.9 %collective-permute-start = (bf16[192,128]{1,0:T(8,128)(2,1)}, bf16[192,128]{1,0:T(8,128)(2,1)S(1)}, u32[]{:S(2)}, u32[]{:S(2)}) collective-permute-start(bf16[192,128]{1,0:T(8,128)(2,1)} %get-tuple-element.28.own), channel_id=1, source_target_pairs={{1,2},{2,1},{3,4},{4,3},{5,6},{6,5},{7,8},{8,7},{9,10},{10,9},{11,... | collective-permute-start | bytes 147464 | tf_op jit(solution)/shard_map/ppermute | solution.py:267
  19.8 7.1 %collective-permute-start.1 = (bf16[192,128]{1,0:T(8,128)(2,1)}, bf16[192,128]{1,0:T(8,128)(2,1)S(1)}, u32[]{:S(2)}, u32[]{:S(2)}) collective-permute-start(bf16[192,128]{1,0:T(8,128)(2,1)} %get-tuple-element.37), channel_id=1, source_target_pairs={{0,1},{1,0},{2,3},{3,2},{4,5},{5,4},{6,7},{7,6},{8,9},{9,8},{10,11... | collective-permute-start | bytes 147464 | tf_op jit(solution)/shard_map/ppermute | solution.py:275
  21.7 1.2 copy-start
  22.9 1.2 copy-start.1
  24.1 0.8 copy-start.2
  24.8 0.8 copy-start.3
  25.6 0.7 copy-start.4
  30.9 4.5 %collective-permute-start.2 = (bf16[28,128,128]{2,1,0:T(8,128)(2,1)S(1)}, bf16[28,128,128]{2,1,0:T(8,128)(2,1)S(1)}, u32[]{:S(2)}, u32[]{:S(2)}) collective-permute-start(bf16[28,128,128]{2,1,0:T(8,128)(2,1)S(1)} %get-tuple-element.39), channel_id=1, source_target_pairs={{0,1},{1,0},{2,3},{3,2},{4,5},{5,4},{6,7},{7,6},{8,9},{9,8},{10,11... | collective-permute-start | bytes 2752520 | tf_op jit(solution)/shard_map/ppermute | solution.py:275
  35.4 1.3 %copy-start.5 = (bf16[28,128,128]{2,1,0:T(8,128)(2,1)}, bf16[28,128,128]{2,1,0:T(8,128)(2,1)S(1)}, u32[]{:S(2)}) copy-start(bf16[28,128,128]{2,1,0:T(8,128)(2,1)S(1)} %collective-permute-done.2) | copy-start | bytes 2752516
  36.6 21.8 %all-to-all-start = ((bf16[16,224,128]{2,1,0:T(8,128)(2,1)}), bf16[16,224,128]{2,1,0:T(8,128)(2,1)}, u32[]{:S(2)}, u32[]{:S(2)}) async-start(bf16[16,224,128]{2,1,0:T(8,128)(2,1)} %bitcast.7), calls=%async_computation | async-start | bytes 1835008 | tf_op jit(solution)/shard_map/all_to_all | solution.py:271
  43.5 16.3 %collective-permute-start.3 = (f32[64,128]{1,0:T(8,128)S(1)}, f32[64,128]{1,0:T(8,128)S(1)}, u32[]{:S(2)}, u32[]{:S(2)}) collective-permute-start(f32[64,128]{1,0:T(8,128)S(1)} %get-tuple-element.42), channel_id=1, source_target_pairs={{1,2},{2,1},{3,4},{4,3},{5,6},{6,5},{7,8},{8,7},{9,10},{10,9},{11,... | collective-permute-start | bytes 98312 | tf_op jit(solution)/shard_map/ppermute | solution.py:267
  59.8 4.9 %collective-permute-start.4 = (f32[112,128]{1,0:T(8,128)S(1)}, f32[112,128]{1,0:T(8,128)S(1)}, u32[]{:S(2)}, u32[]{:S(2)}) collective-permute-start(f32[112,128]{1,0:T(8,128)S(1)} %constant_dynamic-slice_fusion), channel_id=1, source_target_pairs={{0,64},{64,0},{1,65},{65,1},{2,66},{66,2},{3,67},{67,3},{4,68},{68... | collective-permute-start | bytes 172040 | tf_op jit(solution)/shard_map/ppermute | solution.py:279
  65.4 22.3 %all-to-all-start.1 = ((bf16[8,112,128]{2,1,0:T(8,128)(2,1)}), bf16[8,112,128]{2,1,0:T(8,128)(2,1)S(1)}, u32[]{:S(2)}, u32[]{:S(2)}) async-start(bf16[8,112,128]{2,1,0:T(8,128)(2,1)} %broadcast_in_dim.6), calls=%async_computation.1 | async-start | bytes 458752 | tf_op jit(solution)/shard_map/all_to_all | solution.py:271
  87.8 6.4 %collective-permute-start.5 = (bf16[112,128]{1,0:T(8,128)(2,1)S(1)}, bf16[112,128]{1,0:T(8,128)(2,1)S(1)}, u32[]{:S(2)}, u32[]{:S(2)}) collective-permute-start(bf16[112,128]{1,0:T(8,128)(2,1)S(1)} %multiply_convert_fusion), channel_id=1, source_target_pairs={{0,64},{64,0},{1,65},{65,1},{2,66},{66,2},{3,67},{67,3},{4,68},{68... | collective-permute-start | bytes 86024 | tf_op jit(solution)/shard_map/ppermute | solution.py:279
  117.7 7.4 %collective-permute-start.6 = (bf16[28,128,128]{2,1,0:T(8,128)(2,1)S(1)}, bf16[28,128,128]{2,1,0:T(8,128)(2,1)S(1)}, u32[]{:S(2)}, u32[]{:S(2)}) collective-permute-start(bf16[28,128,128]{2,1,0:T(8,128)(2,1)S(1)} %bitcast.8), channel_id=1, source_target_pairs={{0,1},{1,0},{2,3},{3,2},{4,5},{5,4},{6,7},{7,6},{8,9},{9,8},{10,11... | collective-permute-start | bytes 2752520 | tf_op jit(solution)/shard_map/ppermute | solution.py:275

commit v10 on v5

--- a/solution.py
+++ b/solution.py
@@ -9,7 +9,7 @@
 
 AXES = ("column", "pair", "y", "x", "zh", "core")
 SLAB = ("y", "x", "zh", "core")
-BLOCK = ("pair", "y", "x")
+BLOCK = ("y", "x", "pair")
 COLUMN = ("column", "zh")
 BF = jnp.bfloat16
 F32 = jnp.float32

time: 119 us -> 121 us (1.017); the launches traced: 118 us -> 119 us
  starting transfers between devices: 48.7 us -> 50.2 us
    ppermute x2, waiting for transfers between devices: 6.29 us -> 4.42 us  [far_slab(): return lax.ppermute(block, SLAB, pairs)]
    all_to_all x2, starting transfers between devices: 11.8 us -> 13.6 us  [swap(): return lax.all_to_all(block, axis, 0, 0, tiled=True)]
    all_to_all x2, waiting for transfers between devices: 12.1 us -> 13.9 us  [swap(): return lax.all_to_all(block, axis, 0, 0, tiled=True)]
where the time goes in v10:
time: 121 us; the launch traced here: 119 us
  starting transfers between devices  50.2 us (41%)
  blocking collectives  26.7 us (22%)
  waiting for transfers between devices  22.4 us (19%)
  Pallas kernels  7.8 us (6%)
  local copies, waits for them, and re-layouts  6.16 us (5%)
  other arithmetic  3.94 us (3%)
  between operations  1.42 us (1%)
    ppermute x2, starting transfers between devices, far_slab(): return lax.ppermute(block, SLAB, pairs)  28 us
    all_to_all x1, blocking collectives, swap(): return lax.all_to_all(block, axis, 0, 0, tiled=True)  26.7 us
    all_to_all x2, waiting for transfers between devices, swap(): return lax.all_to_all(block, axis, 0, 0, tiled=True)  13.9 us
    all_to_all x2, starting transfers between devices, swap(): return lax.all_to_all(block, axis, 0, 0, tiled=True)  13.6 us
    ppermute x3, starting transfers between devices, other_core(): return lax.ppermute(block, 'core', [(0, 1), (1, 0)])  8.55 us
    unnamed x12, local copies, waits for them, and re-layouts  4.57 us
    ppermute x2, waiting for transfers between devices, far_slab(): return lax.ppermute(block, SLAB, pairs)  4.42 us
    ppermute x3, waiting for transfers between devices, other_core(): return lax.ppermute(block, 'core', [(0, 1), (1, 0)])  4.15 us
  transfers between devices with their start and end apart: 7, of which 5 were waited for; matrix products, arithmetic and copies ran while one was open for 2% of the time, Pallas kernels for 2%

profile of v10, /device:TPU:1, one launch (start us, length us, event | category | flops | bytes accessed | tf_op | source)
XLA Modules:
  0.0 118.6 jit_solution(8122114277851906386)
XLA Ops:
  1.3 1.7 %shard_map.111 = (bf16[192,128]{1,0:T(8,128)(2,1)}, bf16[192,128]{1,0:T(8,128)(2,1)}, f32[2,32]{1,0:T(2,128)}) custom-call(s32[1]{0:T(128)S(6)} %copy.12.counts, bf16[128,128]{1,0:T(8,128)(2,1)} %feat.1, bf16[128,128]{1,0:T(8,128)(2,1)} %cot_h.1, s32[27,128]{1,0:T(8,128)} %bitcast.10, s32[1,32]{1,0:T(1,128)} %bitcast.11, s32[1,32]{1,0:T(1,128)} %bitcast.12), custom_call_target="tpu_custom_call" | custom-call | bytes 3000000 | tf_op jit(solution)/shard_map/pallas_call | solution.py:294
  3.0 16.8 %collective-permute-start = (bf16[192,128]{1,0:T(8,128)(2,1)}, bf16[192,128]{1,0:T(8,128)(2,1)S(1)}, u32[]{:S(2)}, u32[]{:S(2)}) collective-permute-start(bf16[192,128]{1,0:T(8,128)(2,1)} %get-tuple-element.28.own), channel_id=1, source_target_pairs={{1,2},{2,1},{3,4},{4,3},{5,6},{6,5},{7,8},{8,7},{9,10},{10,9},{11,... | collective-permute-start | bytes 147464 | tf_op jit(solution)/shard_map/ppermute | solution.py:267
  19.8 1.9 %collective-permute-start.1 = (bf16[192,128]{1,0:T(8,128)(2,1)}, bf16[192,128]{1,0:T(8,128)(2,1)S(1)}, u32[]{:S(2)}, u32[]{:S(2)}) collective-permute-start(bf16[192,128]{1,0:T(8,128)(2,1)} %get-tuple-element.37), channel_id=1, source_target_pairs={{0,1},{1,0},{2,3},{3,2},{4,5},{5,4},{6,7},{7,6},{8,9},{9,8},{10,11... | collective-permute-start | bytes 147464 | tf_op jit(solution)/shard_map/ppermute | solution.py:275
  21.7 0.0 copy-start
  21.7 1.2 copy-done
  22.9 0.0 copy-start.1
  22.9 1.2 copy-done.1
  24.1 0.0 copy-start.2
  24.1 0.8 copy-done.2
  24.8 0.0 copy-start.3
  24.8 0.8 copy-done.3
  25.6 0.0 copy-start.4
  25.6 0.7 copy-done.4
  26.3 0.6 shard_map.112
  26.9 0.0 collective-permute-done.far
  26.9 0.0 collective-permute-done.1.near
  26.9 3.9 %shard_map.113 = (f32[64,128]{1,0:T(8,128)S(1)}, f32[128,128]{1,0:T(8,128)S(1)}, bf16[128,128]{1,0:T(8,128)(2,1)S(1)}, bf16[28,128,128]{2,1,0:T(8,128)(2,1)S(1)}, bf16[28,128,128]{2,1,0:T(8,128)(2,1)S(1)}) custom-call(s32[1]{0:T(128)S(6)} %copy.12.counts, bf16[128,128]{1,0:T(8,128)(2,1)S(1)} %get-tuple-element.30.masked, ...), custom_call_target="tpu_custom_call" | custom-call | bytes 15000000 | tf_op jit(solution)/shard_map/pallas_call | solution.py:303
  30.9 2.4 %collective-permute-start.2 = (bf16[28,128,128]{2,1,0:T(8,128)(2,1)S(1)}, bf16[28,128,128]{2,1,0:T(8,128)(2,1)S(1)}, u32[]{:S(2)}, u32[]{:S(2)}) collective-permute-start(bf16[28,128,128]{2,1,0:T(8,128)(2,1)S(1)} %get-tuple-element.39), channel_id=1, source_target_pairs={{0,1},{1,0},{2,3},{3,2},{4,5},{5,4},{6,7},{7,6},{8,9},{9,8},{10,11... | collective-permute-start | bytes 2752520 | tf_op jit(solution)/shard_map/ppermute | solution.py:275
  33.3 2.1 %collective-permute-done.2 = bf16[28,128,128]{2,1,0:T(8,128)(2,1)S(1)} collective-permute-done((bf16[28,128,128]{2,1,0:T(8,128)(2,1)S(1)}, bf16[28,128,128]{2,1,0:T(8,128)(2,1)S(1)}, u32[]{:S(2)}, u32[]{:S(2)}) %collective-permute-start.2) | collective-permute-done | bytes 917536 | tf_op jit(solution)/shard_map/ppermute | solution.py:275
  35.4 0.0 copy-start.5
  35.4 1.3 %add_convert_fusion = bf16[28,128,128]{2,1,0:T(8,128)(2,1)} fusion(bf16[28,128,128]{2,1,0:T(8,128)(2,1)S(1)} %collective-permute-done.2, bf16[28,128,128]{2,1,0:T(8,128)(2,1)S(1)} %get-tuple-element.38), kind=kLoop, calls=%fused_computation.1 | loop fusion | flops 1835008 | bytes 2752512 | tf_op jit(solution)/shard_map/convert_element_type | solution.py:310
  36.6 0.0 copy-done.5
  36.6 7.6 %all-to-all-start = ((bf16[32,112,128]{2,1,0:T(8,128)(2,1)}), bf16[32,112,128]{2,1,0:T(8,128)(2,1)}, u32[]{:S(2)}, u32[]{:S(2)}) async-start(bf16[32,112,128]{2,1,0:T(8,128)(2,1)} %bitcast.7), calls=%async_computation | async-start | bytes 1835008 | tf_op jit(solution)/shard_map/all_to_all | solution.py:271
  44.2 11.1 %collective-permute-start.3 = (f32[64,128]{1,0:T(8,128)S(1)}, f32[64,128]{1,0:T(8,128)S(1)}, u32[]{:S(2)}, u32[]{:S(2)}) collective-permute-start(f32[64,128]{1,0:T(8,128)S(1)} %get-tuple-element.42), channel_id=1, source_target_pairs={{1,2},{2,1},{3,4},{4,3},{5,6},{6,5},{7,8},{8,7},{9,10},{10,9},{11,... | collective-permute-start | bytes 98312 | tf_op jit(solution)/shard_map/ppermute | solution.py:267
  55.4 4.4 %all-to-all-done = bf16[32,112,128]{2,1,0:T(8,128)(2,1)} async-done(((bf16[32,112,128]{2,1,0:T(8,128)(2,1)}), bf16[32,112,128]{2,1,0:T(8,128)(2,1)}, u32[]{:S(2)}, u32[]{:S(2)}) %all-to-all-start) | async-done | bytes 917536 | tf_op jit(solution)/shard_map/all_to_all | solution.py:271
  59.8 1.3 %convert_reduce_fusion = f32[112,128]{1,0:T(8,128)S(1)} fusion(bf16[32,112,128]{2,1,0:T(8,128)(2,1)} %all-to-all-done), kind=kLoop, calls=%fused_computation | loop fusion | flops 903168 | bytes 974848 | tf_op jit(solution)/shard_map/reduce_sum | solution.py:314
  61.1 4.4 %collective-permute-done.3.far = f32[64,128]{1,0:T(8,128)S(1)} collective-permute-done((f32[64,128]{1,0:T(8,128)S(1)}, f32[64,128]{1,0:T(8,128)S(1)}, u32[]{:S(2)}, u32[]{:S(2)}) %collective-permute-start.3) | collective-permute-done | bytes 32800 | tf_op jit(solution)/shard_map/ppermute | solution.py:267
  65.6 0.7 broadcast_in_dim.6
  66.3 6.0 %all-to-all-start.1 = ((bf16[8,112,128]{2,1,0:T(8,128)(2,1)}), bf16[8,112,128]{2,1,0:T(8,128)(2,1)S(1)}, u32[]{:S(2)}, u32[]{:S(2)}) async-start(bf16[8,112,128]{2,1,0:T(8,128)(2,1)} %broadcast_in_dim.6), calls=%async_computation.1 | async-start | bytes 458752 | tf_op jit(solution)/shard_map/all_to_all | solution.py:271
  72.3 0.8 slice_bitcast_fusion.near
  73.1 1.6 %shard_map.114 = (bf16[128,128]{1,0:T(8,128)(2,1)}, bf16[128,128]{1,0:T(8,128)(2,1)}) custom-call(s32[1]{0:T(128)S(6)} %copy.12.counts, bf16[128,128]{1,0:T(8,128)(2,1)S(1)} %get-tuple-element.44.hidden, f32[2,32]{1,0:T(2,128)S(1)} %get-tuple-element.33.faces, bf16[128,128]{1,0:T(8,128)(2,1)S(1)} %slice_bitcast_fusion.near, ...), custom_call_target="tpu_custom_call" | custom-call | bytes 9000000 | tf_op jit(solution)/shard_map/pallas_call | solution.py:317
  74.7 9.5 %all-to-all-done.1 = bf16[8,112,128]{2,1,0:T(8,128)(2,1)S(1)} async-done(((bf16[8,112,128]{2,1,0:T(8,128)(2,1)}), bf16[8,112,128]{2,1,0:T(8,128)(2,1)S(1)}, u32[]{:S(2)}, u32[]{:S(2)}) %all-to-all-start.1) | async-done | bytes 229408 | tf_op jit(solution)/shard_map/all_to_all | solution.py:271
  84.2 0.1 broadcast_in_dim.7
  84.3 26.7 %all_to_all.15 = bf16[32,112,128]{2,1,0:T(8,128)(2,1)S(1)} all-to-all(bf16[32,112,128]{2,1,0:T(8,128)(2,1)S(1)} %broadcast_in_dim.7), channel_id=1, replica_groups=mesh['column'=4,'pair'=2,'y'=4,'x'=4,'zh'=2,'core'=2] {'y','x','pair'}, dimensions={0} | all-to-all | bytes 1835008 | tf_op jit(solution)/shard_map/all_to_all | solution.py:271
  111.0 4.2 %collective-permute-start.4 = (bf16[28,128,128]{2,1,0:T(8,128)(2,1)S(1)}, bf16[28,128,128]{2,1,0:T(8,128)(2,1)S(1)}, u32[]{:S(2)}, u32[]{:S(2)}) collective-permute-start(bf16[28,128,128]{2,1,0:T(8,128)(2,1)S(1)} %bitcast.8), channel_id=1, source_target_pairs={{0,1},{1,0},{2,3},{3,2},{4,5},{5,4},{6,7},{7,6},{8,9},{9,8},{10,11... | collective-permute-start | bytes 2752520 | tf_op jit(solution)/shard_map/ppermute | solution.py:275
  115.2 2.1 %collective-permute-done.4 = bf16[28,128,128]{2,1,0:T(8,128)(2,1)S(1)} collective-permute-done((bf16[28,128,128]{2,1,0:T(8,128)(2,1)S(1)}, bf16[28,128,128]{2,1,0:T(8,128)(2,1)S(1)}, u32[]{:S(2)}, u32[]{:S(2)}) %collective-permute-start.4) | collective-permute-done | bytes 917536 | tf_op jit(solution)/shard_map/ppermute | solution.py:275
  117.3 1.3 %broadcast_select_fusion = (bf16[27,128,128]{2,1,0:T(8,128)(2,1)}, bf16[27,128,128]{2,1,0:T(8,128)(2,1)}) fusion(pred[]{:T(512)S(6)} %eq.3, bf16[28,128,128]{2,1,0:T(8,128)(2,1)S(1)} %collective-permute-done.4, bf16[28,128,128]{2,1,0:T(8,128)(2,1)S(1)} %bitcast.9), kind=kLoop, calls=%fused_computation.2 | loop fusion | flops 884736 | bytes 3538945 | tf_op jit(solution)/shard_map/jit(_where)/select_n | solution.py:328
  (3 shorter events, 0.0 us)
Async XLA Ops:
  3.0 23.9 %collective-permute-start = (bf16[192,128]{1,0:T(8,128)(2,1)}, bf16[192,128]{1,0:T(8,128)(2,1)S(1)}, u32[]{:S(2)}, u32[]{:S(2)}) collective-permute-start(bf16[192,128]{1,0:T(8,128)(2,1)} %get-tuple-element.28.own), channel_id=1, source_target_pairs={{1,2},{2,1},{3,4},{4,3},{5,6},{6,5},{7,8},{8,7},{9,10},{10,9},{11,... | collective-permute-start | bytes 147464 | tf_op jit(solution)/shard_map/ppermute | solution.py:267
  19.8 7.1 %collective-permute-start.1 = (bf16[192,128]{1,0:T(8,128)(2,1)}, bf16[192,128]{1,0:T(8,128)(2,1)S(1)}, u32[]{:S(2)}, u32[]{:S(2)}) collective-permute-start(bf16[192,128]{1,0:T(8,128)(2,1)} %get-tuple-element.37), channel_id=1, source_target_pairs={{0,1},{1,0},{2,3},{3,2},{4,5},{5,4},{6,7},{7,6},{8,9},{9,8},{10,11... | collective-permute-start | bytes 147464 | tf_op jit(solution)/shard_map/ppermute | solution.py:275
  21.7 1.2 copy-start
  22.9 1.2 copy-start.1
  24.1 0.8 copy-start.2
  24.8 0.8 copy-start.3
  25.6 0.7 copy-start.4
  30.9 4.5 %collective-permute-start.2 = (bf16[28,128,128]{2,1,0:T(8,128)(2,1)S(1)}, bf16[28,128,128]{2,1,0:T(8,128)(2,1)S(1)}, u32[]{:S(2)}, u32[]{:S(2)}) collective-permute-start(bf16[28,128,128]{2,1,0:T(8,128)(2,1)S(1)} %get-tuple-element.39), channel_id=1, source_target_pairs={{0,1},{1,0},{2,3},{3,2},{4,5},{5,4},{6,7},{7,6},{8,9},{9,8},{10,11... | collective-permute-start | bytes 2752520 | tf_op jit(solution)/shard_map/ppermute | solution.py:275
  35.4 1.3 %copy-start.5 = (bf16[28,128,128]{2,1,0:T(8,128)(2,1)}, bf16[28,128,128]{2,1,0:T(8,128)(2,1)S(1)}, u32[]{:S(2)}) copy-start(bf16[28,128,128]{2,1,0:T(8,128)(2,1)S(1)} %collective-permute-done.2) | copy-start | bytes 2752516
  36.6 23.2 %all-to-all-start = ((bf16[32,112,128]{2,1,0:T(8,128)(2,1)}), bf16[32,112,128]{2,1,0:T(8,128)(2,1)}, u32[]{:S(2)}, u32[]{:S(2)}) async-start(bf16[32,112,128]{2,1,0:T(8,128)(2,1)} %bitcast.7), calls=%async_computation | async-start | bytes 1835008 | tf_op jit(solution)/shard_map/all_to_all | solution.py:271
  44.2 21.3 %collective-permute-start.3 = (f32[64,128]{1,0:T(8,128)S(1)}, f32[64,128]{1,0:T(8,128)S(1)}, u32[]{:S(2)}, u32[]{:S(2)}) collective-permute-start(f32[64,128]{1,0:T(8,128)S(1)} %get-tuple-element.42), channel_id=1, source_target_pairs={{1,2},{2,1},{3,4},{4,3},{5,6},{6,5},{7,8},{8,7},{9,10},{10,9},{11,... | collective-permute-start | bytes 98312 | tf_op jit(solution)/shard_map/ppermute | solution.py:267
  66.3 17.9 %all-to-all-start.1 = ((bf16[8,112,128]{2,1,0:T(8,128)(2,1)}), bf16[8,112,128]{2,1,0:T(8,128)(2,1)S(1)}, u32[]{:S(2)}, u32[]{:S(2)}) async-start(bf16[8,112,128]{2,1,0:T(8,128)(2,1)} %broadcast_in_dim.6), calls=%async_computation.1 | async-start | bytes 458752 | tf_op jit(solution)/shard_map/all_to_all | solution.py:271
  111.0 6.3 %collective-permute-start.4 = (bf16[28,128,128]{2,1,0:T(8,128)(2,1)S(1)}, bf16[28,128,128]{2,1,0:T(8,128)(2,1)S(1)}, u32[]{:S(2)}, u32[]{:S(2)}) collective-permute-start(bf16[28,128,128]{2,1,0:T(8,128)(2,1)S(1)} %bitcast.8), channel_id=1, source_target_pairs={{0,1},{1,0},{2,3},{3,2},{4,5},{5,4},{6,7},{7,6},{8,9},{9,8},{10,11... | collective-permute-start | bytes 2752520 | tf_op jit(solution)/shard_map/ppermute | solution.py:275
